TPU v7x, 32 devices: a whole 2x2x4 slice. The times are simulated.
32 devices in a mesh: pos: 8 (over z, x), tile: 4 (over y, core).
Axes of the slice: x: 2, y: 2, z: 4, core: 2. Of those that a mesh axis runs over, the one named last changes fastest.
Arguments:
- probe_modes: float32 [8, 2, 256, 256], P('tile'), may hold values from -1.1 to 1.1
- object_slices: bfloat16 [2, 2, 512, 2048], P(None, None, 'tile'), may hold values from -6 to 6
- amplitudes: bfloat16 [64, 256, 256], P('pos'), may hold values from 0.5 to 3
- scan_offsets: int32 [64, 2], replicated, may hold values from 0 to 1792, as said below
- slot_counts: int32 [8], replicated, may hold values from 1 to 8, 32 in all
Outputs:
- object_grad: float32 [2, 2, 512, 2048], P(None, None, 'tile', 'pos')
- probe_grad: float32 [8, 2, 256, 256], P('tile', None, 'pos')
Inputs may be any that keep to these rules, and one draw needn't show every extreme that they name: slot_counts[g] is how many leading slots of group g are live scan positions; the counts sum to 32 and the largest is exactly 8. scan_offsets[s] is (row, column); the row is at most 256 and the column at most 1792, both reached in every draw.
All inputs are finite; a program needn't handle non-finite values.
Results may differ from a plain program's by a relative error of at most 0.025.
Values may be sent and summed in bfloat16 or wider, within the bound.
No kernel may reach another device: no remote copies, remote signals or barrier semaphores. Data moves between devices by JAX's collectives and lax.ppermute only.
A program may use at most 128 MiB of HBM per device.

v0:
```python
import functools

import jax
import jax.numpy as jnp
import ml_dtypes
import numpy as np
from jax import lax
from jax.experimental import pallas as pl
from jax.experimental.pallas import tpu as pltpu
from jax.sharding import PartitionSpec as P

FRESNEL = 0.37
BF16 = jnp.bfloat16
F32 = jnp.float32


def split_tables(points):
    half = points // 2
    counter = np.arange(points)
    angle = (2.0 * np.pi / points * (counter[:, None] * counter[None, :] % points)).astype(np.float32)
    factor = np.float32(1.0) / np.sqrt(np.float32(points))
    table_re = np.cos(angle) * factor
    table_im = -np.sin(angle) * factor

    def stacked(rows):
        re, im = table_re[rows, :half], table_im[rows, :half]
        return np.block([[re, -im], [im, re]]).astype(ml_dtypes.bfloat16)

    even, odd = stacked(slice(0, None, 2)), stacked(slice(1, None, 2))
    tables = np.stack([even, odd, even.T, odd.T])
    order = np.concatenate([counter[0::2], counter[1::2]])
    shifted = ((order + half) % points - half).astype(np.float64)
    phase = np.pi * FRESNEL / points * (shifted[:, None] ** 2 + shifted[None, :] ** 2)
    kernel = np.stack([np.cos(phase), -np.sin(phase)]).astype(np.float32)
    mover = np.zeros((points, points), np.float32)
    mover[counter, order] = 1.0
    mover = np.stack([mover, mover.T]).astype(ml_dtypes.bfloat16)
    return tables, kernel, mover


def dot(a, b):
    return jnp.dot(a, b, preferred_element_type=F32)


def fold_rows(re, im):
    half = re.shape[0] // 2
    top = jnp.concatenate([re[:half], im[:half]], axis=0)
    bottom = jnp.concatenate([re[half:], im[half:]], axis=0)
    return (top + bottom).astype(BF16), (top - bottom).astype(BF16)


def join_parts(values, axis):
    return jnp.concatenate(values, axis=axis)


def forward_folded(folded, tables):
    half = folded[0][0].shape[0] // 2
    evens = [dot(tables[0], even) for even, _ in folded]
    odds = [dot(tables[1], odd) for _, odd in folded]
    lanes = []
    for even, odd in zip(evens, odds):
        re = join_parts([even[:half], odd[:half]], 0)
        im = join_parts([even[half:], odd[half:]], 0)
        left = join_parts([re[:, :half], im[:, :half]], 1)
        right = join_parts([re[:, half:], im[:, half:]], 1)
        lanes.append(((left + right).astype(BF16), (left - right).astype(BF16)))
    evens = [dot(even, tables[2]) for even, _ in lanes]
    odds = [dot(odd, tables[3]) for _, odd in lanes]
    return [
        (join_parts([even[:, :half], odd[:, :half]], 1), join_parts([even[:, half:], odd[:, half:]], 1))
        for even, odd in zip(evens, odds)
    ]


def inverse(fields, tables):
    half = fields[0][0].shape[0] // 2
    low = [(re.astype(BF16), im.astype(BF16)) for re, im in fields]
    evens = [dot(tables[2], join_parts([re[:half], im[:half]], 0)) for re, im in low]
    odds = [dot(tables[3], join_parts([re[half:], im[half:]], 0)) for re, im in low]
    lanes = []
    for even, odd in zip(evens, odds):
        total, rest = (even + odd).astype(BF16), (even - odd).astype(BF16)
        re = join_parts([total[:half], rest[:half]], 0)
        im = join_parts([total[half:], rest[half:]], 0)
        lanes.append((join_parts([re[:, :half], im[:, :half]], 1), join_parts([re[:, half:], im[:, half:]], 1)))
    evens = [dot(even, tables[0]) for even, _ in lanes]
    odds = [dot(odd, tables[1]) for _, odd in lanes]
    out = []
    for even, odd in zip(evens, odds):
        total, rest = even + odd, even - odd
        re = join_parts([total[:, :half], rest[:, :half]], 1)
        im = join_parts([total[:, half:], rest[:, half:]], 1)
        out.append((re, im))
    return out


def times(a_re, a_im, b_re, b_im):
    return a_re * b_re - a_im * b_im, a_re * b_im + a_im * b_re


def conj_times(a_re, a_im, b_re, b_im):
    return a_re * b_re + a_im * b_im, a_re * b_im - a_im * b_re


def load_complex(ref, *lead):
    return ref[(*lead, 0)].astype(F32), ref[(*lead, 1)].astype(F32)


VM = pl.BlockSpec(memory_space=pltpu.VMEM)
SM = pl.BlockSpec(memory_space=pltpu.SMEM)
HB = pl.BlockSpec(memory_space=pltpu.HBM)
VK = object()


def call(body, inputs, specs, outs, scratch=(), out_specs=None, name=None, us=0.1, mib=8, keep=()):
    return pl.pallas_call(
        body,
        out_shape=[
            pltpu.VMEM(shape, dtype) if at in keep else jax.ShapeDtypeStruct(shape, dtype)
            for at, (shape, dtype) in enumerate(outs)
        ],
        in_specs=[VM if spec is VK else spec for spec in specs],
        out_specs=[VM] * len(outs) if out_specs is None else out_specs,
        scratch_shapes=list(scratch),
        compiler_params=pltpu.CompilerParams(vmem_limit_bytes=mib * 1024 * 1024),
        cost_estimate=pl.CostEstimate(flops=int(us * 1e9), bytes_accessed=int(us * 3e6), transcendentals=0),
        name=name,
    )(
        *(
            pltpu.with_memory_space_constraint(value, pltpu.VMEM) if spec is VK else value
            for value, spec in zip(inputs, specs)
        )
    )


def fetch(sources, targets, sems):
    copies = [pltpu.make_async_copy(s, t, sems.at[at]) for at, (s, t) in enumerate(zip(sources, targets))]
    for copy in copies:
        copy.start()
    return copies


def slot_at(plan, tiles, turn):
    place = plan[3, 0] * tiles + (plan[3, 1] ^ turn)
    return plan[1, place], plan[2, place]


def first_kernel(groups, tiles, points, counts, offsets, strip_far, amplitudes_far, *refs):
    strips = refs[:tiles]
    same, remote, nearby, plan_out, plan, strip, amplitudes, sems = refs[tiles:]
    layers, rows = strip.shape[0], strip.shape[2]
    slots = amplitudes.shape[0]
    n = offsets.shape[0]
    strip_copy = pltpu.make_async_copy(strip_far, strip, sems.at[1])
    strip_copy.start()
    amplitude_copy = pltpu.make_async_copy(amplitudes_far, amplitudes, sems.at[2])
    amplitude_copy.start()
    pos, tile = lax.axis_index("pos"), lax.axis_index("tile")
    width = plan_out.shape[1]

    number = lax.broadcasted_iota(jnp.int32, (n, 1), 0)
    live = jnp.zeros((n, 1), jnp.int32)
    for group in range(groups):
        live += jnp.where((number >= group * slots) & (number < group * slots + counts[group]), 1, 0)
    row, col = offsets[:, 0:1].astype(F32), offsets[:, 1:2].astype(F32)
    number = number.astype(F32)
    key = jnp.where(live > 0, col, float(1 << 12)) * n + number
    square = (n, n)
    eye = lax.broadcasted_iota(jnp.int32, square, 0) == lax.broadcasted_iota(jnp.int32, square, 1)
    across = jnp.sum(jnp.where(eye, key, 0.0), axis=0, keepdims=True)
    rank = jnp.sum(jnp.where(across < key, 1.0, 0.0), axis=1, keepdims=True).astype(jnp.int32)
    here = lax.broadcasted_iota(jnp.int32, (n, width), 1) == rank
    chosen = [
        jnp.sum(jnp.where(here, value, 0.0), axis=0, keepdims=True).astype(jnp.int32)
        for value in (number, row, col)
    ]
    lane = lax.broadcasted_iota(jnp.int32, (1, width), 1)
    outer = 2 * points
    lowest = jnp.maximum(sum(jnp.where(lane >= i * 2 * tiles, 1, 0) for i in range(1, groups // 2)) - 1, 0)
    far = (chosen[2] < lowest * outer) | (chosen[2] + points > (lowest + jnp.where(lane < 2 * tiles, 2, 3)) * outer)
    distant = jnp.max(jnp.where(far & (lane < groups * slots // 2), 1.0, 0.0), axis=1, keepdims=True)
    for at, value in enumerate(chosen):
        plan_out[at : at + 1, :] = value
    plan_out[3:4, :] = jnp.where(
        lane == 0, pos, jnp.where(lane == 1, tile, jnp.where(lane == 2, distant.astype(jnp.int32), 0))
    )
    plan_out[4:8, :] = jnp.zeros((4, width), jnp.int32)
    copy = pltpu.make_async_copy(plan_out, plan, sems.at[0])
    copy.start()
    copy.wait()
    strip_copy.wait()

    blocks = strip.shape[-1] // points
    lane = lax.broadcasted_iota(jnp.int32, (rows, points), 1)
    for turn in range(tiles):
        _, col = slot_at(plan, tiles, turn)
        block = col // points
        later = jnp.minimum(block + 1, blocks - 1)
        keep = lane >= col % points
        for layer in range(layers):
            for part in range(2):
                here = strip[layer, part, :, pl.ds(pl.multiple_of(block * points, points), points)]
                there = strip[layer, part, :, pl.ds(pl.multiple_of(later * points, points), points)]
                strips[turn][layer, part] = jnp.where(
                    keep, here.astype(F32), there.astype(F32)
                ).astype(BF16)
    amplitude_copy.wait()
    for turn in range(groups // 2):
        across_x = (nearby, remote)[turn // 2]
        for flip, out, at in ((0, same, turn), (1, across_x, turn % 2)):
            slot = plan[0, (pos ^ (2 * turn + flip)) * tiles + tile]

            @pl.when(slot // slots == pos)
            def _(out=out, at=at, slot=slot):
                out[at] = amplitudes[slot % slots]


def merge_kernel(tiles, slots, turns, plan, same, came, *outs):
    pos, tile = plan[3, 0], plan[3, 1]
    for at, (turn, out) in enumerate(zip(turns, outs)):
        source = plan[0, (pos ^ (2 * turn)) * tiles + tile] // slots

        @pl.when(source == pos)
        def _(turn=turn, out=out):
            out[...] = same[turn]

        @pl.when(source == (pos ^ 1))
        def _(at=at, out=out):
            out[...] = came[at]


def join(tiles, points, plan, strips, layer, whole, out):
    own, one, two, three = strips
    rows = own.shape[2]
    row, col = slot_at(plan, tiles, 0)
    core, up = plan[3, 1] % 2, plan[3, 1] // 2
    sub = lax.broadcasted_iota(jnp.int32, (rows, points), 0)
    for near, far, at in ((own, two, core), (one, three, 1 - core)):
        low = jnp.where(sub + at * rows >= row, 0, 1)
        for part in range(2):
            whole[part, pl.ds(pl.multiple_of(at * rows, rows), rows)] = jnp.where(
                low == up, near[layer, part].astype(F32), far[layer, part].astype(F32)
            )
    for part in range(2):
        value = pltpu.roll(whole[part], (points - row % points) % points, 0)
        out[part] = pltpu.roll(value, (points - col % points) % points, 1).astype(BF16)


def forward(probes, first, second, tables, kernel, phi, far):
    modes = probes[0].shape[0]
    fields = []
    for probe in probes:
        for mode in range(modes):
            fields.append(fold_rows(*times(*load_complex(probe, mode), *load_complex(first))))
    fields = forward_folded(fields, tables)
    fields = inverse([times(re, im, kernel[0], kernel[1]) for re, im in fields], tables)
    folded = []
    for at, (re, im) in enumerate(fields):
        phi[at, 0], phi[at, 1] = re.astype(BF16), im.astype(BF16)
        folded.append(fold_rows(*times(re, im, *load_complex(second))))
    fields = forward_folded(folded, tables)
    power = None
    for at, (re, im) in enumerate(fields):
        far[at, 0], far[at, 1] = re.astype(BF16), im.astype(BF16)
        square = re * re + im * im
        power = square if power is None else power + square
    return power


def put_by_residue(plan, tiles, points, total, own, other):
    row, col = slot_at(plan, tiles, 0)
    core = plan[3, 1] % 2
    rows = points // 2
    for part in range(2):
        total[part] = pltpu.roll(pltpu.roll(total[part], row % points, 0), col % points, 1)
    for out, at in ((own, core), (other, 1 - core)):
        for part in range(2):
            out[part] = total[part, pl.ds(pl.multiple_of(at * rows, rows), rows)].astype(BF16)


def ahead_kernel(tiles, points, plan, *refs):
    strips, near, beside, across, diagonal, tables_far, kernel_far = refs[:4], *refs[4:10]
    first, second, phi, far, power = refs[10:15]
    mine, tables, kernel, whole, sems = refs[15:]
    copies = fetch((near, tables_far, kernel_far), (mine, tables, kernel), sems)
    join(tiles, points, plan, strips, 0, whole, first)
    join(tiles, points, plan, strips, 1, whole, second)
    for copy in copies:
        copy.wait()
    size = phi.shape[0] // 2
    power[...] = forward((mine, beside), first, second, tables, kernel, phi.at[:size], far.at[:size])
    power[...] += forward((across, diagonal), first, second, tables, kernel, phi.at[size:], far.at[size:])


def back_kernel(tiles, points, slots, plan, *refs):
    power, phi, far, second, tables_far, mover_far = refs[:6]
    arrived = refs[6:10]
    own, other, inner = refs[10:13]
    tables, mover, amplitude, total, ratio, sems = refs[13:]
    copies = fetch((mover_far, tables_far), (mover, tables), sems)
    source = plan[0, plan[3, 0] * tiles + plan[3, 1]] // slots
    for turn, ref in enumerate(arrived):

        @pl.when(((source ^ plan[3, 0]) >> 1) == turn)
        def _(ref=ref):
            amplitude[...] = ref[...]

    for copy in copies:
        copy.wait()
    measured = dot(dot(mover[0], amplitude[...]).astype(BF16), mover[1])
    ratio[...] = 1.0 - measured / jnp.sqrt(power[...] + 1.0)
    total[...] = jnp.zeros_like(total)
    size = phi.shape[0] // 2
    for start in (0, size):
        fields = []
        for at in range(start, start + size):
            re, im = load_complex(far, at)
            fields.append((re * ratio[...], im * ratio[...]))
        fields = inverse(fields, tables)
        for at, (re, im) in enumerate(fields, start):
            grad_re, grad_im = conj_times(*load_complex(phi, at), re, im)
            total[0] += grad_re
            total[1] += grad_im
            inner[at, 0], inner[at, 1] = fold_rows(*conj_times(*load_complex(second), re, im))
    put_by_residue(plan, tiles, points, total, own, other)


def last_kernel(tiles, points, plan, *refs):
    inner, near, beside, across, diagonal, first, tables_far, kernel_far = refs[:8]
    own, other, near_grad, beyond_grad, beside_grad = refs[8:13]
    mine, tables, kernel, total, sems = refs[13:]
    copies = fetch((tables_far, kernel_far, near), (tables, kernel, mine), sems)
    modes = mine.shape[0]
    probes = (mine, beside, across, diagonal)
    grads = (near_grad, beside_grad.at[0], beyond_grad, beside_grad.at[1])
    total[...] = jnp.zeros_like(total)
    for copy in copies:
        copy.wait()
    for start in range(0, tiles, 2):
        which = [(turn, mode) for turn in range(start, start + 2) for mode in range(modes)]
        fields = forward_folded([(inner[t * modes + m, 0], inner[t * modes + m, 1]) for t, m in which], tables)
        fields = inverse([conj_times(kernel[0], kernel[1], re, im) for re, im in fields], tables)
        for (turn, mode), (re, im) in zip(which, fields):
            grad_re, grad_im = conj_times(*load_complex(probes[turn], mode), re, im)
            total[0] += grad_re
            total[1] += grad_im
            re, im = conj_times(*load_complex(first), re, im)
            grads[turn][mode, 0], grads[turn][mode, 1] = re.astype(BF16), im.astype(BF16)
    put_by_residue(plan, tiles, points, total, own, other)


def place_kernel(tiles, points, plan, *refs):
    pieces, (below, same, above, canvas) = refs[:tiles], refs[tiles:]
    rows = pieces[0].shape[1]
    core, up = plan[3, 1] % 2, plan[3, 1] // 2
    base = plan[3, 0] // 2 * 2 - 2
    sub = lax.broadcasted_iota(jnp.int32, (rows, points), 0) + core * rows
    lane = lax.broadcasted_iota(jnp.int32, (rows, points), 1)
    canvas[...] = jnp.zeros_like(canvas)
    for turn in range(tiles):
        row, col = slot_at(plan, tiles, turn)
        mine = jnp.where(sub >= row, 0, 1) == up
        early = lane >= col % points
        for part in range(2):
            value = jnp.where(mine, pieces[turn][part].astype(F32), 0.0)
            for step, keep in ((0, early), (1, ~early)):
                at = col // points + step - base
                at = jnp.where((at >= 0) & (at < 6), at, 6)
                canvas[at, part] += jnp.where(keep, value, 0.0)
    below[...] = canvas[0:2].astype(BF16)
    same[...] = canvas[2:4]
    above[...] = canvas[4:6].astype(BF16)


def split_kernel(plan, same, low, high, keep, send):
    x_at = plan[3, 0] % 2
    keep[...] = same[x_at] + low[x_at].astype(F32) + high[x_at].astype(F32)
    other = same[1 - x_at] + low[1 - x_at].astype(F32) + high[1 - x_at].astype(F32)
    send[...] = other.astype(BF16)


def end_kernel(layers, *refs):
    extra, out = refs[-2:]
    for layer in range(layers):
        out[layer] = refs[layer][...] + refs[layers + layer][...].astype(F32) + extra[layer].astype(F32)


def spread_kernel(plan, mine, beyond, came, keep, send):
    pos = plan[3, 0]
    rows = keep.shape[-2]
    for which, near in enumerate((mine, beyond)):
        for turn in range(keep.shape[1]):
            for flip in range(2):
                at = pl.ds(pl.multiple_of((pos ^ (2 * turn + flip)) * rows, rows), rows)
                total = near[:, :, at].astype(F32) + came[which, :, :, at].astype(F32)
                if flip:
                    send[which, turn] = total.astype(BF16)
                else:
                    keep[which, turn] = total


def fold_kernel(near, came, keep, send):
    keep[...] = near[0] + came[0].astype(F32)
    send[...] = (near[1] + came[1].astype(F32)).astype(BF16)


def gather_kernel(near, came, own, *sends):
    own[...] = near[0] + came[0].astype(F32)
    for turn, send in enumerate(sends, 1):
        send[...] = (near[turn] + came[turn].astype(F32)).astype(BF16)


def total_kernel(*refs):
    total = refs[0][...]
    for ref in refs[1:-1]:
        total = total + ref[...].astype(F32)
    refs[-1][...] = total


def turned(value, turn, tiles):
    return lax.ppermute(value, "tile", [(i, i ^ turn) for i in range(tiles)])


def distant_blocks(plan, pieces, tiles, points, groups):
    rows = pieces[0][0].shape[1]
    pos, tile = plan[3, 0], plan[3, 1]
    sub = (jnp.arange(rows, dtype=jnp.int32) + tile % 2 * rows)[:, None]
    lane = jnp.arange(points, dtype=jnp.int32)[None, :]
    block = jnp.arange(groups, dtype=jnp.int32)
    outside = jnp.abs(block // 2 - pos // 2) > 1
    canvas = 0.0
    for turn in range(tiles):
        place = pos * tiles + (tile ^ turn)
        row, col = jnp.take(plan[1], place), jnp.take(plan[2], place)
        mine = jnp.where(sub >= row, 0, 1) == tile // 2
        target = col // points + jnp.where(lane >= col % points, 0, 1)
        keep = outside[:, None, None] & mine[None] & (target[None] == block[:, None, None])
        value = jnp.stack([layer[turn] for layer in pieces]).astype(F32)
        canvas = canvas + jnp.where(keep[:, None, None], value[None], 0.0)
    shares = lax.all_to_all(canvas.astype(BF16), "pos", split_axis=0, concat_axis=0, tiled=True)
    return jnp.sum(shares.astype(F32), axis=0).astype(BF16)


def on_device_by_slot(probe_modes, object_slices, amplitudes, scan_offsets, slot_counts):
    groups, tiles = lax.axis_size("pos"), lax.axis_size("tile")
    slots, points = amplitudes.shape[0], amplitudes.shape[-1]
    layers, rows = object_slices.shape[0], object_slices.shape[2]
    modes = probe_modes.shape[0]
    tables, kernel, mover = (jnp.asarray(t) for t in split_tables(points))
    field = (2, points, points)

    low = probe_modes.astype(BF16)
    low, scan_offsets = lax.optimization_barrier((low, scan_offsets))
    across = turned(low, 2, tiles)
    beside = turned(low, 1, tiles)
    shot = (points, points)
    outs = call(
        functools.partial(first_kernel, groups, tiles, points),
        (slot_counts, scan_offsets, object_slices, amplitudes),
        [SM, VM, HB, HB],
        [((layers, 2, rows, points), BF16)] * tiles
        + [((groups // 2, *shot), BF16)]
        + [((groups // 4, *shot), BF16)] * 2
        + [((8, 128), jnp.int32)],
        [
            pltpu.SMEM((8, 128), jnp.int32),
            pltpu.VMEM(object_slices.shape, BF16),
            pltpu.VMEM(amplitudes.shape, BF16),
            pltpu.SemaphoreType.DMA((3,)),
        ],
        name="first",
        us=5.0,
        mib=16,
    )
    (*cut, same, far, near, plan) = outs
    across, cut = lax.optimization_barrier((across, cut))
    aside = [(i, i ^ 1) for i in range(groups)]
    merged = [None] * (groups // 2)
    for turns, value in (((2, 3), far), ((0, 1), near)):
        merged[turns[0]], merged[turns[1]] = call(
            functools.partial(merge_kernel, tiles, slots, turns),
            (plan, same, lax.ppermute(value, "pos", aside)),
            [SM, VM, VM],
            [(shot, BF16)] * 2,
            name="merge",
        )
    arrived = [merged[0]] + [
        lax.ppermute(merged[turn], "pos", [(i, i ^ (2 * turn)) for i in range(groups)])
        for turn in range(1, groups // 2)
    ]
    strips = [cut[0]] + [turned(cut[turn], turn, tiles) for turn in range(1, tiles)]
    probes = [probe_modes, beside, across, turned(across, 1, tiles)]
    half = ((2, points // 2, points), BF16)
    stack = (tiles * modes, *field)
    first, second, phi, far, power = call(
        functools.partial(ahead_kernel, tiles, points),
        (plan, *strips, *probes, tables, kernel),
        [SM] + [VK] * tiles + [HB] + [VK] * 3 + [HB] * 2,
        [(field, BF16), (field, BF16), (stack, BF16), (stack, BF16), ((points, points), F32)],
        [
            pltpu.VMEM(probe_modes.shape, F32),
            pltpu.VMEM(tables.shape, BF16),
            pltpu.VMEM(kernel.shape, F32),
            pltpu.VMEM(field, F32),
            pltpu.SemaphoreType.DMA((3,)),
        ],
        name="ahead",
        us=12.0,
        mib=24,
        keep=range(5),
    )
    own, other, inner = call(
        functools.partial(back_kernel, tiles, points, slots),
        (plan, power, phi, far, second, tables, mover, *arrived),
        [SM] + [VK] * 4 + [HB] * 2 + [VM] * len(arrived),
        [half, half, (stack, BF16)],
        [
            pltpu.VMEM(tables.shape, BF16),
            pltpu.VMEM(mover.shape, BF16),
            pltpu.VMEM((points, points), BF16),
            pltpu.VMEM(field, F32),
            pltpu.VMEM((points, points), F32),
            pltpu.SemaphoreType.DMA((2,)),
        ],
        name="back",
        us=5.0,
        mib=24,
        keep=(2,),
    )
    pieces = [None] * layers
    pieces[1] = [own] + [turned(v, turn, tiles) for turn, v in ((1, other), (2, own), (3, other))]
    own, other, mine, beyond, beside = call(
        functools.partial(last_kernel, tiles, points),
        (plan, inner, *probes, first, tables, kernel),
        [SM, VK, HB] + [VK] * 4 + [HB] * 2,
        [half, half] + [((modes, *field), BF16)] * 2 + [((2, modes, *field), BF16)],
        [
            pltpu.VMEM(probe_modes.shape, F32),
            pltpu.VMEM(tables.shape, BF16),
            pltpu.VMEM(kernel.shape, F32),
            pltpu.VMEM(field, F32),
            pltpu.SemaphoreType.DMA((3,)),
        ],
        name="last",
        us=6.0,
        mib=24,
    )
    pieces[1], own, other, beside = lax.optimization_barrier((pieces[1], own, other, beside))
    pieces[0] = [own] + [turned(v, turn, tiles) for turn, v in ((1, other), (2, own), (3, other))]
    share = (groups // 2, modes, 2, points // groups, points)
    keep, send = call(
        spread_kernel,
        (plan, mine, beyond, turned(beside, 1, tiles)),
        [SM] + [VM] * 3,
        [((2, *share), F32), ((2, *share), BF16)],
        name="spread",
    )
    keep, send = call(
        fold_kernel,
        (keep, lax.ppermute(send, "pos", aside)),
        [VM] * 2,
        [(share, F32), (share, BF16)],
        name="fold",
    )
    own, *sends = call(
        gather_kernel,
        (keep, turned(send, 2, tiles)),
        [VM] * 2,
        [(share[1:], F32)] + [(share[1:], BF16)] * (groups // 2 - 1),
        name="gather",
    )
    came = [
        lax.ppermute(send, "pos", [(i, i ^ (2 * turn)) for i in range(groups)]) for turn, send in enumerate(sends, 1)
    ]
    (probe_grad,) = call(total_kernel, (own, *came), [VM] * (1 + len(came)), [(share[1:], F32)], name="total")

    block = (2, rows, points)
    keeps, swapped = [None] * layers, [None] * layers
    for layer in reversed(range(layers)):
        below, same, above = call(
            functools.partial(place_kernel, tiles, points),
            (plan, *pieces[layer]),
            [SM] + [VM] * tiles,
            [((2, *block), BF16), ((2, *block), F32), ((2, *block), BF16)],
            [pltpu.VMEM((7, *block), F32)],
            name="place",
        )
        if layer:
            pieces[0], above, below = lax.optimization_barrier((pieces[0], above, below))
        low_in = lax.ppermute(above, "pos", [(i, i + 2) for i in range(groups - 2)])
        high_in = lax.ppermute(below, "pos", [(i + 2, i) for i in range(groups - 2)])
        if layer == 0:
            pieces, low_in = lax.optimization_barrier((pieces, low_in))
        keeps[layer], send = call(
            split_kernel,
            (plan, same, low_in, high_in),
            [SM] + [VM] * 3,
            [(block, F32), (block, BF16)],
            name="split",
        )
        swapped[layer] = lax.ppermute(send, "pos", [(i, i ^ 1) for i in range(groups)])
    extra = lax.cond(
        plan[3, 2] > 0,
        lambda p: distant_blocks(plan, p, tiles, points, groups),
        lambda p: jnp.zeros((layers, *block), BF16),
        pieces,
    )
    (object_grad,) = call(
        functools.partial(end_kernel, layers),
        (*keeps, *swapped, extra),
        [VM] * (2 * layers + 1),
        [((layers, *block), F32)],
        name="end",
    )
    return object_grad, probe_grad


def make_tables(points):
    counter = jnp.arange(points, dtype=jnp.int32)
    product = counter[:, None] * counter[None, :] % points
    angle = 2.0 * jnp.pi / points * product.astype(jnp.float32)
    factor = 1.0 / jnp.sqrt(jnp.float32(points))
    table_re = (jnp.cos(angle) * factor).astype(jnp.bfloat16)
    table_im = (-jnp.sin(angle) * factor).astype(jnp.bfloat16)
    shifted = ((counter + points // 2) % points - points // 2).astype(jnp.float32)
    phase = (
        jnp.pi
        * FRESNEL
        / points
        * (shifted[:, None] * shifted[:, None] + shifted[None, :] * shifted[None, :])
    )
    kernel = jnp.stack([jnp.cos(phase), -jnp.sin(phase)])
    return (table_re, table_im, kernel)


def times_complex(first, second):
    real_part = (
        first[..., 0, :, :] * second[..., 0, :, :] - first[..., 1, :, :] * second[..., 1, :, :]
    )
    imag_part = (
        first[..., 0, :, :] * second[..., 1, :, :] + first[..., 1, :, :] * second[..., 0, :, :]
    )
    return jnp.stack([real_part, imag_part], axis=-3)


def conjugate(values):
    return jnp.stack([values[..., 0, :, :], -values[..., 1, :, :]], axis=-3)


def transform_many(values, table_re, table_im):
    tables = jnp.stack([table_re, table_im])
    lowered = values.astype(jnp.bfloat16)
    first = jnp.einsum("gab,nmtbc->nmgtac", tables, lowered, preferred_element_type=jnp.float32)
    middle = jnp.stack(
        [first[:, :, 0, 0] - first[:, :, 1, 1], first[:, :, 0, 1] + first[:, :, 1, 0]], axis=2
    ).astype(jnp.bfloat16)
    second = jnp.einsum("nmtab,gbc->nmtgac", middle, tables, preferred_element_type=jnp.float32)
    return jnp.stack(
        [second[:, :, 0, 0] - second[:, :, 1, 1], second[:, :, 0, 1] + second[:, :, 1, 0]], axis=2
    )


def propagate_many(values, table_re, table_im, kernel):
    return transform_many(
        times_complex(transform_many(values, table_re, table_im), kernel), table_re, -table_im
    )


def window_anchor(place):
    zero_index = jnp.int32(0)
    return (zero_index, zero_index, place[0], place[1])


def on_device_by_mode(probe_modes, object_slices, amplitudes, scan_offsets, slot_counts):
    group = lax.axis_index("pos")
    groups = lax.axis_size("pos")
    tile_at = lax.axis_index("tile")
    strips = lax.axis_size("tile")
    slots = amplitudes.shape[0]
    points = amplitudes.shape[-1]
    layers = object_slices.shape[0]
    strip_rows = object_slices.shape[2]
    starts = jnp.cumsum(slot_counts) - slot_counts
    share = slots // 2
    wanted = jnp.arange(groups * share, dtype=jnp.int32)
    within = wanted - starts[group]
    usable = (within >= 0) & (within < slot_counts[group])
    picked = jnp.take(amplitudes, jnp.clip(within, 0, slots - 1), axis=0)
    outgoing = jnp.where(usable[:, None, None], picked, jnp.zeros_like(picked))
    arrived_rows = lax.all_to_all(outgoing, "pos", split_axis=0, concat_axis=0, tiled=True)
    mine = group * share + jnp.arange(share, dtype=jnp.int32)
    source = jnp.sum((starts[None, :] <= mine[:, None]).astype(jnp.int32), axis=1) - 1
    amplitude = jnp.take(arrived_rows, source * share + jnp.arange(share, dtype=jnp.int32), axis=0)
    places = jnp.take(scan_offsets, source * slots + mine - starts[source], axis=0)
    alive = jnp.ones((share,), jnp.float32)
    padded = jnp.pad(object_slices, ((0, 0), (0, 0), (points, points), (0, 0)))

    def cut_piece(place):
        local_row = jnp.clip(place[0] - tile_at * strip_rows + points, 0, strip_rows + points)
        shifted_place = jnp.stack([local_row, place[1]])
        return lax.dynamic_slice(padded, window_anchor(shifted_place), (layers, 2, points, points))

    pieces = jax.vmap(cut_piece)(places).astype(jnp.float32)
    windows = lax.psum(pieces.astype(jnp.bfloat16), "tile").astype(jnp.float32)
    table_re, table_im, kernel = make_tables(points)
    kernel_conj = conjugate(kernel)
    current = times_complex(probe_modes[None], windows[:, None, 0])
    layer_at = 1
    arrived = propagate_many(current, table_re, table_im, kernel)
    entering = [arrived]
    current = times_complex(arrived, windows[:, None, layer_at])
    far_field = transform_many(current, table_re, table_im)
    partial_power = jnp.sum(far_field * far_field, axis=(1, 2))
    power = lax.psum(partial_power.astype(jnp.bfloat16), "tile").astype(jnp.float32)
    ratio = (1.0 - amplitude.astype(jnp.float32) / jnp.sqrt(power + 1.0)) * alive[:, None, None]
    incoming = transform_many(ratio[:, None, None] * far_field, table_re, -table_im)
    object_terms = [None] * layers
    layer_at = 1
    object_terms[layer_at] = jnp.sum(
        times_complex(conjugate(entering[layer_at - 1]), incoming), axis=1
    )
    incoming = propagate_many(
        times_complex(conjugate(windows[:, None, layer_at]), incoming),
        table_re,
        table_im,
        kernel_conj,
    )
    object_terms[0] = jnp.sum(times_complex(conjugate(probe_modes[None]), incoming), axis=1)
    probe_term = jnp.sum(times_complex(conjugate(windows[:, None, 0]), incoming), axis=0)
    slot_grads = jnp.stack(object_terms, axis=1)
    canvas = jnp.zeros((layers, 2, strip_rows * strips, object_slices.shape[3]), jnp.float32)

    def deposit(canvas, packed):
        place, term = packed
        anchor = window_anchor(place)
        current_part = lax.dynamic_slice(canvas, anchor, term.shape)
        return (lax.dynamic_update_slice(canvas, current_part + term, anchor), None)

    canvas, unused = lax.scan(deposit, canvas, (places, slot_grads))
    column_part = lax.psum_scatter(
        canvas.astype(jnp.bfloat16), "pos", scatter_dimension=3, tiled=True
    )
    object_grad = lax.psum_scatter(column_part, "tile", scatter_dimension=2, tiled=True).astype(
        jnp.float32
    )
    probe_grad = lax.psum_scatter(
        probe_term.astype(jnp.bfloat16), "pos", scatter_dimension=2, tiled=True
    ).astype(jnp.float32)
    return (object_grad, probe_grad)


def solution(mesh):
    in_specs = (
        P("tile", None, None, None),
        P(None, None, "tile", None),
        P("pos", None, None),
        P(),
        P(),
    )
    out_specs = (P(None, None, "tile", "pos"), P("tile", None, "pos", None))
    by_slot = mesh.shape["tile"] == 4 and mesh.shape["pos"] == 8
    return jax.shard_map(
        on_device_by_slot if by_slot else on_device_by_mode,
        mesh=mesh,
        in_specs=in_specs,
        out_specs=out_specs,
        check_vma=False,
    )
```

profile of v0, /device:TPU:0, one launch (start us, length us, event | category | flops | bytes accessed | tf_op | source)
XLA Modules:
  0.0 101.9 jit_solution(7651635401470740919)
XLA Ops:
  0.6 1.3 %convert_element_type.42 = bf16[2,2,256,256]{3,2,1,0:T(8,128)(2,1)S(1)} convert(f32[2,2,256,256]{3,2,1,0:T(8,128)} %refs_1_.1) | non-fusion elementwise | flops 262144 | bytes 1572864 | tf_op jit(solution)/shard_map/convert_element_type | solution.py:452
  1.9 3.0 %collective-permute-start = (bf16[2,2,256,256]{3,2,1,0:T(8,128)(2,1)S(1)}, bf16[2,2,256,256]{3,2,1,0:T(8,128)(2,1)S(1)}, u32[]{:S(2)}, u32[]{:S(2)}) collective-permute-start(bf16[2,2,256,256]{3,2,1,0:T(8,128)(2,1)S(1)} %convert_element_type.42), channel_id=1, source_target_pairs={{0,2},{1,3},{2,0},{3,1},{4,6},{5,7},{6,4},{7,5},{8,10},{9,11},{10,... | collective-permute-start | bytes 1572872 | tf_op jit(solution)/shard_map/ppermute | solution.py:421
  4.9 0.0 collective-permute-start.4
  4.9 0.8 copy.11.offsets
  5.7 1.6 %copy-done.1 = bf16[2,2,128,2048]{3,2,1,0:T(8,128)(2,1)S(1)} copy-done((bf16[2,2,128,2048]{3,2,1,0:T(8,128)(2,1)S(1)}, bf16[2,2,128,2048]{3,2,1,0:T(8,128)(2,1)}, u32[]{:S(2)}) %copy-start.1) | copy-done | bytes 2097176
  7.3 1.2 %copy-done.2 = bf16[8,256,256]{2,1,0:T(8,128)(2,1)S(1)} copy-done((bf16[8,256,256]{2,1,0:T(8,128)(2,1)S(1)}, bf16[8,256,256]{2,1,0:T(8,128)(2,1)}, u32[]{:S(2)}) %copy-start.2) | copy-done | bytes 1048600
  8.5 0.7 copy-done.3
  9.2 2.1 %first.1 = (bf16[2,2,128,256]{3,2,1,0:T(8,128)(2,1)S(1)}, bf16[2,2,128,256]{3,2,1,0:T(8,128)(2,1)S(1)}, bf16[2,2,128,256]{3,2,1,0:T(8,128)(2,1)S(1)}, bf16[2,2,1...) custom-call(s32[8]{0:T(128)S(1)} %copy-done.3, ...), custom_call_target="tpu_custom_call" | custom-call | flops 5000000000 | bytes 15000000 | tf_op jit(solution)/shard_map/first/pallas_call | solution.py:116
  11.3 1.6 %collective-permute-start.8 = (bf16[2,256,256]{2,1,0:T(8,128)(2,1)S(1)}, bf16[2,256,256]{2,1,0:T(8,128)(2,1)S(1)}, u32[]{:S(2)}, u32[]{:S(2)}) collective-permute-start(bf16[2,256,256]{2,1,0:T(8,128)(2,1)S(1)} %get-tuple-element.124), channel_id=1, source_target_pairs={{0,4},{4,0},{8,12},{12,8},{16,20},{20,16},{24,28},{28,24},{1,5},{5... | collective-permute-start | bytes 786440 | tf_op jit(solution)/shard_map/ppermute | solution.py:482
  12.9 0.5 collective-permute-start.6
  13.4 3.5 %collective-permute-done.refs_6_.refs_3_ = bf16[2,2,256,256]{3,2,1,0:T(8,128)(2,1)S(1)} collective-permute-done((bf16[2,2,256,256]{3,2,1,0:T(8,128)(2,1)S(1)}, bf16[2,2,256,256]{3,2,1,0:T(8,128)(2,1)S(1)}, u32[]{:S(2)}, u32[]{:S(2)}) %collective-permute-start) | collective-permute-done | bytes 524320 | tf_op jit(solution)/shard_map/ppermute | solution.py:421
  16.9 0.5 collective-permute-start.1
  17.4 3.1 %collective-permute-done.8.came = bf16[2,256,256]{2,1,0:T(8,128)(2,1)S(1)} collective-permute-done((bf16[2,256,256]{2,1,0:T(8,128)(2,1)S(1)}, bf16[2,256,256]{2,1,0:T(8,128)(2,1)S(1)}, u32[]{:S(2)}, u32[]{:S(2)}) %collective-permute-start.8) | collective-permute-done | bytes 262176 | tf_op jit(solution)/shard_map/ppermute | solution.py:482
  20.5 0.2 collective-permute-start.2
  20.6 5.1 %collective-permute-done.6.came = bf16[2,256,256]{2,1,0:T(8,128)(2,1)S(1)} collective-permute-done((bf16[2,256,256]{2,1,0:T(8,128)(2,1)S(1)}, bf16[2,256,256]{2,1,0:T(8,128)(2,1)S(1)}, u32[]{:S(2)}, u32[]{:S(2)}) %collective-permute-start.6) | collective-permute-done | bytes 262176 | tf_op jit(solution)/shard_map/ppermute | solution.py:482
  25.7 0.0 collective-permute-start.3
  25.7 0.6 merge.3
  26.4 0.7 merge.2
  27.0 3.6 %collective-permute-start.10 = (bf16[256,256]{1,0:T(8,128)(2,1)S(1)}, bf16[256,256]{1,0:T(8,128)(2,1)S(1)}, u32[]{:S(2)}, u32[]{:S(2)}) collective-permute-start(bf16[256,256]{1,0:T(8,128)(2,1)S(1)} %get-tuple-element.126), channel_id=1, source_target_pairs={{0,24},{4,28},{8,16},{12,20},{16,8},{20,12},{24,0},{28,4},{1,25},{... | collective-permute-start | bytes 393224 | tf_op jit(solution)/shard_map/ppermute | solution.py:488
  30.7 0.0 collective-permute-done.1.refs_1_
  30.7 0.0 collective-permute-start.7
  30.7 0.0 collective-permute-done.2.refs_2_
  30.7 0.0 copy-start.6
  30.7 0.8 collective-permute-start.9
  31.5 2.7 %collective-permute-done.3.refs_3_ = bf16[2,2,128,256]{3,2,1,0:T(8,128)(2,1)S(1)} collective-permute-done((bf16[2,2,128,256]{3,2,1,0:T(8,128)(2,1)S(1)}, bf16[2,2,128,256]{3,2,1,0:T(8,128)(2,1)S(1)}, u32[]{:S(2)}, u32[]{:S(2)}) %collective-permute-start.3) | collective-permute-done | bytes 262176 | tf_op jit(solution)/shard_map/ppermute | solution.py:421
  34.2 0.0 collective-permute-done.5.refs_7_.refs_4_
  34.2 7.0 %ahead.1 = (bf16[2,256,256]{2,1,0:T(8,128)(2,1)S(1)}, bf16[2,256,256]{2,1,0:T(8,128)(2,1)S(1)}, bf16[8,2,256,256]{3,2,1,0:T(8,128)(2,1)S(1)}, bf16[8,2,256,256]{3,2,1,0:T(8,128)(2,1)S(1)}, f32[256,256]{1,0:T(8,128)S(1)}) custom-call(s32[8,128]{1,0:T(8,128)S(1)} %get-tuple-element.105.plan, bf16[2,2,128,256]{3,2,1,0:T(8,128)(2,1)S(1)} %get-tuple-element.111.refs_0_, ...), custom_call_target="tpu_custom_call" | custom-call | flops 12000000000 | bytes 36000000 | tf_op jit(solution)/shard_map/ahead/pallas_call | solution.py:116
  41.3 0.0 collective-permute-done.10.refs_9_
  41.3 0.0 collective-permute-done.7.refs_7_
  41.3 1.2 %collective-permute-done.9.refs_8_ = bf16[256,256]{1,0:T(8,128)(2,1)S(1)} collective-permute-done((bf16[256,256]{1,0:T(8,128)(2,1)S(1)}, bf16[256,256]{1,0:T(8,128)(2,1)S(1)}, u32[]{:S(2)}, u32[]{:S(2)}) %collective-permute-start.9) | collective-permute-done | bytes 131104 | tf_op jit(solution)/shard_map/ppermute | solution.py:488
  42.5 4.2 %back.1 = (bf16[2,128,256]{2,1,0:T(8,128)(2,1)S(1)}, bf16[2,128,256]{2,1,0:T(8,128)(2,1)S(1)}, bf16[8,2,256,256]{3,2,1,0:T(8,128)(2,1)S(1)}) custom-call(s32[8,128]{1,0:T(8,128)S(1)} %get-tuple-element.105.plan, f32[256,256]{1,0:T(8,128)S(1)} %get-tuple-element.116.refs_0_, bf16[8,2,256,256]{3,2,1,0:T(8,128)(2,1)S(1)} %get-tuple-element.117.refs_1_, ...), custom_call_target="tpu_custom_call" | custom-call | flops 5000000000 | bytes 15000000 | tf_op jit(solution)/shard_map/back/pallas_call | solution.py:116
  46.8 0.1 collective-permute-start.11
  46.8 1.6 %collective-permute-start.13 = (bf16[2,128,256]{2,1,0:T(8,128)(2,1)S(1)}, bf16[2,128,256]{2,1,0:T(8,128)(2,1)S(1)}, u32[]{:S(2)}, u32[]{:S(2)}) collective-permute-start(bf16[2,128,256]{2,1,0:T(8,128)(2,1)S(1)} %get-tuple-element.128), channel_id=1, source_target_pairs={{0,3},{1,2},{2,1},{3,0},{4,7},{5,6},{6,5},{7,4},{8,11},{9,10},{10,... | collective-permute-start | bytes 393224 | tf_op jit(solution)/shard_map/ppermute | solution.py:421
  48.5 0.5 collective-permute-start.12
  49.0 4.7 %last.1 = (bf16[2,128,256]{2,1,0:T(8,128)(2,1)S(1)}, bf16[2,128,256]{2,1,0:T(8,128)(2,1)S(1)}, bf16[2,2,256,256]{3,2,1,0:T(8,128)(2,1)S(1)}, bf16[2,2,256,256]{3...) custom-call(s32[8,128]{1,0:T(8,128)S(1)} %get-tuple-element.105.plan, ...), custom_call_target="tpu_custom_call" | custom-call | flops 6000000000 | bytes 18000000 | tf_op jit(solution)/shard_map/last/pallas_call | solution.py:116
  53.7 1.8 %collective-permute-done.12.refs_2_ = bf16[2,128,256]{2,1,0:T(8,128)(2,1)S(1)} collective-permute-done((bf16[2,128,256]{2,1,0:T(8,128)(2,1)S(1)}, bf16[2,128,256]{2,1,0:T(8,128)(2,1)S(1)}, u32[]{:S(2)}, u32[]{:S(2)}) %collective-permute-start.12) | collective-permute-done | bytes 131104 | tf_op jit(solution)/shard_map/ppermute | solution.py:421
  55.5 2.7 %collective-permute-done.23.came = bf16[2,2,2,256,256]{4,3,2,1,0:T(8,128)(2,1)S(1)} collective-permute-done((bf16[2,2,2,256,256]{4,3,2,1,0:T(8,128)(2,1)S(1)}, bf16[2,2,2,256,256]{4,3,2,1,0:T(8,128)(2,1)S(1)}, u32[]{:S(2)}, u32[]{:S(2)}) %collective-permute-start.23) | collective-permute-done | bytes 1048608 | tf_op jit(solution)/shard_map/ppermute | solution.py:421
  58.2 0.8 spread.1
  59.0 1.6 %collective-permute-start.24 = (bf16[2,4,2,2,32,256]{5,4,3,2,1,0:T(8,128)(2,1)S(1)}, bf16[2,4,2,2,32,256]{5,4,3,2,1,0:T(8,128)(2,1)S(1)}, u32[]{:S(2)}, u32[]{:S(2)}) collective-permute-start(bf16[2,4,2,2,32,256]{5,4,3,2,1,0:T(8,128)(2,1)S(1)} %get-tuple-element.169), channel_id=1, source_target_pairs={{0,4},{4,0},{8,12},{12,8},{16,20},{20,16},{24,28},{28,24},{1,5},{5... | collective-permute-start | bytes 1572872 | tf_op jit(solution)/shard_map/ppermute | solution.py:560
  60.6 1.5 %collective-permute-start.15 = (bf16[2,128,256]{2,1,0:T(8,128)(2,1)S(1)}, bf16[2,128,256]{2,1,0:T(8,128)(2,1)S(1)}, u32[]{:S(2)}, u32[]{:S(2)}) collective-permute-start(bf16[2,128,256]{2,1,0:T(8,128)(2,1)S(1)} %get-tuple-element.157.refs_0_), channel_id=1, source_target_pairs={{0,2},{1,3},{2,0},{3,1},{4,6},{5,7},{6,4},{7,5},{8,10},{9,11},{10,... | collective-permute-start | bytes 393224 | tf_op jit(solution)/shard_map/ppermute | solution.py:421
  62.1 0.4 collective-permute-start.16
  62.4 1.1 %place.2 = (bf16[2,2,128,256]{3,2,1,0:T(8,128)(2,1)S(1)}, f32[2,2,128,256]{3,2,1,0:T(8,128)S(1)}, bf16[2,2,128,256]{3,2,1,0:T(8,128)(2,1)S(1)}) custom-call(s32[8,128]{1,0:T(8,128)S(1)} %get-tuple-element.105.plan, bf16[2,128,256]{2,1,0:T(8,128)(2,1)S(1)} %get-tuple-element.158.refs_0_, bf16[2,128,256]{2,1,0:T(8,128)(2,1)S(1)} %collective-permute-done.11.refs_1_, ...), custom_call_target="tpu_custom_call" | custom-call | flops 100000000 | bytes 300000 | tf_op jit(solution)/shard_map/place/pallas_call | solution.py:116
  63.5 3.3 %collective-permute-done.15.refs_2_ = bf16[2,128,256]{2,1,0:T(8,128)(2,1)S(1)} collective-permute-done((bf16[2,128,256]{2,1,0:T(8,128)(2,1)S(1)}, bf16[2,128,256]{2,1,0:T(8,128)(2,1)S(1)}, u32[]{:S(2)}, u32[]{:S(2)}) %collective-permute-start.15) | collective-permute-done | bytes 131104 | tf_op jit(solution)/shard_map/ppermute | solution.py:421
  66.9 2.0 %collective-permute-done.16.refs_3_ = bf16[2,128,256]{2,1,0:T(8,128)(2,1)S(1)} collective-permute-done((bf16[2,128,256]{2,1,0:T(8,128)(2,1)S(1)}, bf16[2,128,256]{2,1,0:T(8,128)(2,1)S(1)}, u32[]{:S(2)}, u32[]{:S(2)}) %collective-permute-start.16) | collective-permute-done | bytes 131104 | tf_op jit(solution)/shard_map/ppermute | solution.py:421
  68.9 1.1 %place.3 = (bf16[2,2,128,256]{3,2,1,0:T(8,128)(2,1)S(1)}, f32[2,2,128,256]{3,2,1,0:T(8,128)S(1)}, bf16[2,2,128,256]{3,2,1,0:T(8,128)(2,1)S(1)}) custom-call(s32[8,128]{1,0:T(8,128)S(1)} %get-tuple-element.105.plan, bf16[2,128,256]{2,1,0:T(8,128)(2,1)S(1)} %get-tuple-element.157.refs_0_, bf16[2,128,256]{2,1,0:T(8,128)(2,1)S(1)} %collective-permute-done.14.refs_1_, ...), custom_call_target="tpu_custom_call" | custom-call | flops 100000000 | bytes 300000 | tf_op jit(solution)/shard_map/place/pallas_call | solution.py:116
  70.0 2.2 %collective-permute-start.17 = (bf16[2,2,128,256]{3,2,1,0:T(8,128)(2,1)S(1)}, bf16[2,2,128,256]{3,2,1,0:T(8,128)(2,1)S(1)}, u32[]{:S(2)}, u32[]{:S(2)}) collective-permute-start(bf16[2,2,128,256]{3,2,1,0:T(8,128)(2,1)S(1)} %get-tuple-element.147), channel_id=1, source_target_pairs={{0,8},{4,12},{8,16},{12,20},{16,24},{20,28},{1,9},{5,13},{9,17},{1... | collective-permute-start | bytes 786440 | tf_op jit(solution)/shard_map/ppermute | solution.py:590
  72.2 3.5 %collective-permute-start.19 = (bf16[2,2,128,256]{3,2,1,0:T(8,128)(2,1)S(1)}, bf16[2,2,128,256]{3,2,1,0:T(8,128)(2,1)S(1)}, u32[]{:S(2)}, u32[]{:S(2)}) collective-permute-start(bf16[2,2,128,256]{3,2,1,0:T(8,128)(2,1)S(1)} %get-tuple-element.152), channel_id=1, source_target_pairs={{0,8},{4,12},{8,16},{12,20},{16,24},{20,28},{1,9},{5,13},{9,17},{1... | collective-permute-start | bytes 786440 | tf_op jit(solution)/shard_map/ppermute | solution.py:590
  75.7 1.3 %collective-permute-start.20 = (bf16[2,2,128,256]{3,2,1,0:T(8,128)(2,1)S(1)}, bf16[2,2,128,256]{3,2,1,0:T(8,128)(2,1)S(1)}, u32[]{:S(2)}, u32[]{:S(2)}) collective-permute-start(bf16[2,2,128,256]{3,2,1,0:T(8,128)(2,1)S(1)} %get-tuple-element.153), channel_id=1, source_target_pairs={{8,0},{12,4},{16,8},{20,12},{24,16},{28,20},{9,1},{13,5},{17,9},{2... | collective-permute-start | bytes 786440 | tf_op jit(solution)/shard_map/ppermute | solution.py:591
  77.0 1.3 %collective-permute-start.18 = (bf16[2,2,128,256]{3,2,1,0:T(8,128)(2,1)S(1)}, bf16[2,2,128,256]{3,2,1,0:T(8,128)(2,1)S(1)}, u32[]{:S(2)}, u32[]{:S(2)}) collective-permute-start(bf16[2,2,128,256]{3,2,1,0:T(8,128)(2,1)S(1)} %get-tuple-element.149), channel_id=1, source_target_pairs={{8,0},{12,4},{16,8},{20,12},{24,16},{28,20},{9,1},{13,5},{17,9},{2... | collective-permute-start | bytes 786440 | tf_op jit(solution)/shard_map/ppermute | solution.py:591
  78.3 0.1 fold.1
  78.4 1.1 %collective-permute-start.25 = (bf16[4,2,2,32,256]{4,3,2,1,0:T(8,128)(2,1)S(1)}, bf16[4,2,2,32,256]{4,3,2,1,0:T(8,128)(2,1)S(1)}, u32[]{:S(2)}, u32[]{:S(2)}) collective-permute-start(bf16[4,2,2,32,256]{4,3,2,1,0:T(8,128)(2,1)S(1)} %get-tuple-element.171), channel_id=1, source_target_pairs={{0,2},{1,3},{2,0},{3,1},{4,6},{5,7},{6,4},{7,5},{8,10},{9,11},{10,... | collective-permute-start | bytes 786440 | tf_op jit(solution)/shard_map/ppermute | solution.py:421
  79.5 4.6 %collective-permute-done.19.low = bf16[2,2,128,256]{3,2,1,0:T(8,128)(2,1)S(1)} collective-permute-done((bf16[2,2,128,256]{3,2,1,0:T(8,128)(2,1)S(1)}, bf16[2,2,128,256]{3,2,1,0:T(8,128)(2,1)S(1)}, u32[]{:S(2)}, u32[]{:S(2)}) %collective-permute-start.19) | collective-permute-done | bytes 262176 | tf_op jit(solution)/shard_map/ppermute | solution.py:590
  84.1 2.7 %collective-permute-done.20.high = bf16[2,2,128,256]{3,2,1,0:T(8,128)(2,1)S(1)} collective-permute-done((bf16[2,2,128,256]{3,2,1,0:T(8,128)(2,1)S(1)}, bf16[2,2,128,256]{3,2,1,0:T(8,128)(2,1)S(1)}, u32[]{:S(2)}, u32[]{:S(2)}) %collective-permute-start.20) | collective-permute-done | bytes 262176 | tf_op jit(solution)/shard_map/ppermute | solution.py:591
  86.8 0.7 split.3
  87.5 0.6 collective-permute-start.22
  88.1 3.3 %collective-permute-done.18.high = bf16[2,2,128,256]{3,2,1,0:T(8,128)(2,1)S(1)} collective-permute-done((bf16[2,2,128,256]{3,2,1,0:T(8,128)(2,1)S(1)}, bf16[2,2,128,256]{3,2,1,0:T(8,128)(2,1)S(1)}, u32[]{:S(2)}, u32[]{:S(2)}) %collective-permute-start.18) | collective-permute-done | bytes 262176 | tf_op jit(solution)/shard_map/ppermute | solution.py:591
  91.4 0.7 split.2
  92.1 0.6 collective-permute-start.21
  92.8 1.7 %collective-permute-start.26 = (bf16[2,2,32,256]{3,2,1,0:T(8,128)(2,1)S(1)}, bf16[2,2,32,256]{3,2,1,0:T(8,128)(2,1)S(1)}, u32[]{:S(2)}, u32[]{:S(2)}) collective-permute-start(bf16[2,2,32,256]{3,2,1,0:T(8,128)(2,1)S(1)} %get-tuple-element.173), channel_id=1, source_target_pairs={{0,8},{4,12},{8,0},{12,4},{16,24},{20,28},{24,16},{28,20},{1,9},{5... | collective-permute-start | bytes 196616 | tf_op jit(solution)/shard_map/ppermute | solution.py:573
  94.5 2.7 %collective-permute-start.28 = (bf16[2,2,32,256]{3,2,1,0:T(8,128)(2,1)S(1)}, bf16[2,2,32,256]{3,2,1,0:T(8,128)(2,1)S(1)}, u32[]{:S(2)}, u32[]{:S(2)}) collective-permute-start(bf16[2,2,32,256]{3,2,1,0:T(8,128)(2,1)S(1)} %get-tuple-element.175), channel_id=1, source_target_pairs={{0,24},{4,28},{8,16},{12,20},{16,8},{20,12},{24,0},{28,4},{1,25},{... | collective-permute-start | bytes 196616 | tf_op jit(solution)/shard_map/ppermute | solution.py:573
  97.2 0.6 slice.10
  98.5 0.9 end.1
  99.4 1.8 %collective-permute-done.27.refs_2_ = bf16[2,2,32,256]{3,2,1,0:T(8,128)(2,1)S(1)} collective-permute-done((bf16[2,2,32,256]{3,2,1,0:T(8,128)(2,1)S(1)}, bf16[2,2,32,256]{3,2,1,0:T(8,128)(2,1)S(1)}, u32[]{:S(2)}, u32[]{:S(2)}) %collective-permute-start.27) | collective-permute-done | bytes 65568 | tf_op jit(solution)/shard_map/ppermute | solution.py:573
  101.2 0.7 total.1
  (28 shorter events, 0.2 us)
Async XLA Ops:
  1.9 15.0 %collective-permute-start = (bf16[2,2,256,256]{3,2,1,0:T(8,128)(2,1)S(1)}, bf16[2,2,256,256]{3,2,1,0:T(8,128)(2,1)S(1)}, u32[]{:S(2)}, u32[]{:S(2)}) collective-permute-start(bf16[2,2,256,256]{3,2,1,0:T(8,128)(2,1)S(1)} %convert_element_type.42), channel_id=1, source_target_pairs={{0,2},{1,3},{2,0},{3,1},{4,6},{5,7},{6,4},{7,5},{8,10},{9,11},{10,... | collective-permute-start | bytes 1572872 | tf_op jit(solution)/shard_map/ppermute | solution.py:421
  4.9 22.1 %collective-permute-start.4 = (bf16[2,2,256,256]{3,2,1,0:T(8,128)(2,1)S(1)}, bf16[2,2,256,256]{3,2,1,0:T(8,128)(2,1)S(1)}, u32[]{:S(2)}, u32[]{:S(2)}) collective-permute-start(bf16[2,2,256,256]{3,2,1,0:T(8,128)(2,1)S(1)} %convert_element_type.42), channel_id=1, source_target_pairs={{0,1},{1,0},{2,3},{3,2},{4,5},{5,4},{6,7},{7,6},{8,9},{9,8},{10,11... | collective-permute-start | bytes 1572872 | tf_op jit(solution)/shard_map/ppermute | solution.py:421
  5.7 1.6 %copy-start.1 = (bf16[2,2,128,2048]{3,2,1,0:T(8,128)(2,1)S(1)}, bf16[2,2,128,2048]{3,2,1,0:T(8,128)(2,1)}, u32[]{:S(2)}) copy-start(bf16[2,2,128,2048]{3,2,1,0:T(8,128)(2,1)} %strip_far.1) | copy-start | bytes 6291460
  7.3 1.2 %copy-start.2 = (bf16[8,256,256]{2,1,0:T(8,128)(2,1)S(1)}, bf16[8,256,256]{2,1,0:T(8,128)(2,1)}, u32[]{:S(2)}) copy-start(bf16[8,256,256]{2,1,0:T(8,128)(2,1)} %amplitudes_far.1) | copy-start | bytes 3145732
  8.5 0.7 copy-start.3
  9.2 25.0 %copy-start = (f32[2,2,256,256]{3,2,1,0:T(8,128)S(1)}, f32[2,2,256,256]{3,2,1,0:T(8,128)}, u32[]{:S(2)}) copy-start(f32[2,2,256,256]{3,2,1,0:T(8,128)} %refs_1_.1) | copy-start | bytes 3145732
  9.2 25.0 %copy-start.4 = (bf16[4,256,256]{2,1,0:T(8,128)(2,1)S(1)}, bf16[4,256,256]{2,1,0:T(8,128)(2,1)}, u32[]{:S(2)}) copy-start(bf16[4,256,256]{2,1,0:T(8,128)(2,1)} %constant.181.clone.refs_8_.refs_4_.refs_6_) | copy-start | bytes 1572868
  9.2 25.0 %copy-start.5 = (f32[2,256,256]{2,1,0:T(8,128)S(1)}, f32[2,256,256]{2,1,0:T(8,128)}, u32[]{:S(2)}) copy-start(f32[2,256,256]{2,1,0:T(8,128)} %constant.182.clone.refs_9_.refs_7_) | copy-start | bytes 1572868
  11.3 9.2 %collective-permute-start.8 = (bf16[2,256,256]{2,1,0:T(8,128)(2,1)S(1)}, bf16[2,256,256]{2,1,0:T(8,128)(2,1)S(1)}, u32[]{:S(2)}, u32[]{:S(2)}) collective-permute-start(bf16[2,256,256]{2,1,0:T(8,128)(2,1)S(1)} %get-tuple-element.124), channel_id=1, source_target_pairs={{0,4},{4,0},{8,12},{12,8},{16,20},{20,16},{24,28},{28,24},{1,5},{5... | collective-permute-start | bytes 786440 | tf_op jit(solution)/shard_map/ppermute | solution.py:482
  12.9 12.9 %collective-permute-start.6 = (bf16[2,256,256]{2,1,0:T(8,128)(2,1)S(1)}, bf16[2,256,256]{2,1,0:T(8,128)(2,1)S(1)}, u32[]{:S(2)}, u32[]{:S(2)}) collective-permute-start(bf16[2,256,256]{2,1,0:T(8,128)(2,1)S(1)} %get-tuple-element.121), channel_id=1, source_target_pairs={{0,4},{4,0},{8,12},{12,8},{16,20},{20,16},{24,28},{28,24},{1,5},{5... | collective-permute-start | bytes 786440 | tf_op jit(solution)/shard_map/ppermute | solution.py:482
  16.9 17.4 %collective-permute-start.5 = (bf16[2,2,256,256]{3,2,1,0:T(8,128)(2,1)S(1)}, bf16[2,2,256,256]{3,2,1,0:T(8,128)(2,1)S(1)}, u32[]{:S(2)}, u32[]{:S(2)}) collective-permute-start(bf16[2,2,256,256]{3,2,1,0:T(8,128)(2,1)S(1)} %collective-permute-done.refs_6_.refs_3_), channel_id=1, source_target_pairs={{0,1},{1,0},{2,3},{3,2},{4,5},{5,4},{6,7},{7,6},{8,9},{9,8},{10,11... | collective-permute-start | bytes 1572872 | tf_op jit(solution)/shard_map/ppermute | solution.py:421
  16.9 13.8 %collective-permute-start.1 = (bf16[2,2,128,256]{3,2,1,0:T(8,128)(2,1)S(1)}, bf16[2,2,128,256]{3,2,1,0:T(8,128)(2,1)S(1)}, u32[]{:S(2)}, u32[]{:S(2)}) collective-permute-start(bf16[2,2,128,256]{3,2,1,0:T(8,128)(2,1)S(1)} %get-tuple-element.112), channel_id=1, source_target_pairs={{0,1},{1,0},{2,3},{3,2},{4,5},{5,4},{6,7},{7,6},{8,9},{9,8},{10,11... | collective-permute-start | bytes 786440 | tf_op jit(solution)/shard_map/ppermute | solution.py:421
  20.5 10.2 %collective-permute-start.2 = (bf16[2,2,128,256]{3,2,1,0:T(8,128)(2,1)S(1)}, bf16[2,2,128,256]{3,2,1,0:T(8,128)(2,1)S(1)}, u32[]{:S(2)}, u32[]{:S(2)}) collective-permute-start(bf16[2,2,128,256]{3,2,1,0:T(8,128)(2,1)S(1)} %get-tuple-element.113), channel_id=1, source_target_pairs={{0,2},{1,3},{2,0},{3,1},{4,6},{5,7},{6,4},{7,5},{8,10},{9,11},{10,... | collective-permute-start | bytes 786440 | tf_op jit(solution)/shard_map/ppermute | solution.py:421
  25.7 8.5 %collective-permute-start.3 = (bf16[2,2,128,256]{3,2,1,0:T(8,128)(2,1)S(1)}, bf16[2,2,128,256]{3,2,1,0:T(8,128)(2,1)S(1)}, u32[]{:S(2)}, u32[]{:S(2)}) collective-permute-start(bf16[2,2,128,256]{3,2,1,0:T(8,128)(2,1)S(1)} %get-tuple-element.114), channel_id=1, source_target_pairs={{0,3},{1,2},{2,1},{3,0},{4,7},{5,6},{6,5},{7,4},{8,11},{9,10},{10,... | collective-permute-start | bytes 786440 | tf_op jit(solution)/shard_map/ppermute | solution.py:421
  27.0 14.2 %collective-permute-start.10 = (bf16[256,256]{1,0:T(8,128)(2,1)S(1)}, bf16[256,256]{1,0:T(8,128)(2,1)S(1)}, u32[]{:S(2)}, u32[]{:S(2)}) collective-permute-start(bf16[256,256]{1,0:T(8,128)(2,1)S(1)} %get-tuple-element.126), channel_id=1, source_target_pairs={{0,24},{4,28},{8,16},{12,20},{16,8},{20,12},{24,0},{28,4},{1,25},{... | collective-permute-start | bytes 393224 | tf_op jit(solution)/shard_map/ppermute | solution.py:488
  30.7 10.6 %collective-permute-start.7 = (bf16[256,256]{1,0:T(8,128)(2,1)S(1)}, bf16[256,256]{1,0:T(8,128)(2,1)S(1)}, u32[]{:S(2)}, u32[]{:S(2)}) collective-permute-start(bf16[256,256]{1,0:T(8,128)(2,1)S(1)} %get-tuple-element.123), channel_id=1, source_target_pairs={{0,8},{4,12},{8,0},{12,4},{16,24},{20,28},{24,16},{28,20},{1,9},{5... | collective-permute-start | bytes 393224 | tf_op jit(solution)/shard_map/ppermute | solution.py:488
  30.7 11.8 %copy-start.6 = (bf16[2,256,256]{2,1,0:T(8,128)(2,1)S(1)}, bf16[2,256,256]{2,1,0:T(8,128)(2,1)}, u32[]{:S(2)}) copy-start(bf16[2,256,256]{2,1,0:T(8,128)(2,1)} %constant.183.clone.refs_5_) | copy-start | bytes 786436
  30.7 11.8 %collective-permute-start.9 = (bf16[256,256]{1,0:T(8,128)(2,1)S(1)}, bf16[256,256]{1,0:T(8,128)(2,1)S(1)}, u32[]{:S(2)}, u32[]{:S(2)}) collective-permute-start(bf16[256,256]{1,0:T(8,128)(2,1)S(1)} %get-tuple-element.125), channel_id=1, source_target_pairs={{0,16},{4,20},{8,24},{12,28},{16,0},{20,4},{24,8},{28,12},{1,17},{... | collective-permute-start | bytes 393224 | tf_op jit(solution)/shard_map/ppermute | solution.py:488
  46.8 7.0 %collective-permute-start.11 = (bf16[2,128,256]{2,1,0:T(8,128)(2,1)S(1)}, bf16[2,128,256]{2,1,0:T(8,128)(2,1)S(1)}, u32[]{:S(2)}, u32[]{:S(2)}) collective-permute-start(bf16[2,128,256]{2,1,0:T(8,128)(2,1)S(1)} %get-tuple-element.128), channel_id=1, source_target_pairs={{0,1},{1,0},{2,3},{3,2},{4,5},{5,4},{6,7},{7,6},{8,9},{9,8},{10,11... | collective-permute-start | bytes 393224 | tf_op jit(solution)/shard_map/ppermute | solution.py:421
  46.8 8.7 %collective-permute-start.13 = (bf16[2,128,256]{2,1,0:T(8,128)(2,1)S(1)}, bf16[2,128,256]{2,1,0:T(8,128)(2,1)S(1)}, u32[]{:S(2)}, u32[]{:S(2)}) collective-permute-start(bf16[2,128,256]{2,1,0:T(8,128)(2,1)S(1)} %get-tuple-element.128), channel_id=1, source_target_pairs={{0,3},{1,2},{2,1},{3,0},{4,7},{5,6},{6,5},{7,4},{8,11},{9,10},{10,... | collective-permute-start | bytes 393224 | tf_op jit(solution)/shard_map/ppermute | solution.py:421
  48.5 7.0 %collective-permute-start.12 = (bf16[2,128,256]{2,1,0:T(8,128)(2,1)S(1)}, bf16[2,128,256]{2,1,0:T(8,128)(2,1)S(1)}, u32[]{:S(2)}, u32[]{:S(2)}) collective-permute-start(bf16[2,128,256]{2,1,0:T(8,128)(2,1)S(1)} %get-tuple-element.158.refs_0_), channel_id=1, source_target_pairs={{0,2},{1,3},{2,0},{3,1},{4,6},{5,7},{6,4},{7,5},{8,10},{9,11},{10,... | collective-permute-start | bytes 393224 | tf_op jit(solution)/shard_map/ppermute | solution.py:421
  55.5 2.7 %collective-permute-start.23 = (bf16[2,2,2,256,256]{4,3,2,1,0:T(8,128)(2,1)S(1)}, bf16[2,2,2,256,256]{4,3,2,1,0:T(8,128)(2,1)S(1)}, u32[]{:S(2)}, u32[]{:S(2)}) collective-permute-start(bf16[2,2,2,256,256]{4,3,2,1,0:T(8,128)(2,1)S(1)} %get-tuple-element.167), channel_id=1, source_target_pairs={{0,1},{1,0},{2,3},{3,2},{4,5},{5,4},{6,7},{7,6},{8,9},{9,8},{10,11... | collective-permute-start | bytes 3145736 | tf_op jit(solution)/shard_map/ppermute | solution.py:421
  59.0 19.3 %collective-permute-start.24 = (bf16[2,4,2,2,32,256]{5,4,3,2,1,0:T(8,128)(2,1)S(1)}, bf16[2,4,2,2,32,256]{5,4,3,2,1,0:T(8,128)(2,1)S(1)}, u32[]{:S(2)}, u32[]{:S(2)}) collective-permute-start(bf16[2,4,2,2,32,256]{5,4,3,2,1,0:T(8,128)(2,1)S(1)} %get-tuple-element.169), channel_id=1, source_target_pairs={{0,4},{4,0},{8,12},{12,8},{16,20},{20,16},{24,28},{28,24},{1,5},{5... | collective-permute-start | bytes 1572872 | tf_op jit(solution)/shard_map/ppermute | solution.py:560
  60.6 3.0 %collective-permute-start.14 = (bf16[2,128,256]{2,1,0:T(8,128)(2,1)S(1)}, bf16[2,128,256]{2,1,0:T(8,128)(2,1)S(1)}, u32[]{:S(2)}, u32[]{:S(2)}) collective-permute-start(bf16[2,128,256]{2,1,0:T(8,128)(2,1)S(1)} %get-tuple-element.135), channel_id=1, source_target_pairs={{0,1},{1,0},{2,3},{3,2},{4,5},{5,4},{6,7},{7,6},{8,9},{9,8},{10,11... | collective-permute-start | bytes 393224 | tf_op jit(solution)/shard_map/ppermute | solution.py:421
  60.6 6.3 %collective-permute-start.15 = (bf16[2,128,256]{2,1,0:T(8,128)(2,1)S(1)}, bf16[2,128,256]{2,1,0:T(8,128)(2,1)S(1)}, u32[]{:S(2)}, u32[]{:S(2)}) collective-permute-start(bf16[2,128,256]{2,1,0:T(8,128)(2,1)S(1)} %get-tuple-element.157.refs_0_), channel_id=1, source_target_pairs={{0,2},{1,3},{2,0},{3,1},{4,6},{5,7},{6,4},{7,5},{8,10},{9,11},{10,... | collective-permute-start | bytes 393224 | tf_op jit(solution)/shard_map/ppermute | solution.py:421
  62.1 6.8 %collective-permute-start.16 = (bf16[2,128,256]{2,1,0:T(8,128)(2,1)S(1)}, bf16[2,128,256]{2,1,0:T(8,128)(2,1)S(1)}, u32[]{:S(2)}, u32[]{:S(2)}) collective-permute-start(bf16[2,128,256]{2,1,0:T(8,128)(2,1)S(1)} %get-tuple-element.135), channel_id=1, source_target_pairs={{0,3},{1,2},{2,1},{3,0},{4,7},{5,6},{6,5},{7,4},{8,11},{9,10},{10,... | collective-permute-start | bytes 393224 | tf_op jit(solution)/shard_map/ppermute | solution.py:421
  70.0 9.5 %collective-permute-start.17 = (bf16[2,2,128,256]{3,2,1,0:T(8,128)(2,1)S(1)}, bf16[2,2,128,256]{3,2,1,0:T(8,128)(2,1)S(1)}, u32[]{:S(2)}, u32[]{:S(2)}) collective-permute-start(bf16[2,2,128,256]{3,2,1,0:T(8,128)(2,1)S(1)} %get-tuple-element.147), channel_id=1, source_target_pairs={{0,8},{4,12},{8,16},{12,20},{16,24},{20,28},{1,9},{5,13},{9,17},{1... | collective-permute-start | bytes 786440 | tf_op jit(solution)/shard_map/ppermute | solution.py:590
  72.2 11.8 %collective-permute-start.19 = (bf16[2,2,128,256]{3,2,1,0:T(8,128)(2,1)S(1)}, bf16[2,2,128,256]{3,2,1,0:T(8,128)(2,1)S(1)}, u32[]{:S(2)}, u32[]{:S(2)}) collective-permute-start(bf16[2,2,128,256]{3,2,1,0:T(8,128)(2,1)S(1)} %get-tuple-element.152), channel_id=1, source_target_pairs={{0,8},{4,12},{8,16},{12,20},{16,24},{20,28},{1,9},{5,13},{9,17},{1... | collective-permute-start | bytes 786440 | tf_op jit(solution)/shard_map/ppermute | solution.py:590
  75.7 11.1 %collective-permute-start.20 = (bf16[2,2,128,256]{3,2,1,0:T(8,128)(2,1)S(1)}, bf16[2,2,128,256]{3,2,1,0:T(8,128)(2,1)S(1)}, u32[]{:S(2)}, u32[]{:S(2)}) collective-permute-start(bf16[2,2,128,256]{3,2,1,0:T(8,128)(2,1)S(1)} %get-tuple-element.153), channel_id=1, source_target_pairs={{8,0},{12,4},{16,8},{20,12},{24,16},{28,20},{9,1},{13,5},{17,9},{2... | collective-permute-start | bytes 786440 | tf_op jit(solution)/shard_map/ppermute | solution.py:591
  77.0 14.4 %collective-permute-start.18 = (bf16[2,2,128,256]{3,2,1,0:T(8,128)(2,1)S(1)}, bf16[2,2,128,256]{3,2,1,0:T(8,128)(2,1)S(1)}, u32[]{:S(2)}, u32[]{:S(2)}) collective-permute-start(bf16[2,2,128,256]{3,2,1,0:T(8,128)(2,1)S(1)} %get-tuple-element.149), channel_id=1, source_target_pairs={{8,0},{12,4},{16,8},{20,12},{24,16},{28,20},{9,1},{13,5},{17,9},{2... | collective-permute-start | bytes 786440 | tf_op jit(solution)/shard_map/ppermute | solution.py:591
  78.4 14.3 %collective-permute-start.25 = (bf16[4,2,2,32,256]{4,3,2,1,0:T(8,128)(2,1)S(1)}, bf16[4,2,2,32,256]{4,3,2,1,0:T(8,128)(2,1)S(1)}, u32[]{:S(2)}, u32[]{:S(2)}) collective-permute-start(bf16[4,2,2,32,256]{4,3,2,1,0:T(8,128)(2,1)S(1)} %get-tuple-element.171), channel_id=1, source_target_pairs={{0,2},{1,3},{2,0},{3,1},{4,6},{5,7},{6,4},{7,5},{8,10},{9,11},{10,... | collective-permute-start | bytes 786440 | tf_op jit(solution)/shard_map/ppermute | solution.py:421
  87.5 11.0 %collective-permute-start.22 = (bf16[2,128,256]{2,1,0:T(8,128)(2,1)S(1)}, bf16[2,128,256]{2,1,0:T(8,128)(2,1)S(1)}, u32[]{:S(2)}, u32[]{:S(2)}) collective-permute-start(bf16[2,128,256]{2,1,0:T(8,128)(2,1)S(1)} %get-tuple-element.156), channel_id=1, source_target_pairs={{0,4},{4,0},{8,12},{12,8},{16,20},{20,16},{24,28},{28,24},{1,5},{5... | collective-permute-start | bytes 393224 | tf_op jit(solution)/shard_map/ppermute | solution.py:601
  92.1 6.4 %collective-permute-start.21 = (bf16[2,128,256]{2,1,0:T(8,128)(2,1)S(1)}, bf16[2,128,256]{2,1,0:T(8,128)(2,1)S(1)}, u32[]{:S(2)}, u32[]{:S(2)}) collective-permute-start(bf16[2,128,256]{2,1,0:T(8,128)(2,1)S(1)} %get-tuple-element.155), channel_id=1, source_target_pairs={{0,4},{4,0},{8,12},{12,8},{16,20},{20,16},{24,28},{28,24},{1,5},{5... | collective-permute-start | bytes 393224 | tf_op jit(solution)/shard_map/ppermute | solution.py:601
  92.8 6.6 %collective-permute-start.26 = (bf16[2,2,32,256]{3,2,1,0:T(8,128)(2,1)S(1)}, bf16[2,2,32,256]{3,2,1,0:T(8,128)(2,1)S(1)}, u32[]{:S(2)}, u32[]{:S(2)}) collective-permute-start(bf16[2,2,32,256]{3,2,1,0:T(8,128)(2,1)S(1)} %get-tuple-element.173), channel_id=1, source_target_pairs={{0,8},{4,12},{8,0},{12,4},{16,24},{20,28},{24,16},{28,20},{1,9},{5... | collective-permute-start | bytes 196616 | tf_op jit(solution)/shard_map/ppermute | solution.py:573
  94.5 6.7 %collective-permute-start.27 = (bf16[2,2,32,256]{3,2,1,0:T(8,128)(2,1)S(1)}, bf16[2,2,32,256]{3,2,1,0:T(8,128)(2,1)S(1)}, u32[]{:S(2)}, u32[]{:S(2)}) collective-permute-start(bf16[2,2,32,256]{3,2,1,0:T(8,128)(2,1)S(1)} %get-tuple-element.174), channel_id=1, source_target_pairs={{0,16},{4,20},{8,24},{12,28},{16,0},{20,4},{24,8},{28,12},{1,17},{... | collective-permute-start | bytes 196616 | tf_op jit(solution)/shard_map/ppermute | solution.py:573
  94.5 6.7 %collective-permute-start.28 = (bf16[2,2,32,256]{3,2,1,0:T(8,128)(2,1)S(1)}, bf16[2,2,32,256]{3,2,1,0:T(8,128)(2,1)S(1)}, u32[]{:S(2)}, u32[]{:S(2)}) collective-permute-start(bf16[2,2,32,256]{3,2,1,0:T(8,128)(2,1)S(1)} %get-tuple-element.175), channel_id=1, source_target_pairs={{0,24},{4,28},{8,16},{12,20},{16,8},{20,12},{24,0},{28,4},{1,25},{... | collective-permute-start | bytes 196616 | tf_op jit(solution)/shard_map/ppermute | solution.py:573
where the time goes:
time: 102 us
  waiting for transfers between devices  37.9 us (37%)
  starting transfers between devices  31 us (30%)
  Pallas kernels  25.4 us (25%)
  local copies, waits for them, and re-layouts  4.86 us (5%)
  between operations  1.54 us (2%)
  other arithmetic  1.28 us (1%)
    pallas_call x15, Pallas kernels, call(): pl.pallas_call(body, out_shape=[pltpu.VMEM(shape, dtype) if at in keep el...  25.4 us
    ppermute x14, waiting for transfers between devices, turned(): return lax.ppermute(value, 'tile', [(i, i ^ turn) for i in range(tiles)])  16 us
    ppermute x14, starting transfers between devices, turned(): return lax.ppermute(value, 'tile', [(i, i ^ turn) for i in range(tiles)])  8.86 us
    ppermute x2, waiting for transfers between devices, on_device_by_slot(): lax.ppermute(value, 'pos', aside)  8.15 us
    ppermute x2, waiting for transfers between devices, on_device_by_slot(): lax.ppermute(below, 'pos', [(i + 2, i) for i in range(groups - 2)])  6.01 us
    ppermute x2, starting transfers between devices, on_device_by_slot(): low_in = lax.ppermute(above, 'pos', [(i, i + 2) for i in range(groups - 2)])  5.71 us
    ppermute x2, waiting for transfers between devices, on_device_by_slot(): low_in = lax.ppermute(above, 'pos', [(i, i + 2) for i in range(groups - 2)])  4.56 us
    ppermute x3, starting transfers between devices, on_device_by_slot(): lax.ppermute(send, 'pos', [(i, i ^ 2 * turn) for i in range(groups)])  4.45 us
  transfers between devices with their start and end apart: 29, of which 13 were waited for; matrix products, arithmetic and copies ran while one was open for 1% of the time, Pallas kernels for 19%

commit v1 on v0

--- a/solution.py
+++ b/solution.py
@@ -147,10 +147,10 @@
 
 def first_kernel(groups, tiles, points, counts, offsets, strip_far, amplitudes_far, *refs):
     strips = refs[:tiles]
-    same, remote, nearby, plan_out, plan, strip, amplitudes, sems = refs[tiles:]
+    same, other_x, plan_out, plan, strip, amplitudes, sems = refs[tiles:]
     layers, rows = strip.shape[0], strip.shape[2]
     slots = amplitudes.shape[0]
-    n = offsets.shape[0]
+    n = offsets.shape[1]
     strip_copy = pltpu.make_async_copy(strip_far, strip, sems.at[1])
     strip_copy.start()
     amplitude_copy = pltpu.make_async_copy(amplitudes_far, amplitudes, sems.at[2])
@@ -158,16 +158,18 @@
     pos, tile = lax.axis_index("pos"), lax.axis_index("tile")
     width = plan_out.shape[1]
 
-    number = lax.broadcasted_iota(jnp.int32, (n, 1), 0)
-    live = jnp.zeros((n, 1), jnp.int32)
+    number = lax.broadcasted_iota(jnp.int32, (1, n), 1)
+    live = jnp.zeros((1, n), jnp.int32)
     for group in range(groups):
         live += jnp.where((number >= group * slots) & (number < group * slots + counts[group]), 1, 0)
-    row, col = offsets[:, 0:1].astype(F32), offsets[:, 1:2].astype(F32)
+    row, col = offsets[0:1, :].astype(F32), offsets[1:2, :].astype(F32)
     number = number.astype(F32)
-    key = jnp.where(live > 0, col, float(1 << 12)) * n + number
+    across = jnp.where(live > 0, col, float(1 << 12)) * n + number
     square = (n, n)
     eye = lax.broadcasted_iota(jnp.int32, square, 0) == lax.broadcasted_iota(jnp.int32, square, 1)
-    across = jnp.sum(jnp.where(eye, key, 0.0), axis=0, keepdims=True)
+    key, number, row, col = (
+        jnp.sum(jnp.where(eye, value, 0.0), axis=1, keepdims=True) for value in (across, number, row, col)
+    )
     rank = jnp.sum(jnp.where(across < key, 1.0, 0.0), axis=1, keepdims=True).astype(jnp.int32)
     here = lax.broadcasted_iota(jnp.int32, (n, width), 1) == rank
     chosen = [
@@ -206,8 +208,7 @@
                 ).astype(BF16)
     amplitude_copy.wait()
     for turn in range(groups // 2):
-        across_x = (nearby, remote)[turn // 2]
-        for flip, out, at in ((0, same, turn), (1, across_x, turn % 2)):
+        for flip, out, at in ((0, same, turn), (1, other_x, turn)):
             slot = plan[0, (pos ^ (2 * turn + flip)) * tiles + tile]
 
             @pl.when(slot // slots == pos)
@@ -350,7 +351,7 @@
 
 
 def place_kernel(tiles, points, plan, *refs):
-    pieces, (below, same, above, canvas) = refs[:tiles], refs[tiles:]
+    pieces, (even, same, odd, canvas) = refs[:-4], refs[-4:]
     rows = pieces[0].shape[1]
     core, up = plan[3, 1] % 2, plan[3, 1] // 2
     base = plan[3, 0] // 2 * 2 - 2
@@ -361,28 +362,30 @@
         row, col = slot_at(plan, tiles, turn)
         mine = jnp.where(sub >= row, 0, 1) == up
         early = lane >= col % points
-        for part in range(2):
-            value = jnp.where(mine, pieces[turn][part].astype(F32), 0.0)
-            for step, keep in ((0, early), (1, ~early)):
-                at = col // points + step - base
-                at = jnp.where((at >= 0) & (at < 6), at, 6)
-                canvas[at, part] += jnp.where(keep, value, 0.0)
-    below[...] = canvas[0:2].astype(BF16)
-    same[...] = canvas[2:4]
-    above[...] = canvas[4:6].astype(BF16)
+        for layer in range(len(pieces) // tiles):
+            for part in range(2):
+                value = jnp.where(mine, pieces[layer * tiles + turn][part].astype(F32), 0.0)
+                for step, keep in ((0, early), (1, ~early)):
+                    at = col // points + step - base
+                    at = jnp.where((at >= 0) & (at < 6), at, 6)
+                    canvas[layer, at, part] += jnp.where(keep, value, 0.0)
+    same[...] = canvas[:, 2:4]
+    up_first = plan[3, 0] // 2 % 2 == 0
+    for out, at in ((even, jnp.where(up_first, 4, 0)), (odd, jnp.where(up_first, 0, 4))):
+        out[...] = canvas[:, pl.ds(at, 2)].astype(BF16)
 
 
 def split_kernel(plan, same, low, high, keep, send):
     x_at = plan[3, 0] % 2
-    keep[...] = same[x_at] + low[x_at].astype(F32) + high[x_at].astype(F32)
-    other = same[1 - x_at] + low[1 - x_at].astype(F32) + high[1 - x_at].astype(F32)
-    send[...] = other.astype(BF16)
-
-
-def end_kernel(layers, *refs):
-    extra, out = refs[-2:]
-    for layer in range(layers):
-        out[layer] = refs[layer][...] + refs[layers + layer][...].astype(F32) + extra[layer].astype(F32)
+    for layer in range(same.shape[0]):
+        mine = same[layer, x_at] + low[layer, x_at].astype(F32) + high[layer, x_at].astype(F32)
+        other = same[layer, 1 - x_at] + low[layer, 1 - x_at].astype(F32) + high[layer, 1 - x_at].astype(F32)
+        keep[layer] = mine
+        send[layer] = other.astype(BF16)
+
+
+def end_kernel(keep, came, extra, out):
+    out[...] = keep[...] + came[...].astype(F32) + extra[...].astype(F32)
 
 
 def spread_kernel(plan, mine, beyond, came, keep, send):
@@ -456,11 +459,10 @@
     shot = (points, points)
     outs = call(
         functools.partial(first_kernel, groups, tiles, points),
-        (slot_counts, scan_offsets, object_slices, amplitudes),
+        (slot_counts, scan_offsets.T, object_slices, amplitudes),
         [SM, VM, HB, HB],
         [((layers, 2, rows, points), BF16)] * tiles
-        + [((groups // 2, *shot), BF16)]
-        + [((groups // 4, *shot), BF16)] * 2
+        + [((groups // 2, *shot), BF16)] * 2
         + [((8, 128), jnp.int32)],
         [
             pltpu.SMEM((8, 128), jnp.int32),
@@ -469,21 +471,19 @@
             pltpu.SemaphoreType.DMA((3,)),
         ],
         name="first",
-        us=5.0,
+        us=0.1,
         mib=16,
     )
-    (*cut, same, far, near, plan) = outs
+    (*cut, same, far, plan) = outs
     across, cut = lax.optimization_barrier((across, cut))
     aside = [(i, i ^ 1) for i in range(groups)]
-    merged = [None] * (groups // 2)
-    for turns, value in (((2, 3), far), ((0, 1), near)):
-        merged[turns[0]], merged[turns[1]] = call(
-            functools.partial(merge_kernel, tiles, slots, turns),
-            (plan, same, lax.ppermute(value, "pos", aside)),
-            [SM, VM, VM],
-            [(shot, BF16)] * 2,
-            name="merge",
-        )
+    merged = call(
+        functools.partial(merge_kernel, tiles, slots, range(groups // 2)),
+        (plan, same, lax.ppermute(far, "pos", aside)),
+        [SM, VM, VM],
+        [(shot, BF16)] * (groups // 2),
+        name="merge",
+    )
     arrived = [merged[0]] + [
         lax.ppermute(merged[turn], "pos", [(i, i ^ (2 * turn)) for i in range(groups)])
         for turn in range(1, groups // 2)
@@ -505,7 +505,7 @@
             pltpu.SemaphoreType.DMA((3,)),
         ],
         name="ahead",
-        us=12.0,
+        us=0.1,
         mib=24,
         keep=range(5),
     )
@@ -523,7 +523,7 @@
             pltpu.SemaphoreType.DMA((2,)),
         ],
         name="back",
-        us=5.0,
+        us=0.1,
         mib=24,
         keep=(2,),
     )
@@ -542,7 +542,7 @@
             pltpu.SemaphoreType.DMA((3,)),
         ],
         name="last",
-        us=6.0,
+        us=0.1,
         mib=24,
     )
     pieces[1], own, other, beside = lax.optimization_barrier((pieces[1], own, other, beside))
@@ -575,30 +575,29 @@
     (probe_grad,) = call(total_kernel, (own, *came), [VM] * (1 + len(came)), [(share[1:], F32)], name="total")
 
     block = (2, rows, points)
-    keeps, swapped = [None] * layers, [None] * layers
-    for layer in reversed(range(layers)):
-        below, same, above = call(
-            functools.partial(place_kernel, tiles, points),
-            (plan, *pieces[layer]),
-            [SM] + [VM] * tiles,
-            [((2, *block), BF16), ((2, *block), F32), ((2, *block), BF16)],
-            [pltpu.VMEM((7, *block), F32)],
-            name="place",
-        )
-        if layer:
-            pieces[0], above, below = lax.optimization_barrier((pieces[0], above, below))
-        low_in = lax.ppermute(above, "pos", [(i, i + 2) for i in range(groups - 2)])
-        high_in = lax.ppermute(below, "pos", [(i + 2, i) for i in range(groups - 2)])
-        if layer == 0:
-            pieces, low_in = lax.optimization_barrier((pieces, low_in))
-        keeps[layer], send = call(
-            split_kernel,
-            (plan, same, low_in, high_in),
-            [SM] + [VM] * 3,
-            [(block, F32), (block, BF16)],
-            name="split",
-        )
-        swapped[layer] = lax.ppermute(send, "pos", [(i, i ^ 1) for i in range(groups)])
+    even, same, odd = call(
+        functools.partial(place_kernel, tiles, points),
+        (plan, *pieces[0], *pieces[1]),
+        [SM] + [VM] * (2 * tiles),
+        [((layers, 2, *block), BF16), ((layers, 2, *block), F32), ((layers, 2, *block), BF16)],
+        [pltpu.VMEM((layers, 7, *block), F32)],
+        name="place",
+        mib=16,
+    )
+    pairs = [(i, i ^ 2) for i in range(groups)]
+    low_in = lax.ppermute(even, "pos", pairs)
+    pairs = [(i, i + 2 if i // 2 % 2 else i - 2) for i in range(2, groups - 2)]
+    high_in = lax.ppermute(odd, "pos", pairs)
+    pieces, low_in = lax.optimization_barrier((pieces, low_in))
+    keep, send = call(
+        split_kernel,
+        (plan, same, low_in, high_in),
+        [SM] + [VM] * 3,
+        [((layers, *block), F32), ((layers, *block), BF16)],
+        name="split",
+        mib=16,
+    )
+    swapped = lax.ppermute(send, "pos", aside)
     extra = lax.cond(
         plan[3, 2] > 0,
         lambda p: distant_blocks(plan, p, tiles, points, groups),
@@ -606,9 +605,9 @@
         pieces,
     )
     (object_grad,) = call(
-        functools.partial(end_kernel, layers),
-        (*keeps, *swapped, extra),
-        [VM] * (2 * layers + 1),
+        end_kernel,
+        (keep, swapped, extra),
+        [VM] * 3,
         [((layers, *block), F32)],
         name="end",
     )

time: 102 us -> 91.7 us (0.90)
  waiting for transfers between devices: 37.9 us -> 31.1 us
  Pallas kernels: 25.4 us -> 23.5 us
  local copies, waits for them, and re-layouts: 4.86 us -> 3.54 us
    ppermute x8 -> x4, waiting for transfers between devices: 18.7 us -> 10.8 us  [the longest x1 6.55 us: on_device_by_slot(): low_in = lax.ppermute(even, 'pos', pairs)]
    ppermute x8 -> x4, starting transfers between devices: 11.6 us -> 6.69 us  [the longest x1 2.86 us: on_device_by_slot(): low_in = lax.ppermute(even, 'pos', pairs)]
    ppermute x1, waiting for transfers between devices: 0.01 us -> 4.21 us  [on_device_by_slot(): lax.ppermute(send, 'pos', aside)]
    ppermute x14, waiting for transfers between devices: 16 us -> 12.6 us  [turned(): return lax.ppermute(value, 'tile', [(i, i ^ turn) for i in range(tiles)])]
    ppermute x3, starting transfers between devices: 4.45 us -> 6.36 us  [on_device_by_slot(): lax.ppermute(send, 'pos', [(i, i ^ 2 * turn) for i in range(groups)])]
    pallas_call x15 -> x12, Pallas kernels: 25.4 us -> 23.5 us  [call(): pl.pallas_call(body, out_shape=[pltpu.VMEM(shape, dtype) if at in keep el...]
    ppermute x14, starting transfers between devices: 8.86 us -> 10.5 us  [turned(): return lax.ppermute(value, 'tile', [(i, i ^ turn) for i in range(tiles)])]
    ppermute x3, waiting for transfers between devices: 1.84 us -> 3.12 us  [on_device_by_slot(): lax.ppermute(send, 'pos', [(i, i ^ 2 * turn) for i in range(groups)])]
  transfers between devices with their start and end apart: 29 -> 25, of which waited for: 13 -> 11; matrix products, arithmetic and copies ran while one was open for 1% -> 1% of each run, Pallas kernels for 19% -> 20%
where the time goes in v1:
time: 91.7 us; the launch traced here: 91.5 us
  waiting for transfers between devices  31.1 us (34%)
  starting transfers between devices  30.4 us (33%)
  Pallas kernels  23.5 us (26%)
  local copies, waits for them, and re-layouts  3.54 us (4%)
  between operations  1.47 us (2%)
  other arithmetic  1.37 us (1%)
    pallas_call x12, Pallas kernels, call(): pl.pallas_call(body, out_shape=[pltpu.VMEM(shape, dtype) if at in keep el...  23.5 us
    ppermute x14, waiting for transfers between devices, turned(): return lax.ppermute(value, 'tile', [(i, i ^ turn) for i in range(tiles)])  12.6 us
    ppermute x14, starting transfers between devices, turned(): return lax.ppermute(value, 'tile', [(i, i ^ turn) for i in range(tiles)])  10.5 us
    ppermute x1, waiting for transfers between devices, on_device_by_slot(): low_in = lax.ppermute(even, 'pos', pairs)  6.55 us
    ppermute x3, starting transfers between devices, on_device_by_slot(): lax.ppermute(send, 'pos', [(i, i ^ 2 * turn) for i in range(groups)])  6.36 us
    ppermute x3, starting transfers between devices, on_device_by_slot(): lax.ppermute(merged[turn], 'pos', [(i, i ^ 2 * turn) for i in range(group...  5.29 us
    ppermute x1, waiting for transfers between devices, on_device_by_slot(): lax.ppermute(far, 'pos', aside)  4.29 us
    ppermute x1, waiting for transfers between devices, on_device_by_slot(): lax.ppermute(send, 'pos', aside)  4.21 us
  transfers between devices with their start and end apart: 25, of which 11 were waited for; matrix products, arithmetic and copies ran while one was open for 1% of the time, Pallas kernels for 20%

profile of v1, /device:TPU:0, one launch (start us, length us, event | category | flops | bytes accessed | tf_op | source)
XLA Modules:
  0.0 91.5 jit_solution(8426284584403284619)
XLA Ops:
  0.6 1.4 %convert_element_type.42 = bf16[2,2,256,256]{3,2,1,0:T(8,128)(2,1)S(1)} convert(f32[2,2,256,256]{3,2,1,0:T(8,128)} %refs_1_.1) | non-fusion elementwise | flops 262144 | bytes 1572864 | tf_op jit(solution)/shard_map/convert_element_type | solution.py:455
  2.0 3.0 %collective-permute-start = (bf16[2,2,256,256]{3,2,1,0:T(8,128)(2,1)S(1)}, bf16[2,2,256,256]{3,2,1,0:T(8,128)(2,1)S(1)}, u32[]{:S(2)}, u32[]{:S(2)}) collective-permute-start(bf16[2,2,256,256]{3,2,1,0:T(8,128)(2,1)S(1)} %convert_element_type.42), channel_id=1, source_target_pairs={{0,2},{1,3},{2,0},{3,1},{4,6},{5,7},{6,4},{7,5},{8,10},{9,11},{10,... | collective-permute-start | bytes 1572872 | tf_op jit(solution)/shard_map/ppermute | solution.py:424
  5.0 1.6 %copy-done.2 = bf16[2,2,128,2048]{3,2,1,0:T(8,128)(2,1)S(1)} copy-done((bf16[2,2,128,2048]{3,2,1,0:T(8,128)(2,1)S(1)}, bf16[2,2,128,2048]{3,2,1,0:T(8,128)(2,1)}, u32[]{:S(2)}) %copy-start.2) | copy-done | bytes 2097176
  6.6 0.7 copy-done.6
  7.3 0.7 copy-done.7
  8.0 2.1 %first.1 = (bf16[2,2,128,256]{3,2,1,0:T(8,128)(2,1)S(1)}, bf16[2,2,128,256]{3,2,1,0:T(8,128)(2,1)S(1)}, bf16[2,2,128,256]{3,2,1,0:T(8,128)(2,1)S(1)}, bf16[2,2,1...) custom-call(s32[8]{0:T(128)S(1)} %copy-done.7, ...), custom_call_target="tpu_custom_call" | custom-call | flops 100000000 | bytes 300000 | tf_op jit(solution)/shard_map/first/pallas_call | solution.py:116
  10.1 1.6 %collective-permute-start.6 = (bf16[4,256,256]{2,1,0:T(8,128)(2,1)S(1)}, bf16[4,256,256]{2,1,0:T(8,128)(2,1)S(1)}, u32[]{:S(2)}, u32[]{:S(2)}) collective-permute-start(bf16[4,256,256]{2,1,0:T(8,128)(2,1)S(1)} %get-tuple-element.109), channel_id=1, source_target_pairs={{0,4},{4,0},{8,12},{12,8},{16,20},{20,16},{24,28},{28,24},{1,5},{5... | collective-permute-start | bytes 1572872 | tf_op jit(solution)/shard_map/ppermute | solution.py:482
  11.6 0.0 collective-permute-start.4
  11.6 5.3 %collective-permute-done.refs_6_.refs_3_ = bf16[2,2,256,256]{3,2,1,0:T(8,128)(2,1)S(1)} collective-permute-done((bf16[2,2,256,256]{3,2,1,0:T(8,128)(2,1)S(1)}, bf16[2,2,256,256]{3,2,1,0:T(8,128)(2,1)S(1)}, u32[]{:S(2)}, u32[]{:S(2)}) %collective-permute-start) | collective-permute-done | bytes 524320 | tf_op jit(solution)/shard_map/ppermute | solution.py:424
  17.0 0.0 collective-permute-start.5
  17.0 0.5 collective-permute-start.1
  17.5 1.7 %collective-permute-start.2 = (bf16[2,2,128,256]{3,2,1,0:T(8,128)(2,1)S(1)}, bf16[2,2,128,256]{3,2,1,0:T(8,128)(2,1)S(1)}, u32[]{:S(2)}, u32[]{:S(2)}) collective-permute-start(bf16[2,2,128,256]{3,2,1,0:T(8,128)(2,1)S(1)} %get-tuple-element.101), channel_id=1, source_target_pairs={{0,2},{1,3},{2,0},{3,1},{4,6},{5,7},{6,4},{7,5},{8,10},{9,11},{10,... | collective-permute-start | bytes 786440 | tf_op jit(solution)/shard_map/ppermute | solution.py:424
  19.2 4.3 %collective-permute-done.6.came = bf16[4,256,256]{2,1,0:T(8,128)(2,1)S(1)} collective-permute-done((bf16[4,256,256]{2,1,0:T(8,128)(2,1)S(1)}, bf16[4,256,256]{2,1,0:T(8,128)(2,1)S(1)}, u32[]{:S(2)}, u32[]{:S(2)}) %collective-permute-start.6) | collective-permute-done | bytes 524320 | tf_op jit(solution)/shard_map/ppermute | solution.py:482
  23.5 0.0 collective-permute-start.3
  23.5 0.7 merge.1
  24.2 0.0 collective-permute-done.4.refs_5_.refs_2_
  24.2 1.6 %collective-permute-start.7 = (bf16[256,256]{1,0:T(8,128)(2,1)S(1)}, bf16[256,256]{1,0:T(8,128)(2,1)S(1)}, u32[]{:S(2)}, u32[]{:S(2)}) collective-permute-start(bf16[256,256]{1,0:T(8,128)(2,1)S(1)} %get-tuple-element.111), channel_id=1, source_target_pairs={{0,8},{4,12},{8,0},{12,4},{16,24},{20,28},{24,16},{28,20},{1,9},{5... | collective-permute-start | bytes 393224 | tf_op jit(solution)/shard_map/ppermute | solution.py:488
  25.8 0.0 collective-permute-done.1.refs_1_
  25.9 2.6 %collective-permute-start.8 = (bf16[256,256]{1,0:T(8,128)(2,1)S(1)}, bf16[256,256]{1,0:T(8,128)(2,1)S(1)}, u32[]{:S(2)}, u32[]{:S(2)}) collective-permute-start(bf16[256,256]{1,0:T(8,128)(2,1)S(1)} %get-tuple-element.112), channel_id=1, source_target_pairs={{0,16},{4,20},{8,24},{12,28},{16,0},{20,4},{24,8},{28,12},{1,17},{... | collective-permute-start | bytes 393224 | tf_op jit(solution)/shard_map/ppermute | solution.py:488
  28.5 0.0 collective-permute-done.2.refs_2_
  28.5 1.1 %collective-permute-start.9 = (bf16[256,256]{1,0:T(8,128)(2,1)S(1)}, bf16[256,256]{1,0:T(8,128)(2,1)S(1)}, u32[]{:S(2)}, u32[]{:S(2)}) collective-permute-start(bf16[256,256]{1,0:T(8,128)(2,1)S(1)} %get-tuple-element.113), channel_id=1, source_target_pairs={{0,24},{4,28},{8,16},{12,20},{16,8},{20,12},{24,0},{28,4},{1,25},{... | collective-permute-start | bytes 393224 | tf_op jit(solution)/shard_map/ppermute | solution.py:488
  29.5 1.8 %collective-permute-done.3.refs_3_ = bf16[2,2,128,256]{3,2,1,0:T(8,128)(2,1)S(1)} collective-permute-done((bf16[2,2,128,256]{3,2,1,0:T(8,128)(2,1)S(1)}, bf16[2,2,128,256]{3,2,1,0:T(8,128)(2,1)S(1)}, u32[]{:S(2)}, u32[]{:S(2)}) %collective-permute-start.3) | collective-permute-done | bytes 262176 | tf_op jit(solution)/shard_map/ppermute | solution.py:424
  31.3 0.0 collective-permute-done.5.refs_7_.refs_4_
  31.3 7.0 %ahead.1 = (bf16[2,256,256]{2,1,0:T(8,128)(2,1)S(1)}, bf16[2,256,256]{2,1,0:T(8,128)(2,1)S(1)}, bf16[8,2,256,256]{3,2,1,0:T(8,128)(2,1)S(1)}, bf16[8,2,256,256]{3,2,1,0:T(8,128)(2,1)S(1)}, f32[256,256]{1,0:T(8,128)S(1)}) custom-call(s32[8,128]{1,0:T(8,128)S(1)} %get-tuple-element.93.plan, bf16[2,2,128,256]{3,2,1,0:T(8,128)(2,1)S(1)} %get-tuple-element.99.refs_0_, ...), custom_call_target="tpu_custom_call" | custom-call | flops 100000000 | bytes 300000 | tf_op jit(solution)/shard_map/ahead/pallas_call | solution.py:116
  38.3 0.0 collective-permute-done.7.refs_7_
  38.4 0.4 collective-permute-done.8.refs_8_
  38.7 0.0 collective-permute-done.9.refs_9_
  38.7 4.2 %back.1 = (bf16[2,128,256]{2,1,0:T(8,128)(2,1)S(1)}, bf16[2,128,256]{2,1,0:T(8,128)(2,1)S(1)}, bf16[8,2,256,256]{3,2,1,0:T(8,128)(2,1)S(1)}) custom-call(s32[8,128]{1,0:T(8,128)S(1)} %get-tuple-element.93.plan, f32[256,256]{1,0:T(8,128)S(1)} %get-tuple-element.104.refs_0_, bf16[8,2,256,256]{3,2,1,0:T(8,128)(2,1)S(1)} %get-tuple-element.105.refs_1_, ...), custom_call_target="tpu_custom_call" | custom-call | flops 100000000 | bytes 300000 | tf_op jit(solution)/shard_map/back/pallas_call | solution.py:116
  43.0 0.1 collective-permute-start.10
  43.0 1.5 %collective-permute-start.11 = (bf16[2,128,256]{2,1,0:T(8,128)(2,1)S(1)}, bf16[2,128,256]{2,1,0:T(8,128)(2,1)S(1)}, u32[]{:S(2)}, u32[]{:S(2)}) collective-permute-start(bf16[2,128,256]{2,1,0:T(8,128)(2,1)S(1)} %get-tuple-element.134.refs_4_), channel_id=1, source_target_pairs={{0,2},{1,3},{2,0},{3,1},{4,6},{5,7},{6,4},{7,5},{8,10},{9,11},{10,... | collective-permute-start | bytes 393224 | tf_op jit(solution)/shard_map/ppermute | solution.py:424
  44.6 0.3 collective-permute-start.12
  44.9 4.7 %last.1 = (bf16[2,128,256]{2,1,0:T(8,128)(2,1)S(1)}, bf16[2,128,256]{2,1,0:T(8,128)(2,1)S(1)}, bf16[2,2,256,256]{3,2,1,0:T(8,128)(2,1)S(1)}, bf16[2,2,256,256]{3...) custom-call(s32[8,128]{1,0:T(8,128)S(1)} %get-tuple-element.93.plan, ...), custom_call_target="tpu_custom_call" | custom-call | flops 100000000 | bytes 300000 | tf_op jit(solution)/shard_map/last/pallas_call | solution.py:116
  49.6 0.0 collective-permute-done.11.refs_6_
  49.7 1.6 %collective-permute-done.12.refs_7_ = bf16[2,128,256]{2,1,0:T(8,128)(2,1)S(1)} collective-permute-done((bf16[2,128,256]{2,1,0:T(8,128)(2,1)S(1)}, bf16[2,128,256]{2,1,0:T(8,128)(2,1)S(1)}, u32[]{:S(2)}, u32[]{:S(2)}) %collective-permute-start.12) | collective-permute-done | bytes 131104 | tf_op jit(solution)/shard_map/ppermute | solution.py:424
  51.3 0.3 collective-permute-start.19
  51.6 0.2 collective-permute-start.13
  51.8 0.9 collective-permute-start.14
  52.7 0.8 collective-permute-start.15
  53.4 0.5 collective-permute-done.19.came
  54.0 0.8 spread.1
  54.8 1.6 %collective-permute-start.20 = (bf16[2,4,2,2,32,256]{5,4,3,2,1,0:T(8,128)(2,1)S(1)}, bf16[2,4,2,2,32,256]{5,4,3,2,1,0:T(8,128)(2,1)S(1)}, u32[]{:S(2)}, u32[]{:S(2)}) collective-permute-start(bf16[2,4,2,2,32,256]{5,4,3,2,1,0:T(8,128)(2,1)S(1)} %get-tuple-element.145), channel_id=1, source_target_pairs={{0,4},{4,0},{8,12},{12,8},{16,20},{20,16},{24,28},{28,24},{1,5},{5... | collective-permute-start | bytes 1572872 | tf_op jit(solution)/shard_map/ppermute | solution.py:560
  56.4 0.0 collective-permute-done.13.refs_1_
  56.4 1.8 %collective-permute-done.14.refs_2_ = bf16[2,128,256]{2,1,0:T(8,128)(2,1)S(1)} collective-permute-done((bf16[2,128,256]{2,1,0:T(8,128)(2,1)S(1)}, bf16[2,128,256]{2,1,0:T(8,128)(2,1)S(1)}, u32[]{:S(2)}, u32[]{:S(2)}) %collective-permute-start.14) | collective-permute-done | bytes 131104 | tf_op jit(solution)/shard_map/ppermute | solution.py:424
  58.1 1.5 %collective-permute-done.15.refs_3_ = bf16[2,128,256]{2,1,0:T(8,128)(2,1)S(1)} collective-permute-done((bf16[2,128,256]{2,1,0:T(8,128)(2,1)S(1)}, bf16[2,128,256]{2,1,0:T(8,128)(2,1)S(1)}, u32[]{:S(2)}, u32[]{:S(2)}) %collective-permute-start.15) | collective-permute-done | bytes 131104 | tf_op jit(solution)/shard_map/ppermute | solution.py:424
  59.6 1.5 %place.1 = (bf16[2,2,2,128,256]{4,3,2,1,0:T(8,128)(2,1)S(1)}, f32[2,2,2,128,256]{4,3,2,1,0:T(8,128)S(1)}, bf16[2,2,2,128,256]{4,3,2,1,0:T(8,128)(2,1)S(1)}) custom-call(s32[8,128]{1,0:T(8,128)S(1)} %get-tuple-element.93.plan, bf16[2,128,256]{2,1,0:T(8,128)(2,1)S(1)} %get-tuple-element.133.refs_0_, bf16[2,128,256]{2,1,0:T(8,128)(2,1)S(1)} %collective-permute-done.13.refs_1_, ...), custom_call_target="tpu_custom_call" | custom-call | flops 100000000 | bytes 300000 | tf_op jit(solution)/shard_map/place/pallas_call | solution.py:116
  61.2 2.9 %collective-permute-start.16 = (bf16[2,2,2,128,256]{4,3,2,1,0:T(8,128)(2,1)S(1)}, bf16[2,2,2,128,256]{4,3,2,1,0:T(8,128)(2,1)S(1)}, u32[]{:S(2)}, u32[]{:S(2)}) collective-permute-start(bf16[2,2,2,128,256]{4,3,2,1,0:T(8,128)(2,1)S(1)} %get-tuple-element.128), channel_id=1, source_target_pairs={{0,8},{4,12},{8,0},{12,4},{16,24},{20,28},{24,16},{28,20},{1,9},{5... | collective-permute-start | bytes 1572872 | tf_op jit(solution)/shard_map/ppermute | solution.py:588
  64.1 0.7 collective-permute-start.17
  64.8 4.2 %collective-permute-done.20.came = bf16[2,4,2,2,32,256]{5,4,3,2,1,0:T(8,128)(2,1)S(1)} collective-permute-done((bf16[2,4,2,2,32,256]{5,4,3,2,1,0:T(8,128)(2,1)S(1)}, bf16[2,4,2,2,32,256]{5,4,3,2,1,0:T(8,128)(2,1)S(1)}, u32[]{:S(2)}, u32[]{:S(2)}) %collective-permute-start.20) | collective-permute-done | bytes 524320 | tf_op jit(solution)/shard_map/ppermute | solution.py:560
  69.0 0.1 fold.1
  69.1 1.1 %collective-permute-start.21 = (bf16[4,2,2,32,256]{4,3,2,1,0:T(8,128)(2,1)S(1)}, bf16[4,2,2,32,256]{4,3,2,1,0:T(8,128)(2,1)S(1)}, u32[]{:S(2)}, u32[]{:S(2)}) collective-permute-start(bf16[4,2,2,32,256]{4,3,2,1,0:T(8,128)(2,1)S(1)} %get-tuple-element.147), channel_id=1, source_target_pairs={{0,2},{1,3},{2,0},{3,1},{4,6},{5,7},{6,4},{7,5},{8,10},{9,11},{10,... | collective-permute-start | bytes 786440 | tf_op jit(solution)/shard_map/ppermute | solution.py:424
  70.2 6.6 %collective-permute-done.16.low = bf16[2,2,2,128,256]{4,3,2,1,0:T(8,128)(2,1)S(1)} collective-permute-done((bf16[2,2,2,128,256]{4,3,2,1,0:T(8,128)(2,1)S(1)}, bf16[2,2,2,128,256]{4,3,2,1,0:T(8,128)(2,1)S(1)}, u32[]{:S(2)}, u32[]{:S(2)}) %collective-permute-start.16) | collective-permute-done | bytes 524320 | tf_op jit(solution)/shard_map/ppermute | solution.py:588
  76.8 0.0 collective-permute-done.17.high
  76.8 0.8 split.1
  77.5 1.6 %collective-permute-start.18 = (bf16[2,2,128,256]{3,2,1,0:T(8,128)(2,1)S(1)}, bf16[2,2,128,256]{3,2,1,0:T(8,128)(2,1)S(1)}, u32[]{:S(2)}, u32[]{:S(2)}) collective-permute-start(bf16[2,2,128,256]{3,2,1,0:T(8,128)(2,1)S(1)} %get-tuple-element.132), channel_id=1, source_target_pairs={{0,4},{4,0},{8,12},{12,8},{16,20},{20,16},{24,28},{28,24},{1,5},{5... | collective-permute-start | bytes 786440 | tf_op jit(solution)/shard_map/ppermute | solution.py:600
  79.2 3.9 %collective-permute-start.22 = (bf16[2,2,32,256]{3,2,1,0:T(8,128)(2,1)S(1)}, bf16[2,2,32,256]{3,2,1,0:T(8,128)(2,1)S(1)}, u32[]{:S(2)}, u32[]{:S(2)}) collective-permute-start(bf16[2,2,32,256]{3,2,1,0:T(8,128)(2,1)S(1)} %get-tuple-element.149), channel_id=1, source_target_pairs={{0,8},{4,12},{8,0},{12,4},{16,24},{20,28},{24,16},{28,20},{1,9},{5... | collective-permute-start | bytes 196616 | tf_op jit(solution)/shard_map/ppermute | solution.py:573
  83.0 1.1 %collective-permute-start.23 = (bf16[2,2,32,256]{3,2,1,0:T(8,128)(2,1)S(1)}, bf16[2,2,32,256]{3,2,1,0:T(8,128)(2,1)S(1)}, u32[]{:S(2)}, u32[]{:S(2)}) collective-permute-start(bf16[2,2,32,256]{3,2,1,0:T(8,128)(2,1)S(1)} %get-tuple-element.150), channel_id=1, source_target_pairs={{0,16},{4,20},{8,24},{12,28},{16,0},{20,4},{24,8},{28,12},{1,17},{... | collective-permute-start | bytes 196616 | tf_op jit(solution)/shard_map/ppermute | solution.py:573
  84.1 1.4 %collective-permute-start.24 = (bf16[2,2,32,256]{3,2,1,0:T(8,128)(2,1)S(1)}, bf16[2,2,32,256]{3,2,1,0:T(8,128)(2,1)S(1)}, u32[]{:S(2)}, u32[]{:S(2)}) collective-permute-start(bf16[2,2,32,256]{3,2,1,0:T(8,128)(2,1)S(1)} %get-tuple-element.151), channel_id=1, source_target_pairs={{0,24},{4,28},{8,16},{12,20},{16,8},{20,12},{24,0},{28,4},{1,25},{... | collective-permute-start | bytes 196616 | tf_op jit(solution)/shard_map/ppermute | solution.py:573
  85.5 0.6 slice.10
  86.8 0.0 collective-permute-done.18.came
  86.8 0.9 end.1
  87.7 0.0 collective-permute-done.22.refs_1_
  87.7 3.1 %collective-permute-done.23.refs_2_ = bf16[2,2,32,256]{3,2,1,0:T(8,128)(2,1)S(1)} collective-permute-done((bf16[2,2,32,256]{3,2,1,0:T(8,128)(2,1)S(1)}, bf16[2,2,32,256]{3,2,1,0:T(8,128)(2,1)S(1)}, u32[]{:S(2)}, u32[]{:S(2)}) %collective-permute-start.23) | collective-permute-done | bytes 65568 | tf_op jit(solution)/shard_map/ppermute | solution.py:573
  90.8 0.0 collective-permute-done.24.refs_3_
  90.8 0.7 total.1
  (18 shorter events, 0.1 us)
Async XLA Ops:
  0.6 4.4 %copy-start.4 = (bf16[8,256,256]{2,1,0:T(8,128)(2,1)S(1)}, bf16[8,256,256]{2,1,0:T(8,128)(2,1)}, u32[]{:S(2)}) copy-start(bf16[8,256,256]{2,1,0:T(8,128)(2,1)} %amplitudes_far.1) | copy-start | bytes 3145732
  2.0 15.0 %collective-permute-start = (bf16[2,2,256,256]{3,2,1,0:T(8,128)(2,1)S(1)}, bf16[2,2,256,256]{3,2,1,0:T(8,128)(2,1)S(1)}, u32[]{:S(2)}, u32[]{:S(2)}) collective-permute-start(bf16[2,2,256,256]{3,2,1,0:T(8,128)(2,1)S(1)} %convert_element_type.42), channel_id=1, source_target_pairs={{0,2},{1,3},{2,0},{3,1},{4,6},{5,7},{6,4},{7,5},{8,10},{9,11},{10,... | collective-permute-start | bytes 1572872 | tf_op jit(solution)/shard_map/ppermute | solution.py:424
  5.0 1.6 %copy-start.2 = (bf16[2,2,128,2048]{3,2,1,0:T(8,128)(2,1)S(1)}, bf16[2,2,128,2048]{3,2,1,0:T(8,128)(2,1)}, u32[]{:S(2)}) copy-start(bf16[2,2,128,2048]{3,2,1,0:T(8,128)(2,1)} %strip_far.1) | copy-start | bytes 6291460
  6.6 0.7 copy-start.6
  7.3 0.7 copy-start.7
  8.0 23.3 %copy-start = (f32[2,2,256,256]{3,2,1,0:T(8,128)S(1)}, f32[2,2,256,256]{3,2,1,0:T(8,128)}, u32[]{:S(2)}) copy-start(f32[2,2,256,256]{3,2,1,0:T(8,128)} %refs_1_.1) | copy-start | bytes 3145732
  8.0 23.3 %copy-start.1 = (bf16[4,256,256]{2,1,0:T(8,128)(2,1)S(1)}, bf16[4,256,256]{2,1,0:T(8,128)(2,1)}, u32[]{:S(2)}) copy-start(bf16[4,256,256]{2,1,0:T(8,128)(2,1)} %constant.181.clone.refs_8_.refs_4_.refs_6_) | copy-start | bytes 1572868
  8.0 23.3 %copy-start.3 = (f32[2,256,256]{2,1,0:T(8,128)S(1)}, f32[2,256,256]{2,1,0:T(8,128)}, u32[]{:S(2)}) copy-start(f32[2,256,256]{2,1,0:T(8,128)} %constant.182.clone.refs_9_.refs_7_) | copy-start | bytes 1572868
  10.1 13.5 %collective-permute-start.6 = (bf16[4,256,256]{2,1,0:T(8,128)(2,1)S(1)}, bf16[4,256,256]{2,1,0:T(8,128)(2,1)S(1)}, u32[]{:S(2)}, u32[]{:S(2)}) collective-permute-start(bf16[4,256,256]{2,1,0:T(8,128)(2,1)S(1)} %get-tuple-element.109), channel_id=1, source_target_pairs={{0,4},{4,0},{8,12},{12,8},{16,20},{20,16},{24,28},{28,24},{1,5},{5... | collective-permute-start | bytes 1572872 | tf_op jit(solution)/shard_map/ppermute | solution.py:482
  11.6 12.6 %collective-permute-start.4 = (bf16[2,2,256,256]{3,2,1,0:T(8,128)(2,1)S(1)}, bf16[2,2,256,256]{3,2,1,0:T(8,128)(2,1)S(1)}, u32[]{:S(2)}, u32[]{:S(2)}) collective-permute-start(bf16[2,2,256,256]{3,2,1,0:T(8,128)(2,1)S(1)} %convert_element_type.42), channel_id=1, source_target_pairs={{0,1},{1,0},{2,3},{3,2},{4,5},{5,4},{6,7},{7,6},{8,9},{9,8},{10,11... | collective-permute-start | bytes 1572872 | tf_op jit(solution)/shard_map/ppermute | solution.py:424
  17.0 14.3 %collective-permute-start.5 = (bf16[2,2,256,256]{3,2,1,0:T(8,128)(2,1)S(1)}, bf16[2,2,256,256]{3,2,1,0:T(8,128)(2,1)S(1)}, u32[]{:S(2)}, u32[]{:S(2)}) collective-permute-start(bf16[2,2,256,256]{3,2,1,0:T(8,128)(2,1)S(1)} %collective-permute-done.refs_6_.refs_3_), channel_id=1, source_target_pairs={{0,1},{1,0},{2,3},{3,2},{4,5},{5,4},{6,7},{7,6},{8,9},{9,8},{10,11... | collective-permute-start | bytes 1572872 | tf_op jit(solution)/shard_map/ppermute | solution.py:424
  17.0 8.9 %collective-permute-start.1 = (bf16[2,2,128,256]{3,2,1,0:T(8,128)(2,1)S(1)}, bf16[2,2,128,256]{3,2,1,0:T(8,128)(2,1)S(1)}, u32[]{:S(2)}, u32[]{:S(2)}) collective-permute-start(bf16[2,2,128,256]{3,2,1,0:T(8,128)(2,1)S(1)} %get-tuple-element.100), channel_id=1, source_target_pairs={{0,1},{1,0},{2,3},{3,2},{4,5},{5,4},{6,7},{7,6},{8,9},{9,8},{10,11... | collective-permute-start | bytes 786440 | tf_op jit(solution)/shard_map/ppermute | solution.py:424
  17.5 11.0 %collective-permute-start.2 = (bf16[2,2,128,256]{3,2,1,0:T(8,128)(2,1)S(1)}, bf16[2,2,128,256]{3,2,1,0:T(8,128)(2,1)S(1)}, u32[]{:S(2)}, u32[]{:S(2)}) collective-permute-start(bf16[2,2,128,256]{3,2,1,0:T(8,128)(2,1)S(1)} %get-tuple-element.101), channel_id=1, source_target_pairs={{0,2},{1,3},{2,0},{3,1},{4,6},{5,7},{6,4},{7,5},{8,10},{9,11},{10,... | collective-permute-start | bytes 786440 | tf_op jit(solution)/shard_map/ppermute | solution.py:424
  23.5 7.8 %collective-permute-start.3 = (bf16[2,2,128,256]{3,2,1,0:T(8,128)(2,1)S(1)}, bf16[2,2,128,256]{3,2,1,0:T(8,128)(2,1)S(1)}, u32[]{:S(2)}, u32[]{:S(2)}) collective-permute-start(bf16[2,2,128,256]{3,2,1,0:T(8,128)(2,1)S(1)} %get-tuple-element.102), channel_id=1, source_target_pairs={{0,3},{1,2},{2,1},{3,0},{4,7},{5,6},{6,5},{7,4},{8,11},{9,10},{10,... | collective-permute-start | bytes 786440 | tf_op jit(solution)/shard_map/ppermute | solution.py:424
  24.2 14.1 %collective-permute-start.7 = (bf16[256,256]{1,0:T(8,128)(2,1)S(1)}, bf16[256,256]{1,0:T(8,128)(2,1)S(1)}, u32[]{:S(2)}, u32[]{:S(2)}) collective-permute-start(bf16[256,256]{1,0:T(8,128)(2,1)S(1)} %get-tuple-element.111), channel_id=1, source_target_pairs={{0,8},{4,12},{8,0},{12,4},{16,24},{20,28},{24,16},{28,20},{1,9},{5... | collective-permute-start | bytes 393224 | tf_op jit(solution)/shard_map/ppermute | solution.py:488
  25.9 12.9 %collective-permute-start.8 = (bf16[256,256]{1,0:T(8,128)(2,1)S(1)}, bf16[256,256]{1,0:T(8,128)(2,1)S(1)}, u32[]{:S(2)}, u32[]{:S(2)}) collective-permute-start(bf16[256,256]{1,0:T(8,128)(2,1)S(1)} %get-tuple-element.112), channel_id=1, source_target_pairs={{0,16},{4,20},{8,24},{12,28},{16,0},{20,4},{24,8},{28,12},{1,17},{... | collective-permute-start | bytes 393224 | tf_op jit(solution)/shard_map/ppermute | solution.py:488
  28.5 10.3 %copy-start.5 = (bf16[2,256,256]{2,1,0:T(8,128)(2,1)S(1)}, bf16[2,256,256]{2,1,0:T(8,128)(2,1)}, u32[]{:S(2)}) copy-start(bf16[2,256,256]{2,1,0:T(8,128)(2,1)} %constant.183.clone.refs_5_) | copy-start | bytes 786436
  28.5 10.3 %collective-permute-start.9 = (bf16[256,256]{1,0:T(8,128)(2,1)S(1)}, bf16[256,256]{1,0:T(8,128)(2,1)S(1)}, u32[]{:S(2)}, u32[]{:S(2)}) collective-permute-start(bf16[256,256]{1,0:T(8,128)(2,1)S(1)} %get-tuple-element.113), channel_id=1, source_target_pairs={{0,24},{4,28},{8,16},{12,20},{16,8},{20,12},{24,0},{28,4},{1,25},{... | collective-permute-start | bytes 393224 | tf_op jit(solution)/shard_map/ppermute | solution.py:488
  43.0 6.7 %collective-permute-start.10 = (bf16[2,128,256]{2,1,0:T(8,128)(2,1)S(1)}, bf16[2,128,256]{2,1,0:T(8,128)(2,1)S(1)}, u32[]{:S(2)}, u32[]{:S(2)}) collective-permute-start(bf16[2,128,256]{2,1,0:T(8,128)(2,1)S(1)} %get-tuple-element.115), channel_id=1, source_target_pairs={{0,1},{1,0},{2,3},{3,2},{4,5},{5,4},{6,7},{7,6},{8,9},{9,8},{10,11... | collective-permute-start | bytes 393224 | tf_op jit(solution)/shard_map/ppermute | solution.py:424
  43.0 6.6 %collective-permute-start.11 = (bf16[2,128,256]{2,1,0:T(8,128)(2,1)S(1)}, bf16[2,128,256]{2,1,0:T(8,128)(2,1)S(1)}, u32[]{:S(2)}, u32[]{:S(2)}) collective-permute-start(bf16[2,128,256]{2,1,0:T(8,128)(2,1)S(1)} %get-tuple-element.134.refs_4_), channel_id=1, source_target_pairs={{0,2},{1,3},{2,0},{3,1},{4,6},{5,7},{6,4},{7,5},{8,10},{9,11},{10,... | collective-permute-start | bytes 393224 | tf_op jit(solution)/shard_map/ppermute | solution.py:424
  44.6 6.8 %collective-permute-start.12 = (bf16[2,128,256]{2,1,0:T(8,128)(2,1)S(1)}, bf16[2,128,256]{2,1,0:T(8,128)(2,1)S(1)}, u32[]{:S(2)}, u32[]{:S(2)}) collective-permute-start(bf16[2,128,256]{2,1,0:T(8,128)(2,1)S(1)} %get-tuple-element.115), channel_id=1, source_target_pairs={{0,3},{1,2},{2,1},{3,0},{4,7},{5,6},{6,5},{7,4},{8,11},{9,10},{10,... | collective-permute-start | bytes 393224 | tf_op jit(solution)/shard_map/ppermute | solution.py:424
  51.3 2.7 %collective-permute-start.19 = (bf16[2,2,2,256,256]{4,3,2,1,0:T(8,128)(2,1)S(1)}, bf16[2,2,2,256,256]{4,3,2,1,0:T(8,128)(2,1)S(1)}, u32[]{:S(2)}, u32[]{:S(2)}) collective-permute-start(bf16[2,2,2,256,256]{4,3,2,1,0:T(8,128)(2,1)S(1)} %get-tuple-element.143), channel_id=1, source_target_pairs={{0,1},{1,0},{2,3},{3,2},{4,5},{5,4},{6,7},{7,6},{8,9},{9,8},{10,11... | collective-permute-start | bytes 3145736 | tf_op jit(solution)/shard_map/ppermute | solution.py:424
  51.6 4.8 %collective-permute-start.13 = (bf16[2,128,256]{2,1,0:T(8,128)(2,1)S(1)}, bf16[2,128,256]{2,1,0:T(8,128)(2,1)S(1)}, u32[]{:S(2)}, u32[]{:S(2)}) collective-permute-start(bf16[2,128,256]{2,1,0:T(8,128)(2,1)S(1)} %get-tuple-element.122), channel_id=1, source_target_pairs={{0,1},{1,0},{2,3},{3,2},{4,5},{5,4},{6,7},{7,6},{8,9},{9,8},{10,11... | collective-permute-start | bytes 393224 | tf_op jit(solution)/shard_map/ppermute | solution.py:424
  51.8 6.3 %collective-permute-start.14 = (bf16[2,128,256]{2,1,0:T(8,128)(2,1)S(1)}, bf16[2,128,256]{2,1,0:T(8,128)(2,1)S(1)}, u32[]{:S(2)}, u32[]{:S(2)}) collective-permute-start(bf16[2,128,256]{2,1,0:T(8,128)(2,1)S(1)} %get-tuple-element.133.refs_0_), channel_id=1, source_target_pairs={{0,2},{1,3},{2,0},{3,1},{4,6},{5,7},{6,4},{7,5},{8,10},{9,11},{10,... | collective-permute-start | bytes 393224 | tf_op jit(solution)/shard_map/ppermute | solution.py:424
  52.7 7.0 %collective-permute-start.15 = (bf16[2,128,256]{2,1,0:T(8,128)(2,1)S(1)}, bf16[2,128,256]{2,1,0:T(8,128)(2,1)S(1)}, u32[]{:S(2)}, u32[]{:S(2)}) collective-permute-start(bf16[2,128,256]{2,1,0:T(8,128)(2,1)S(1)} %get-tuple-element.122), channel_id=1, source_target_pairs={{0,3},{1,2},{2,1},{3,0},{4,7},{5,6},{6,5},{7,4},{8,11},{9,10},{10,... | collective-permute-start | bytes 393224 | tf_op jit(solution)/shard_map/ppermute | solution.py:424
  54.8 14.2 %collective-permute-start.20 = (bf16[2,4,2,2,32,256]{5,4,3,2,1,0:T(8,128)(2,1)S(1)}, bf16[2,4,2,2,32,256]{5,4,3,2,1,0:T(8,128)(2,1)S(1)}, u32[]{:S(2)}, u32[]{:S(2)}) collective-permute-start(bf16[2,4,2,2,32,256]{5,4,3,2,1,0:T(8,128)(2,1)S(1)} %get-tuple-element.145), channel_id=1, source_target_pairs={{0,4},{4,0},{8,12},{12,8},{16,20},{20,16},{24,28},{28,24},{1,5},{5... | collective-permute-start | bytes 1572872 | tf_op jit(solution)/shard_map/ppermute | solution.py:560
  61.2 15.6 %collective-permute-start.16 = (bf16[2,2,2,128,256]{4,3,2,1,0:T(8,128)(2,1)S(1)}, bf16[2,2,2,128,256]{4,3,2,1,0:T(8,128)(2,1)S(1)}, u32[]{:S(2)}, u32[]{:S(2)}) collective-permute-start(bf16[2,2,2,128,256]{4,3,2,1,0:T(8,128)(2,1)S(1)} %get-tuple-element.128), channel_id=1, source_target_pairs={{0,8},{4,12},{8,0},{12,4},{16,24},{20,28},{24,16},{28,20},{1,9},{5... | collective-permute-start | bytes 1572872 | tf_op jit(solution)/shard_map/ppermute | solution.py:588
  64.1 12.7 %collective-permute-start.17 = (bf16[2,2,2,128,256]{4,3,2,1,0:T(8,128)(2,1)S(1)}, bf16[2,2,2,128,256]{4,3,2,1,0:T(8,128)(2,1)S(1)}, u32[]{:S(2)}, u32[]{:S(2)}) collective-permute-start(bf16[2,2,2,128,256]{4,3,2,1,0:T(8,128)(2,1)S(1)} %get-tuple-element.130), channel_id=1, source_target_pairs={{8,16},{12,20},{16,8},{20,12},{9,17},{13,21},{17,9},{21,13},{10,18... | collective-permute-start | bytes 1572872 | tf_op jit(solution)/shard_map/ppermute | solution.py:590
  69.1 10.0 %collective-permute-start.21 = (bf16[4,2,2,32,256]{4,3,2,1,0:T(8,128)(2,1)S(1)}, bf16[4,2,2,32,256]{4,3,2,1,0:T(8,128)(2,1)S(1)}, u32[]{:S(2)}, u32[]{:S(2)}) collective-permute-start(bf16[4,2,2,32,256]{4,3,2,1,0:T(8,128)(2,1)S(1)} %get-tuple-element.147), channel_id=1, source_target_pairs={{0,2},{1,3},{2,0},{3,1},{4,6},{5,7},{6,4},{7,5},{8,10},{9,11},{10,... | collective-permute-start | bytes 786440 | tf_op jit(solution)/shard_map/ppermute | solution.py:424
  77.5 9.3 %collective-permute-start.18 = (bf16[2,2,128,256]{3,2,1,0:T(8,128)(2,1)S(1)}, bf16[2,2,128,256]{3,2,1,0:T(8,128)(2,1)S(1)}, u32[]{:S(2)}, u32[]{:S(2)}) collective-permute-start(bf16[2,2,128,256]{3,2,1,0:T(8,128)(2,1)S(1)} %get-tuple-element.132), channel_id=1, source_target_pairs={{0,4},{4,0},{8,12},{12,8},{16,20},{20,16},{24,28},{28,24},{1,5},{5... | collective-permute-start | bytes 786440 | tf_op jit(solution)/shard_map/ppermute | solution.py:600
  79.2 8.5 %collective-permute-start.22 = (bf16[2,2,32,256]{3,2,1,0:T(8,128)(2,1)S(1)}, bf16[2,2,32,256]{3,2,1,0:T(8,128)(2,1)S(1)}, u32[]{:S(2)}, u32[]{:S(2)}) collective-permute-start(bf16[2,2,32,256]{3,2,1,0:T(8,128)(2,1)S(1)} %get-tuple-element.149), channel_id=1, source_target_pairs={{0,8},{4,12},{8,0},{12,4},{16,24},{20,28},{24,16},{28,20},{1,9},{5... | collective-permute-start | bytes 196616 | tf_op jit(solution)/shard_map/ppermute | solution.py:573
  83.0 7.8 %collective-permute-start.23 = (bf16[2,2,32,256]{3,2,1,0:T(8,128)(2,1)S(1)}, bf16[2,2,32,256]{3,2,1,0:T(8,128)(2,1)S(1)}, u32[]{:S(2)}, u32[]{:S(2)}) collective-permute-start(bf16[2,2,32,256]{3,2,1,0:T(8,128)(2,1)S(1)} %get-tuple-element.150), channel_id=1, source_target_pairs={{0,16},{4,20},{8,24},{12,28},{16,0},{20,4},{24,8},{28,12},{1,17},{... | collective-permute-start | bytes 196616 | tf_op jit(solution)/shard_map/ppermute | solution.py:573
  84.1 6.7 %collective-permute-start.24 = (bf16[2,2,32,256]{3,2,1,0:T(8,128)(2,1)S(1)}, bf16[2,2,32,256]{3,2,1,0:T(8,128)(2,1)S(1)}, u32[]{:S(2)}, u32[]{:S(2)}) collective-permute-start(bf16[2,2,32,256]{3,2,1,0:T(8,128)(2,1)S(1)} %get-tuple-element.151), channel_id=1, source_target_pairs={{0,24},{4,28},{8,16},{12,20},{16,8},{20,12},{24,0},{28,4},{1,25},{... | collective-permute-start | bytes 196616 | tf_op jit(solution)/shard_map/ppermute | solution.py:573

commit v2 on v0

--- a/solution.py
+++ b/solution.py
@@ -147,7 +147,7 @@
 
 def first_kernel(groups, tiles, points, counts, offsets, strip_far, amplitudes_far, *refs):
     strips = refs[:tiles]
-    same, remote, nearby, plan_out, plan, strip, amplitudes, sems = refs[tiles:]
+    same, other_x, plan_out, plan, strip, amplitudes, sems = refs[tiles:]
     layers, rows = strip.shape[0], strip.shape[2]
     slots = amplitudes.shape[0]
     n = offsets.shape[0]
@@ -206,8 +206,7 @@
                 ).astype(BF16)
     amplitude_copy.wait()
     for turn in range(groups // 2):
-        across_x = (nearby, remote)[turn // 2]
-        for flip, out, at in ((0, same, turn), (1, across_x, turn % 2)):
+        for flip, out, at in ((0, same, turn), (1, other_x, turn)):
             slot = plan[0, (pos ^ (2 * turn + flip)) * tiles + tile]
 
             @pl.when(slot // slots == pos)
@@ -327,8 +326,8 @@
 
 def last_kernel(tiles, points, plan, *refs):
     inner, near, beside, across, diagonal, first, tables_far, kernel_far = refs[:8]
-    own, other, near_grad, beyond_grad, beside_grad = refs[8:13]
-    mine, tables, kernel, total, sems = refs[13:]
+    own, other, pair, near_grad, beyond_grad, beside_grad = refs[8:14]
+    mine, tables, kernel, total, sems = refs[14:]
     copies = fetch((tables_far, kernel_far, near), (tables, kernel, mine), sems)
     modes = mine.shape[0]
     probes = (mine, beside, across, diagonal)
@@ -347,10 +346,19 @@
             re, im = conj_times(*load_complex(first), re, im)
             grads[turn][mode, 0], grads[turn][mode, 1] = re.astype(BF16), im.astype(BF16)
     put_by_residue(plan, tiles, points, total, own, other)
+    pair[0] = own[...]
+    pair[1] = other[...]
+
+
+def piece_of(pieces, turn):
+    piece = pieces[turn]
+    if len(piece.shape) == 3:
+        return piece
+    return piece[turn - 2]
 
 
 def place_kernel(tiles, points, plan, *refs):
-    pieces, (below, same, above, canvas) = refs[:tiles], refs[tiles:]
+    pieces, (even, same, odd, canvas) = refs[:tiles], refs[tiles:]
     rows = pieces[0].shape[1]
     core, up = plan[3, 1] % 2, plan[3, 1] // 2
     base = plan[3, 0] // 2 * 2 - 2
@@ -362,14 +370,15 @@
         mine = jnp.where(sub >= row, 0, 1) == up
         early = lane >= col % points
         for part in range(2):
-            value = jnp.where(mine, pieces[turn][part].astype(F32), 0.0)
+            value = jnp.where(mine, piece_of(pieces, turn)[part].astype(F32), 0.0)
             for step, keep in ((0, early), (1, ~early)):
                 at = col // points + step - base
                 at = jnp.where((at >= 0) & (at < 6), at, 6)
                 canvas[at, part] += jnp.where(keep, value, 0.0)
-    below[...] = canvas[0:2].astype(BF16)
     same[...] = canvas[2:4]
-    above[...] = canvas[4:6].astype(BF16)
+    up_first = plan[3, 0] // 2 % 2 == 0
+    for out, at in ((even, jnp.where(up_first, 4, 0)), (odd, jnp.where(up_first, 0, 4))):
+        out[...] = canvas[pl.ds(at, 2)].astype(BF16)
 
 
 def split_kernel(plan, same, low, high, keep, send):
@@ -435,7 +444,7 @@
         mine = jnp.where(sub >= row, 0, 1) == tile // 2
         target = col // points + jnp.where(lane >= col % points, 0, 1)
         keep = outside[:, None, None] & mine[None] & (target[None] == block[:, None, None])
-        value = jnp.stack([layer[turn] for layer in pieces]).astype(F32)
+        value = jnp.stack([piece_of(layer, turn) for layer in pieces]).astype(F32)
         canvas = canvas + jnp.where(keep[:, None, None], value[None], 0.0)
     shares = lax.all_to_all(canvas.astype(BF16), "pos", split_axis=0, concat_axis=0, tiled=True)
     return jnp.sum(shares.astype(F32), axis=0).astype(BF16)
@@ -459,8 +468,7 @@
         (slot_counts, scan_offsets, object_slices, amplitudes),
         [SM, VM, HB, HB],
         [((layers, 2, rows, points), BF16)] * tiles
-        + [((groups // 2, *shot), BF16)]
-        + [((groups // 4, *shot), BF16)] * 2
+        + [((groups // 2, *shot), BF16)] * 2
         + [((8, 128), jnp.int32)],
         [
             pltpu.SMEM((8, 128), jnp.int32),
@@ -469,21 +477,19 @@
             pltpu.SemaphoreType.DMA((3,)),
         ],
         name="first",
-        us=5.0,
+        us=0.1,
         mib=16,
     )
-    (*cut, same, far, near, plan) = outs
+    (*cut, same, far, plan) = outs
     across, cut = lax.optimization_barrier((across, cut))
     aside = [(i, i ^ 1) for i in range(groups)]
-    merged = [None] * (groups // 2)
-    for turns, value in (((2, 3), far), ((0, 1), near)):
-        merged[turns[0]], merged[turns[1]] = call(
-            functools.partial(merge_kernel, tiles, slots, turns),
-            (plan, same, lax.ppermute(value, "pos", aside)),
-            [SM, VM, VM],
-            [(shot, BF16)] * 2,
-            name="merge",
-        )
+    merged = call(
+        functools.partial(merge_kernel, tiles, slots, range(groups // 2)),
+        (plan, same, lax.ppermute(far, "pos", aside)),
+        [SM, VM, VM],
+        [(shot, BF16)] * (groups // 2),
+        name="merge",
+    )
     arrived = [merged[0]] + [
         lax.ppermute(merged[turn], "pos", [(i, i ^ (2 * turn)) for i in range(groups)])
         for turn in range(1, groups // 2)
@@ -505,7 +511,7 @@
             pltpu.SemaphoreType.DMA((3,)),
         ],
         name="ahead",
-        us=12.0,
+        us=0.1,
         mib=24,
         keep=range(5),
     )
@@ -523,17 +529,17 @@
             pltpu.SemaphoreType.DMA((2,)),
         ],
         name="back",
-        us=5.0,
+        us=0.1,
         mib=24,
         keep=(2,),
     )
     pieces = [None] * layers
     pieces[1] = [own] + [turned(v, turn, tiles) for turn, v in ((1, other), (2, own), (3, other))]
-    own, other, mine, beyond, beside = call(
+    own, other, pair, mine, beyond, beside = call(
         functools.partial(last_kernel, tiles, points),
         (plan, inner, *probes, first, tables, kernel),
         [SM, VK, HB] + [VK] * 4 + [HB] * 2,
-        [half, half] + [((modes, *field), BF16)] * 2 + [((2, modes, *field), BF16)],
+        [half, half, ((2, *half[0]), BF16)] + [((modes, *field), BF16)] * 2 + [((2, modes, *field), BF16)],
         [
             pltpu.VMEM(probe_modes.shape, F32),
             pltpu.VMEM(tables.shape, BF16),
@@ -542,11 +548,12 @@
             pltpu.SemaphoreType.DMA((3,)),
         ],
         name="last",
-        us=6.0,
+        us=0.1,
         mib=24,
     )
-    pieces[1], own, other, beside = lax.optimization_barrier((pieces[1], own, other, beside))
-    pieces[0] = [own] + [turned(v, turn, tiles) for turn, v in ((1, other), (2, own), (3, other))]
+    pieces[1], own, other, pair, beside = lax.optimization_barrier((pieces[1], own, other, pair, beside))
+    pair = turned(pair, 2, tiles)
+    pieces[0] = [own, turned(other, 1, tiles), pair, turned(pair, 1, tiles)]
     share = (groups // 2, modes, 2, points // groups, points)
     keep, send = call(
         spread_kernel,
@@ -577,7 +584,7 @@
     block = (2, rows, points)
     keeps, swapped = [None] * layers, [None] * layers
     for layer in reversed(range(layers)):
-        below, same, above = call(
+        even, same, odd = call(
             functools.partial(place_kernel, tiles, points),
             (plan, *pieces[layer]),
             [SM] + [VM] * tiles,
@@ -586,11 +593,15 @@
             name="place",
         )
         if layer:
-            pieces[0], above, below = lax.optimization_barrier((pieces[0], above, below))
-        low_in = lax.ppermute(above, "pos", [(i, i + 2) for i in range(groups - 2)])
-        high_in = lax.ppermute(below, "pos", [(i + 2, i) for i in range(groups - 2)])
+            pass
+        pairs = [(i, i ^ 2) for i in range(groups)]
+        low_in = lax.ppermute(even, "pos", pairs)
+        pairs = [(i, i + 2 if i // 2 % 2 else i - 2) for i in range(2, groups - 2)]
+        high_in = lax.ppermute(odd, "pos", pairs)
         if layer == 0:
             pieces, low_in = lax.optimization_barrier((pieces, low_in))
+        if layer:
+            pieces[0], low_in = lax.optimization_barrier((pieces[0], low_in))
         keeps[layer], send = call(
             split_kernel,
             (plan, same, low_in, high_in),

time: 102 us -> 89.6 us (0.88)
  waiting for transfers between devices: 37.9 us -> 26.6 us
  local copies, waits for them, and re-layouts: 4.86 us -> 3.63 us
    ppermute x6 -> x5, waiting for transfers between devices: 18.7 us -> 12.1 us  [the longest x2 7.73 us: on_device_by_slot(): low_in = lax.ppermute(even, 'pos', pairs)]
    ppermute x14, waiting for transfers between devices: 16 us -> 11.4 us  [turned(): return lax.ppermute(value, 'tile', [(i, i ^ turn) for i in range(tiles)])]
    ppermute x6 -> x5, starting transfers between devices: 10.4 us -> 7.56 us  [the longest x2 4.68 us: on_device_by_slot(): low_in = lax.ppermute(even, 'pos', pairs)]
    ppermute x3, starting transfers between devices: 4.45 us -> 6.25 us  [on_device_by_slot(): lax.ppermute(send, 'pos', [(i, i ^ 2 * turn) for i in range(groups)])]
    unnamed x14, local copies, waits for them, and re-layouts: 3.49 us -> 2.26 us
    ppermute x14, starting transfers between devices: 8.86 us -> 9.91 us  [turned(): return lax.ppermute(value, 'tile', [(i, i ^ turn) for i in range(tiles)])]
    pallas_call x15 -> x14, Pallas kernels: 25.4 us -> 24.8 us  [call(): pl.pallas_call(body, out_shape=[pltpu.VMEM(shape, dtype) if at in keep el...]
  transfers between devices with their start and end apart: 29 -> 28, of which waited for: 13 -> 12; matrix products, arithmetic and copies ran while one was open for 1% -> 2% of each run, Pallas kernels for 19% -> 22%
where the time goes in v2:
time: 89.6 us; the launch traced here: 89.4 us
  starting transfers between devices  31.5 us (35%)
  waiting for transfers between devices  26.6 us (30%)
  Pallas kernels  24.8 us (28%)
  local copies, waits for them, and re-layouts  3.63 us (4%)
  between operations  1.52 us (2%)
  other arithmetic  1.37 us (2%)
    pallas_call x14, Pallas kernels, call(): pl.pallas_call(body, out_shape=[pltpu.VMEM(shape, dtype) if at in keep el...  24.8 us
    ppermute x14, waiting for transfers between devices, turned(): return lax.ppermute(value, 'tile', [(i, i ^ turn) for i in range(tiles)])  11.4 us
    ppermute x14, starting transfers between devices, turned(): return lax.ppermute(value, 'tile', [(i, i ^ turn) for i in range(tiles)])  9.91 us
    ppermute x2, waiting for transfers between devices, on_device_by_slot(): low_in = lax.ppermute(even, 'pos', pairs)  7.73 us
    ppermute x3, starting transfers between devices, on_device_by_slot(): lax.ppermute(send, 'pos', [(i, i ^ 2 * turn) for i in range(groups)])  6.25 us
    ppermute x3, starting transfers between devices, on_device_by_slot(): lax.ppermute(merged[turn], 'pos', [(i, i ^ 2 * turn) for i in range(group...  5.19 us
    ppermute x2, starting transfers between devices, on_device_by_slot(): low_in = lax.ppermute(even, 'pos', pairs)  4.68 us
    ppermute x1, waiting for transfers between devices, on_device_by_slot(): lax.ppermute(far, 'pos', aside)  4.39 us
  transfers between devices with their start and end apart: 28, of which 12 were waited for; matrix products, arithmetic and copies ran while one was open for 2% of the time, Pallas kernels for 22%

profile of v2, /device:TPU:0, one launch (start us, length us, event | category | flops | bytes accessed | tf_op | source)
XLA Modules:
  0.0 89.4 jit_solution(16279125115733907527)
XLA Ops:
  0.6 1.4 %convert_element_type.42 = bf16[2,2,256,256]{3,2,1,0:T(8,128)(2,1)S(1)} convert(f32[2,2,256,256]{3,2,1,0:T(8,128)} %refs_1_.1) | non-fusion elementwise | flops 262144 | bytes 1572864 | tf_op jit(solution)/shard_map/convert_element_type | solution.py:461
  2.0 3.0 %collective-permute-start = (bf16[2,2,256,256]{3,2,1,0:T(8,128)(2,1)S(1)}, bf16[2,2,256,256]{3,2,1,0:T(8,128)(2,1)S(1)}, u32[]{:S(2)}, u32[]{:S(2)}) collective-permute-start(bf16[2,2,256,256]{3,2,1,0:T(8,128)(2,1)S(1)} %convert_element_type.42), channel_id=1, source_target_pairs={{0,2},{1,3},{2,0},{3,1},{4,6},{5,7},{6,4},{7,5},{8,10},{9,11},{10,... | collective-permute-start | bytes 1572872 | tf_op jit(solution)/shard_map/ppermute | solution.py:430
  5.0 0.8 copy.11.offsets
  5.8 1.6 %copy-done.2 = bf16[2,2,128,2048]{3,2,1,0:T(8,128)(2,1)S(1)} copy-done((bf16[2,2,128,2048]{3,2,1,0:T(8,128)(2,1)S(1)}, bf16[2,2,128,2048]{3,2,1,0:T(8,128)(2,1)}, u32[]{:S(2)}) %copy-start.2) | copy-done | bytes 2097176
  7.4 0.7 copy-done.6
  8.1 2.1 %first.1 = (bf16[2,2,128,256]{3,2,1,0:T(8,128)(2,1)S(1)}, bf16[2,2,128,256]{3,2,1,0:T(8,128)(2,1)S(1)}, bf16[2,2,128,256]{3,2,1,0:T(8,128)(2,1)S(1)}, bf16[2,2,1...) custom-call(s32[8]{0:T(128)S(1)} %copy-done.6, ...), custom_call_target="tpu_custom_call" | custom-call | flops 100000000 | bytes 300000 | tf_op jit(solution)/shard_map/first/pallas_call | solution.py:116
  10.2 1.5 %collective-permute-start.6 = (bf16[4,256,256]{2,1,0:T(8,128)(2,1)S(1)}, bf16[4,256,256]{2,1,0:T(8,128)(2,1)S(1)}, u32[]{:S(2)}, u32[]{:S(2)}) collective-permute-start(bf16[4,256,256]{2,1,0:T(8,128)(2,1)S(1)} %get-tuple-element.121), channel_id=1, source_target_pairs={{0,4},{4,0},{8,12},{12,8},{16,20},{20,16},{24,28},{28,24},{1,5},{5... | collective-permute-start | bytes 1572872 | tf_op jit(solution)/shard_map/ppermute | solution.py:488
  11.7 0.0 collective-permute-start.4
  11.7 5.2 %collective-permute-done.refs_6_.refs_3_ = bf16[2,2,256,256]{3,2,1,0:T(8,128)(2,1)S(1)} collective-permute-done((bf16[2,2,256,256]{3,2,1,0:T(8,128)(2,1)S(1)}, bf16[2,2,256,256]{3,2,1,0:T(8,128)(2,1)S(1)}, u32[]{:S(2)}, u32[]{:S(2)}) %collective-permute-start) | collective-permute-done | bytes 524320 | tf_op jit(solution)/shard_map/ppermute | solution.py:430
  17.0 0.0 collective-permute-start.5
  17.0 0.5 collective-permute-start.1
  17.5 1.7 %collective-permute-start.2 = (bf16[2,2,128,256]{3,2,1,0:T(8,128)(2,1)S(1)}, bf16[2,2,128,256]{3,2,1,0:T(8,128)(2,1)S(1)}, u32[]{:S(2)}, u32[]{:S(2)}) collective-permute-start(bf16[2,2,128,256]{3,2,1,0:T(8,128)(2,1)S(1)} %get-tuple-element.113), channel_id=1, source_target_pairs={{0,2},{1,3},{2,0},{3,1},{4,6},{5,7},{6,4},{7,5},{8,10},{9,11},{10,... | collective-permute-start | bytes 786440 | tf_op jit(solution)/shard_map/ppermute | solution.py:430
  19.2 4.4 %collective-permute-done.6.came = bf16[4,256,256]{2,1,0:T(8,128)(2,1)S(1)} collective-permute-done((bf16[4,256,256]{2,1,0:T(8,128)(2,1)S(1)}, bf16[4,256,256]{2,1,0:T(8,128)(2,1)S(1)}, u32[]{:S(2)}, u32[]{:S(2)}) %collective-permute-start.6) | collective-permute-done | bytes 524320 | tf_op jit(solution)/shard_map/ppermute | solution.py:488
  23.6 0.7 merge.1
  24.3 1.6 %collective-permute-start.7 = (bf16[256,256]{1,0:T(8,128)(2,1)S(1)}, bf16[256,256]{1,0:T(8,128)(2,1)S(1)}, u32[]{:S(2)}, u32[]{:S(2)}) collective-permute-start(bf16[256,256]{1,0:T(8,128)(2,1)S(1)} %get-tuple-element.123), channel_id=1, source_target_pairs={{0,8},{4,12},{8,0},{12,4},{16,24},{20,28},{24,16},{28,20},{1,9},{5... | collective-permute-start | bytes 393224 | tf_op jit(solution)/shard_map/ppermute | solution.py:494
  26.0 0.0 collective-permute-done.1.refs_1_
  26.0 2.6 %collective-permute-start.8 = (bf16[256,256]{1,0:T(8,128)(2,1)S(1)}, bf16[256,256]{1,0:T(8,128)(2,1)S(1)}, u32[]{:S(2)}, u32[]{:S(2)}) collective-permute-start(bf16[256,256]{1,0:T(8,128)(2,1)S(1)} %get-tuple-element.124), channel_id=1, source_target_pairs={{0,16},{4,20},{8,24},{12,28},{16,0},{20,4},{24,8},{28,12},{1,17},{... | collective-permute-start | bytes 393224 | tf_op jit(solution)/shard_map/ppermute | solution.py:494
  28.6 0.9 %collective-permute-start.9 = (bf16[256,256]{1,0:T(8,128)(2,1)S(1)}, bf16[256,256]{1,0:T(8,128)(2,1)S(1)}, u32[]{:S(2)}, u32[]{:S(2)}) collective-permute-start(bf16[256,256]{1,0:T(8,128)(2,1)S(1)} %get-tuple-element.125), channel_id=1, source_target_pairs={{0,24},{4,28},{8,16},{12,20},{16,8},{20,12},{24,0},{28,4},{1,25},{... | collective-permute-start | bytes 393224 | tf_op jit(solution)/shard_map/ppermute | solution.py:494
  29.5 1.8 %collective-permute-done.3.refs_3_ = bf16[2,2,128,256]{3,2,1,0:T(8,128)(2,1)S(1)} collective-permute-done((bf16[2,2,128,256]{3,2,1,0:T(8,128)(2,1)S(1)}, bf16[2,2,128,256]{3,2,1,0:T(8,128)(2,1)S(1)}, u32[]{:S(2)}, u32[]{:S(2)}) %collective-permute-start.3) | collective-permute-done | bytes 262176 | tf_op jit(solution)/shard_map/ppermute | solution.py:430
  31.3 0.0 collective-permute-done.5.refs_7_.refs_4_
  31.3 7.0 %ahead.1 = (bf16[2,256,256]{2,1,0:T(8,128)(2,1)S(1)}, bf16[2,256,256]{2,1,0:T(8,128)(2,1)S(1)}, bf16[8,2,256,256]{3,2,1,0:T(8,128)(2,1)S(1)}, bf16[8,2,256,256]{3,2,1,0:T(8,128)(2,1)S(1)}, f32[256,256]{1,0:T(8,128)S(1)}) custom-call(s32[8,128]{1,0:T(8,128)S(1)} %get-tuple-element.105.plan, bf16[2,2,128,256]{3,2,1,0:T(8,128)(2,1)S(1)} %get-tuple-element.111.refs_0_, ...), custom_call_target="tpu_custom_call" | custom-call | flops 100000000 | bytes 300000 | tf_op jit(solution)/shard_map/ahead/pallas_call | solution.py:116
  38.3 0.0 collective-permute-done.7.refs_7_
  38.4 0.5 collective-permute-done.8.refs_8_
  38.9 0.0 collective-permute-done.9.refs_9_
  38.9 4.2 %back.1 = (bf16[2,128,256]{2,1,0:T(8,128)(2,1)S(1)}, bf16[2,128,256]{2,1,0:T(8,128)(2,1)S(1)}, bf16[8,2,256,256]{3,2,1,0:T(8,128)(2,1)S(1)}) custom-call(s32[8,128]{1,0:T(8,128)S(1)} %get-tuple-element.105.plan, f32[256,256]{1,0:T(8,128)S(1)} %get-tuple-element.116.refs_0_, bf16[8,2,256,256]{3,2,1,0:T(8,128)(2,1)S(1)} %get-tuple-element.117.refs_1_, ...), custom_call_target="tpu_custom_call" | custom-call | flops 100000000 | bytes 300000 | tf_op jit(solution)/shard_map/back/pallas_call | solution.py:116
  43.1 0.1 collective-permute-start.10
  43.2 1.4 %collective-permute-start.11 = (bf16[2,128,256]{2,1,0:T(8,128)(2,1)S(1)}, bf16[2,128,256]{2,1,0:T(8,128)(2,1)S(1)}, u32[]{:S(2)}, u32[]{:S(2)}) collective-permute-start(bf16[2,128,256]{2,1,0:T(8,128)(2,1)S(1)} %get-tuple-element.158.refs_0_), channel_id=1, source_target_pairs={{0,2},{1,3},{2,0},{3,1},{4,6},{5,7},{6,4},{7,5},{8,10},{9,11},{10,... | collective-permute-start | bytes 393224 | tf_op jit(solution)/shard_map/ppermute | solution.py:430
  44.6 0.5 collective-permute-start.12
  45.0 4.7 %last.1 = (bf16[2,128,256]{2,1,0:T(8,128)(2,1)S(1)}, bf16[2,128,256]{2,1,0:T(8,128)(2,1)S(1)}, bf16[2,2,128,256]{3,2,1,0:T(8,128)(2,1)S(1)}, bf16[2,2,256,256]{3...) custom-call(s32[8,128]{1,0:T(8,128)S(1)} %get-tuple-element.105.plan, ...), custom_call_target="tpu_custom_call" | custom-call | flops 100000000 | bytes 300000 | tf_op jit(solution)/shard_map/last/pallas_call | solution.py:116
  49.8 1.7 %collective-permute-done.12.refs_3_ = bf16[2,128,256]{2,1,0:T(8,128)(2,1)S(1)} collective-permute-done((bf16[2,128,256]{2,1,0:T(8,128)(2,1)S(1)}, bf16[2,128,256]{2,1,0:T(8,128)(2,1)S(1)}, u32[]{:S(2)}, u32[]{:S(2)}) %collective-permute-start.12) | collective-permute-done | bytes 131104 | tf_op jit(solution)/shard_map/ppermute | solution.py:430
  51.4 0.3 collective-permute-start.22
  51.7 1.0 %collective-permute-start.14 = (bf16[2,2,128,256]{3,2,1,0:T(8,128)(2,1)S(1)}, bf16[2,2,128,256]{3,2,1,0:T(8,128)(2,1)S(1)}, u32[]{:S(2)}, u32[]{:S(2)}) collective-permute-start(bf16[2,2,128,256]{3,2,1,0:T(8,128)(2,1)S(1)} %get-tuple-element.136), channel_id=1, source_target_pairs={{0,2},{1,3},{2,0},{3,1},{4,6},{5,7},{6,4},{7,5},{8,10},{9,11},{10,... | collective-permute-start | bytes 786440 | tf_op jit(solution)/shard_map/ppermute | solution.py:430
  52.7 1.4 %collective-permute-done.22.came = bf16[2,2,2,256,256]{4,3,2,1,0:T(8,128)(2,1)S(1)} collective-permute-done((bf16[2,2,2,256,256]{4,3,2,1,0:T(8,128)(2,1)S(1)}, bf16[2,2,2,256,256]{4,3,2,1,0:T(8,128)(2,1)S(1)}, u32[]{:S(2)}, u32[]{:S(2)}) %collective-permute-start.22) | collective-permute-done | bytes 1048608 | tf_op jit(solution)/shard_map/ppermute | solution.py:430
  54.1 0.8 spread.1
  54.9 1.5 %collective-permute-start.23 = (bf16[2,4,2,2,32,256]{5,4,3,2,1,0:T(8,128)(2,1)S(1)}, bf16[2,4,2,2,32,256]{5,4,3,2,1,0:T(8,128)(2,1)S(1)}, u32[]{:S(2)}, u32[]{:S(2)}) collective-permute-start(bf16[2,4,2,2,32,256]{5,4,3,2,1,0:T(8,128)(2,1)S(1)} %get-tuple-element.169), channel_id=1, source_target_pairs={{0,4},{4,0},{8,12},{12,8},{16,20},{20,16},{24,28},{28,24},{1,5},{5... | collective-permute-start | bytes 1572872 | tf_op jit(solution)/shard_map/ppermute | solution.py:567
  56.5 1.1 %place.2 = (bf16[2,2,128,256]{3,2,1,0:T(8,128)(2,1)S(1)}, f32[2,2,128,256]{3,2,1,0:T(8,128)S(1)}, bf16[2,2,128,256]{3,2,1,0:T(8,128)(2,1)S(1)}) custom-call(s32[8,128]{1,0:T(8,128)S(1)} %get-tuple-element.105.plan, bf16[2,128,256]{2,1,0:T(8,128)(2,1)S(1)} %get-tuple-element.158.refs_0_, bf16[2,128,256]{2,1,0:T(8,128)(2,1)S(1)} %collective-permute-done.10.refs_1_, ...), custom_call_target="tpu_custom_call" | custom-call | flops 100000000 | bytes 300000 | tf_op jit(solution)/shard_map/place/pallas_call | solution.py:116
  57.5 2.9 %collective-permute-start.16 = (bf16[2,2,128,256]{3,2,1,0:T(8,128)(2,1)S(1)}, bf16[2,2,128,256]{3,2,1,0:T(8,128)(2,1)S(1)}, u32[]{:S(2)}, u32[]{:S(2)}) collective-permute-start(bf16[2,2,128,256]{3,2,1,0:T(8,128)(2,1)S(1)} %get-tuple-element.141), channel_id=1, source_target_pairs={{0,8},{4,12},{8,0},{12,4},{16,24},{20,28},{24,16},{28,20},{1,9},{5... | collective-permute-start | bytes 786440 | tf_op jit(solution)/shard_map/ppermute | solution.py:598
  60.4 0.0 collective-permute-done.14.refs_2_
  60.4 0.0 collective-permute-start.15
  60.4 0.5 collective-permute-start.13
  60.9 0.7 collective-permute-start.19
  61.6 0.5 collective-permute-done.13.refs_1_
  62.1 4.7 %collective-permute-done.16.low = bf16[2,2,128,256]{3,2,1,0:T(8,128)(2,1)S(1)} collective-permute-done((bf16[2,2,128,256]{3,2,1,0:T(8,128)(2,1)S(1)}, bf16[2,2,128,256]{3,2,1,0:T(8,128)(2,1)S(1)}, u32[]{:S(2)}, u32[]{:S(2)}) %collective-permute-start.16) | collective-permute-done | bytes 262176 | tf_op jit(solution)/shard_map/ppermute | solution.py:598
  66.9 1.1 %place.3 = (bf16[2,2,128,256]{3,2,1,0:T(8,128)(2,1)S(1)}, f32[2,2,128,256]{3,2,1,0:T(8,128)S(1)}, bf16[2,2,128,256]{3,2,1,0:T(8,128)(2,1)S(1)}) custom-call(s32[8,128]{1,0:T(8,128)S(1)} %get-tuple-element.105.plan, bf16[2,128,256]{2,1,0:T(8,128)(2,1)S(1)} %get-tuple-element.157.refs_0_, bf16[2,128,256]{2,1,0:T(8,128)(2,1)S(1)} %collective-permute-done.13.refs_1_, ...), custom_call_target="tpu_custom_call" | custom-call | flops 100000000 | bytes 300000 | tf_op jit(solution)/shard_map/place/pallas_call | solution.py:116
  68.0 1.8 %collective-permute-start.17 = (bf16[2,2,128,256]{3,2,1,0:T(8,128)(2,1)S(1)}, bf16[2,2,128,256]{3,2,1,0:T(8,128)(2,1)S(1)}, u32[]{:S(2)}, u32[]{:S(2)}) collective-permute-start(bf16[2,2,128,256]{3,2,1,0:T(8,128)(2,1)S(1)} %get-tuple-element.147), channel_id=1, source_target_pairs={{0,8},{4,12},{8,0},{12,4},{16,24},{20,28},{24,16},{28,20},{1,9},{5... | collective-permute-start | bytes 786440 | tf_op jit(solution)/shard_map/ppermute | solution.py:598
  69.8 0.7 collective-permute-start.18
  70.5 0.1 fold.1
  70.6 1.0 %collective-permute-start.24 = (bf16[4,2,2,32,256]{4,3,2,1,0:T(8,128)(2,1)S(1)}, bf16[4,2,2,32,256]{4,3,2,1,0:T(8,128)(2,1)S(1)}, u32[]{:S(2)}, u32[]{:S(2)}) collective-permute-start(bf16[4,2,2,32,256]{4,3,2,1,0:T(8,128)(2,1)S(1)} %get-tuple-element.171), channel_id=1, source_target_pairs={{0,2},{1,3},{2,0},{3,1},{4,6},{5,7},{6,4},{7,5},{8,10},{9,11},{10,... | collective-permute-start | bytes 786440 | tf_op jit(solution)/shard_map/ppermute | solution.py:430
  71.5 0.7 split.3
  72.2 0.5 collective-permute-start.21
  72.7 3.0 %collective-permute-done.17.low = bf16[2,2,128,256]{3,2,1,0:T(8,128)(2,1)S(1)} collective-permute-done((bf16[2,2,128,256]{3,2,1,0:T(8,128)(2,1)S(1)}, bf16[2,2,128,256]{3,2,1,0:T(8,128)(2,1)S(1)}, u32[]{:S(2)}, u32[]{:S(2)}) %collective-permute-start.17) | collective-permute-done | bytes 262176 | tf_op jit(solution)/shard_map/ppermute | solution.py:598
  75.7 0.0 collective-permute-done.18.high
  75.7 0.7 split.2
  76.4 0.6 collective-permute-start.20
  77.0 0.7 collective-permute-done.24.came
  77.8 3.8 %collective-permute-start.25 = (bf16[2,2,32,256]{3,2,1,0:T(8,128)(2,1)S(1)}, bf16[2,2,32,256]{3,2,1,0:T(8,128)(2,1)S(1)}, u32[]{:S(2)}, u32[]{:S(2)}) collective-permute-start(bf16[2,2,32,256]{3,2,1,0:T(8,128)(2,1)S(1)} %get-tuple-element.173), channel_id=1, source_target_pairs={{0,8},{4,12},{8,0},{12,4},{16,24},{20,28},{24,16},{28,20},{1,9},{5... | collective-permute-start | bytes 196616 | tf_op jit(solution)/shard_map/ppermute | solution.py:580
  81.5 1.1 %collective-permute-start.26 = (bf16[2,2,32,256]{3,2,1,0:T(8,128)(2,1)S(1)}, bf16[2,2,32,256]{3,2,1,0:T(8,128)(2,1)S(1)}, u32[]{:S(2)}, u32[]{:S(2)}) collective-permute-start(bf16[2,2,32,256]{3,2,1,0:T(8,128)(2,1)S(1)} %get-tuple-element.174), channel_id=1, source_target_pairs={{0,16},{4,20},{8,24},{12,28},{16,0},{20,4},{24,8},{28,12},{1,17},{... | collective-permute-start | bytes 196616 | tf_op jit(solution)/shard_map/ppermute | solution.py:580
  82.6 1.4 %collective-permute-start.27 = (bf16[2,2,32,256]{3,2,1,0:T(8,128)(2,1)S(1)}, bf16[2,2,32,256]{3,2,1,0:T(8,128)(2,1)S(1)}, u32[]{:S(2)}, u32[]{:S(2)}) collective-permute-start(bf16[2,2,32,256]{3,2,1,0:T(8,128)(2,1)S(1)} %get-tuple-element.175), channel_id=1, source_target_pairs={{0,24},{4,28},{8,16},{12,20},{16,8},{20,12},{24,0},{28,4},{1,25},{... | collective-permute-start | bytes 196616 | tf_op jit(solution)/shard_map/ppermute | solution.py:580
  84.0 0.6 slice.27
  85.3 0.0 collective-permute-done.21.refs_3_
  85.3 0.9 end.1
  86.2 1.7 %collective-permute-done.26.refs_2_ = bf16[2,2,32,256]{3,2,1,0:T(8,128)(2,1)S(1)} collective-permute-done((bf16[2,2,32,256]{3,2,1,0:T(8,128)(2,1)S(1)}, bf16[2,2,32,256]{3,2,1,0:T(8,128)(2,1)S(1)}, u32[]{:S(2)}, u32[]{:S(2)}) %collective-permute-start.26) | collective-permute-done | bytes 65568 | tf_op jit(solution)/shard_map/ppermute | solution.py:580
  87.8 0.9 %collective-permute-done.27.refs_3_ = bf16[2,2,32,256]{3,2,1,0:T(8,128)(2,1)S(1)} collective-permute-done((bf16[2,2,32,256]{3,2,1,0:T(8,128)(2,1)S(1)}, bf16[2,2,32,256]{3,2,1,0:T(8,128)(2,1)S(1)}, u32[]{:S(2)}, u32[]{:S(2)}) %collective-permute-start.27) | collective-permute-done | bytes 65568 | tf_op jit(solution)/shard_map/ppermute | solution.py:580
  88.7 0.7 total.1
  (25 shorter events, 0.2 us)
Async XLA Ops:
  0.6 5.2 %copy-start.4 = (bf16[8,256,256]{2,1,0:T(8,128)(2,1)S(1)}, bf16[8,256,256]{2,1,0:T(8,128)(2,1)}, u32[]{:S(2)}) copy-start(bf16[8,256,256]{2,1,0:T(8,128)(2,1)} %amplitudes_far.1) | copy-start | bytes 3145732
  2.0 15.0 %collective-permute-start = (bf16[2,2,256,256]{3,2,1,0:T(8,128)(2,1)S(1)}, bf16[2,2,256,256]{3,2,1,0:T(8,128)(2,1)S(1)}, u32[]{:S(2)}, u32[]{:S(2)}) collective-permute-start(bf16[2,2,256,256]{3,2,1,0:T(8,128)(2,1)S(1)} %convert_element_type.42), channel_id=1, source_target_pairs={{0,2},{1,3},{2,0},{3,1},{4,6},{5,7},{6,4},{7,5},{8,10},{9,11},{10,... | collective-permute-start | bytes 1572872 | tf_op jit(solution)/shard_map/ppermute | solution.py:430
  5.8 1.6 %copy-start.2 = (bf16[2,2,128,2048]{3,2,1,0:T(8,128)(2,1)S(1)}, bf16[2,2,128,2048]{3,2,1,0:T(8,128)(2,1)}, u32[]{:S(2)}) copy-start(bf16[2,2,128,2048]{3,2,1,0:T(8,128)(2,1)} %strip_far.1) | copy-start | bytes 6291460
  7.4 0.7 copy-start.6
  8.1 23.3 %copy-start = (f32[2,2,256,256]{3,2,1,0:T(8,128)S(1)}, f32[2,2,256,256]{3,2,1,0:T(8,128)}, u32[]{:S(2)}) copy-start(f32[2,2,256,256]{3,2,1,0:T(8,128)} %refs_1_.1) | copy-start | bytes 3145732
  8.1 23.3 %copy-start.1 = (bf16[4,256,256]{2,1,0:T(8,128)(2,1)S(1)}, bf16[4,256,256]{2,1,0:T(8,128)(2,1)}, u32[]{:S(2)}) copy-start(bf16[4,256,256]{2,1,0:T(8,128)(2,1)} %constant.181.clone.refs_8_.refs_4_.refs_6_) | copy-start | bytes 1572868
  8.1 23.3 %copy-start.3 = (f32[2,256,256]{2,1,0:T(8,128)S(1)}, f32[2,256,256]{2,1,0:T(8,128)}, u32[]{:S(2)}) copy-start(f32[2,256,256]{2,1,0:T(8,128)} %constant.182.clone.refs_9_.refs_7_) | copy-start | bytes 1572868
  10.2 13.4 %collective-permute-start.6 = (bf16[4,256,256]{2,1,0:T(8,128)(2,1)S(1)}, bf16[4,256,256]{2,1,0:T(8,128)(2,1)S(1)}, u32[]{:S(2)}, u32[]{:S(2)}) collective-permute-start(bf16[4,256,256]{2,1,0:T(8,128)(2,1)S(1)} %get-tuple-element.121), channel_id=1, source_target_pairs={{0,4},{4,0},{8,12},{12,8},{16,20},{20,16},{24,28},{28,24},{1,5},{5... | collective-permute-start | bytes 1572872 | tf_op jit(solution)/shard_map/ppermute | solution.py:488
  11.7 12.6 %collective-permute-start.4 = (bf16[2,2,256,256]{3,2,1,0:T(8,128)(2,1)S(1)}, bf16[2,2,256,256]{3,2,1,0:T(8,128)(2,1)S(1)}, u32[]{:S(2)}, u32[]{:S(2)}) collective-permute-start(bf16[2,2,256,256]{3,2,1,0:T(8,128)(2,1)S(1)} %convert_element_type.42), channel_id=1, source_target_pairs={{0,1},{1,0},{2,3},{3,2},{4,5},{5,4},{6,7},{7,6},{8,9},{9,8},{10,11... | collective-permute-start | bytes 1572872 | tf_op jit(solution)/shard_map/ppermute | solution.py:430
  17.0 14.3 %collective-permute-start.5 = (bf16[2,2,256,256]{3,2,1,0:T(8,128)(2,1)S(1)}, bf16[2,2,256,256]{3,2,1,0:T(8,128)(2,1)S(1)}, u32[]{:S(2)}, u32[]{:S(2)}) collective-permute-start(bf16[2,2,256,256]{3,2,1,0:T(8,128)(2,1)S(1)} %collective-permute-done.refs_6_.refs_3_), channel_id=1, source_target_pairs={{0,1},{1,0},{2,3},{3,2},{4,5},{5,4},{6,7},{7,6},{8,9},{9,8},{10,11... | collective-permute-start | bytes 1572872 | tf_op jit(solution)/shard_map/ppermute | solution.py:430
  17.0 9.0 %collective-permute-start.1 = (bf16[2,2,128,256]{3,2,1,0:T(8,128)(2,1)S(1)}, bf16[2,2,128,256]{3,2,1,0:T(8,128)(2,1)S(1)}, u32[]{:S(2)}, u32[]{:S(2)}) collective-permute-start(bf16[2,2,128,256]{3,2,1,0:T(8,128)(2,1)S(1)} %get-tuple-element.112), channel_id=1, source_target_pairs={{0,1},{1,0},{2,3},{3,2},{4,5},{5,4},{6,7},{7,6},{8,9},{9,8},{10,11... | collective-permute-start | bytes 786440 | tf_op jit(solution)/shard_map/ppermute | solution.py:430
  17.5 11.1 %collective-permute-start.2 = (bf16[2,2,128,256]{3,2,1,0:T(8,128)(2,1)S(1)}, bf16[2,2,128,256]{3,2,1,0:T(8,128)(2,1)S(1)}, u32[]{:S(2)}, u32[]{:S(2)}) collective-permute-start(bf16[2,2,128,256]{3,2,1,0:T(8,128)(2,1)S(1)} %get-tuple-element.113), channel_id=1, source_target_pairs={{0,2},{1,3},{2,0},{3,1},{4,6},{5,7},{6,4},{7,5},{8,10},{9,11},{10,... | collective-permute-start | bytes 786440 | tf_op jit(solution)/shard_map/ppermute | solution.py:430
  23.6 7.7 %collective-permute-start.3 = (bf16[2,2,128,256]{3,2,1,0:T(8,128)(2,1)S(1)}, bf16[2,2,128,256]{3,2,1,0:T(8,128)(2,1)S(1)}, u32[]{:S(2)}, u32[]{:S(2)}) collective-permute-start(bf16[2,2,128,256]{3,2,1,0:T(8,128)(2,1)S(1)} %get-tuple-element.114), channel_id=1, source_target_pairs={{0,3},{1,2},{2,1},{3,0},{4,7},{5,6},{6,5},{7,4},{8,11},{9,10},{10,... | collective-permute-start | bytes 786440 | tf_op jit(solution)/shard_map/ppermute | solution.py:430
  24.3 14.0 %collective-permute-start.7 = (bf16[256,256]{1,0:T(8,128)(2,1)S(1)}, bf16[256,256]{1,0:T(8,128)(2,1)S(1)}, u32[]{:S(2)}, u32[]{:S(2)}) collective-permute-start(bf16[256,256]{1,0:T(8,128)(2,1)S(1)} %get-tuple-element.123), channel_id=1, source_target_pairs={{0,8},{4,12},{8,0},{12,4},{16,24},{20,28},{24,16},{28,20},{1,9},{5... | collective-permute-start | bytes 393224 | tf_op jit(solution)/shard_map/ppermute | solution.py:494
  26.0 12.9 %collective-permute-start.8 = (bf16[256,256]{1,0:T(8,128)(2,1)S(1)}, bf16[256,256]{1,0:T(8,128)(2,1)S(1)}, u32[]{:S(2)}, u32[]{:S(2)}) collective-permute-start(bf16[256,256]{1,0:T(8,128)(2,1)S(1)} %get-tuple-element.124), channel_id=1, source_target_pairs={{0,16},{4,20},{8,24},{12,28},{16,0},{20,4},{24,8},{28,12},{1,17},{... | collective-permute-start | bytes 393224 | tf_op jit(solution)/shard_map/ppermute | solution.py:494
  28.6 10.3 %copy-start.5 = (bf16[2,256,256]{2,1,0:T(8,128)(2,1)S(1)}, bf16[2,256,256]{2,1,0:T(8,128)(2,1)}, u32[]{:S(2)}) copy-start(bf16[2,256,256]{2,1,0:T(8,128)(2,1)} %constant.183.clone.refs_5_) | copy-start | bytes 786436
  28.6 10.3 %collective-permute-start.9 = (bf16[256,256]{1,0:T(8,128)(2,1)S(1)}, bf16[256,256]{1,0:T(8,128)(2,1)S(1)}, u32[]{:S(2)}, u32[]{:S(2)}) collective-permute-start(bf16[256,256]{1,0:T(8,128)(2,1)S(1)} %get-tuple-element.125), channel_id=1, source_target_pairs={{0,24},{4,28},{8,16},{12,20},{16,8},{20,12},{24,0},{28,4},{1,25},{... | collective-permute-start | bytes 393224 | tf_op jit(solution)/shard_map/ppermute | solution.py:494
  43.1 6.7 %collective-permute-start.10 = (bf16[2,128,256]{2,1,0:T(8,128)(2,1)S(1)}, bf16[2,128,256]{2,1,0:T(8,128)(2,1)S(1)}, u32[]{:S(2)}, u32[]{:S(2)}) collective-permute-start(bf16[2,128,256]{2,1,0:T(8,128)(2,1)S(1)} %get-tuple-element.127), channel_id=1, source_target_pairs={{0,1},{1,0},{2,3},{3,2},{4,5},{5,4},{6,7},{7,6},{8,9},{9,8},{10,11... | collective-permute-start | bytes 393224 | tf_op jit(solution)/shard_map/ppermute | solution.py:430
  43.2 6.6 %collective-permute-start.11 = (bf16[2,128,256]{2,1,0:T(8,128)(2,1)S(1)}, bf16[2,128,256]{2,1,0:T(8,128)(2,1)S(1)}, u32[]{:S(2)}, u32[]{:S(2)}) collective-permute-start(bf16[2,128,256]{2,1,0:T(8,128)(2,1)S(1)} %get-tuple-element.158.refs_0_), channel_id=1, source_target_pairs={{0,2},{1,3},{2,0},{3,1},{4,6},{5,7},{6,4},{7,5},{8,10},{9,11},{10,... | collective-permute-start | bytes 393224 | tf_op jit(solution)/shard_map/ppermute | solution.py:430
  44.6 6.9 %collective-permute-start.12 = (bf16[2,128,256]{2,1,0:T(8,128)(2,1)S(1)}, bf16[2,128,256]{2,1,0:T(8,128)(2,1)S(1)}, u32[]{:S(2)}, u32[]{:S(2)}) collective-permute-start(bf16[2,128,256]{2,1,0:T(8,128)(2,1)S(1)} %get-tuple-element.127), channel_id=1, source_target_pairs={{0,3},{1,2},{2,1},{3,0},{4,7},{5,6},{6,5},{7,4},{8,11},{9,10},{10,... | collective-permute-start | bytes 393224 | tf_op jit(solution)/shard_map/ppermute | solution.py:430
  51.4 2.7 %collective-permute-start.22 = (bf16[2,2,2,256,256]{4,3,2,1,0:T(8,128)(2,1)S(1)}, bf16[2,2,2,256,256]{4,3,2,1,0:T(8,128)(2,1)S(1)}, u32[]{:S(2)}, u32[]{:S(2)}) collective-permute-start(bf16[2,2,2,256,256]{4,3,2,1,0:T(8,128)(2,1)S(1)} %get-tuple-element.167), channel_id=1, source_target_pairs={{0,1},{1,0},{2,3},{3,2},{4,5},{5,4},{6,7},{7,6},{8,9},{9,8},{10,11... | collective-permute-start | bytes 3145736 | tf_op jit(solution)/shard_map/ppermute | solution.py:430
  51.7 8.7 %collective-permute-start.14 = (bf16[2,2,128,256]{3,2,1,0:T(8,128)(2,1)S(1)}, bf16[2,2,128,256]{3,2,1,0:T(8,128)(2,1)S(1)}, u32[]{:S(2)}, u32[]{:S(2)}) collective-permute-start(bf16[2,2,128,256]{3,2,1,0:T(8,128)(2,1)S(1)} %get-tuple-element.136), channel_id=1, source_target_pairs={{0,2},{1,3},{2,0},{3,1},{4,6},{5,7},{6,4},{7,5},{8,10},{9,11},{10,... | collective-permute-start | bytes 786440 | tf_op jit(solution)/shard_map/ppermute | solution.py:430
  54.9 15.5 %collective-permute-start.23 = (bf16[2,4,2,2,32,256]{5,4,3,2,1,0:T(8,128)(2,1)S(1)}, bf16[2,4,2,2,32,256]{5,4,3,2,1,0:T(8,128)(2,1)S(1)}, u32[]{:S(2)}, u32[]{:S(2)}) collective-permute-start(bf16[2,4,2,2,32,256]{5,4,3,2,1,0:T(8,128)(2,1)S(1)} %get-tuple-element.169), channel_id=1, source_target_pairs={{0,4},{4,0},{8,12},{12,8},{16,20},{20,16},{24,28},{28,24},{1,5},{5... | collective-permute-start | bytes 1572872 | tf_op jit(solution)/shard_map/ppermute | solution.py:567
  57.5 9.3 %collective-permute-start.16 = (bf16[2,2,128,256]{3,2,1,0:T(8,128)(2,1)S(1)}, bf16[2,2,128,256]{3,2,1,0:T(8,128)(2,1)S(1)}, u32[]{:S(2)}, u32[]{:S(2)}) collective-permute-start(bf16[2,2,128,256]{3,2,1,0:T(8,128)(2,1)S(1)} %get-tuple-element.141), channel_id=1, source_target_pairs={{0,8},{4,12},{8,0},{12,4},{16,24},{20,28},{24,16},{28,20},{1,9},{5... | collective-permute-start | bytes 786440 | tf_op jit(solution)/shard_map/ppermute | solution.py:598
  60.4 6.5 %collective-permute-start.15 = (bf16[2,2,128,256]{3,2,1,0:T(8,128)(2,1)S(1)}, bf16[2,2,128,256]{3,2,1,0:T(8,128)(2,1)S(1)}, u32[]{:S(2)}, u32[]{:S(2)}) collective-permute-start(bf16[2,2,128,256]{3,2,1,0:T(8,128)(2,1)S(1)} %collective-permute-done.14.refs_2_), channel_id=1, source_target_pairs={{0,1},{1,0},{2,3},{3,2},{4,5},{5,4},{6,7},{7,6},{8,9},{9,8},{10,11... | collective-permute-start | bytes 786440 | tf_op jit(solution)/shard_map/ppermute | solution.py:430
  60.4 1.7 %collective-permute-start.13 = (bf16[2,128,256]{2,1,0:T(8,128)(2,1)S(1)}, bf16[2,128,256]{2,1,0:T(8,128)(2,1)S(1)}, u32[]{:S(2)}, u32[]{:S(2)}) collective-permute-start(bf16[2,128,256]{2,1,0:T(8,128)(2,1)S(1)} %get-tuple-element.135), channel_id=1, source_target_pairs={{0,1},{1,0},{2,3},{3,2},{4,5},{5,4},{6,7},{7,6},{8,9},{9,8},{10,11... | collective-permute-start | bytes 393224 | tf_op jit(solution)/shard_map/ppermute | solution.py:430
  60.9 10.6 %collective-permute-start.19 = (bf16[2,2,128,256]{3,2,1,0:T(8,128)(2,1)S(1)}, bf16[2,2,128,256]{3,2,1,0:T(8,128)(2,1)S(1)}, u32[]{:S(2)}, u32[]{:S(2)}) collective-permute-start(bf16[2,2,128,256]{3,2,1,0:T(8,128)(2,1)S(1)} %get-tuple-element.153), channel_id=1, source_target_pairs={{8,16},{12,20},{16,8},{20,12},{9,17},{13,21},{17,9},{21,13},{10,18... | collective-permute-start | bytes 786440 | tf_op jit(solution)/shard_map/ppermute | solution.py:600
  68.0 7.7 %collective-permute-start.17 = (bf16[2,2,128,256]{3,2,1,0:T(8,128)(2,1)S(1)}, bf16[2,2,128,256]{3,2,1,0:T(8,128)(2,1)S(1)}, u32[]{:S(2)}, u32[]{:S(2)}) collective-permute-start(bf16[2,2,128,256]{3,2,1,0:T(8,128)(2,1)S(1)} %get-tuple-element.147), channel_id=1, source_target_pairs={{0,8},{4,12},{8,0},{12,4},{16,24},{20,28},{24,16},{28,20},{1,9},{5... | collective-permute-start | bytes 786440 | tf_op jit(solution)/shard_map/ppermute | solution.py:598
  69.8 5.9 %collective-permute-start.18 = (bf16[2,2,128,256]{3,2,1,0:T(8,128)(2,1)S(1)}, bf16[2,2,128,256]{3,2,1,0:T(8,128)(2,1)S(1)}, u32[]{:S(2)}, u32[]{:S(2)}) collective-permute-start(bf16[2,2,128,256]{3,2,1,0:T(8,128)(2,1)S(1)} %get-tuple-element.149), channel_id=1, source_target_pairs={{8,16},{12,20},{16,8},{20,12},{9,17},{13,21},{17,9},{21,13},{10,18... | collective-permute-start | bytes 786440 | tf_op jit(solution)/shard_map/ppermute | solution.py:600
  70.6 7.1 %collective-permute-start.24 = (bf16[4,2,2,32,256]{4,3,2,1,0:T(8,128)(2,1)S(1)}, bf16[4,2,2,32,256]{4,3,2,1,0:T(8,128)(2,1)S(1)}, u32[]{:S(2)}, u32[]{:S(2)}) collective-permute-start(bf16[4,2,2,32,256]{4,3,2,1,0:T(8,128)(2,1)S(1)} %get-tuple-element.171), channel_id=1, source_target_pairs={{0,2},{1,3},{2,0},{3,1},{4,6},{5,7},{6,4},{7,5},{8,10},{9,11},{10,... | collective-permute-start | bytes 786440 | tf_op jit(solution)/shard_map/ppermute | solution.py:430
  72.2 13.1 %collective-permute-start.21 = (bf16[2,128,256]{2,1,0:T(8,128)(2,1)S(1)}, bf16[2,128,256]{2,1,0:T(8,128)(2,1)S(1)}, u32[]{:S(2)}, u32[]{:S(2)}) collective-permute-start(bf16[2,128,256]{2,1,0:T(8,128)(2,1)S(1)} %get-tuple-element.156), channel_id=1, source_target_pairs={{0,4},{4,0},{8,12},{12,8},{16,20},{20,16},{24,28},{28,24},{1,5},{5... | collective-permute-start | bytes 393224 | tf_op jit(solution)/shard_map/ppermute | solution.py:612
  76.4 8.9 %collective-permute-start.20 = (bf16[2,128,256]{2,1,0:T(8,128)(2,1)S(1)}, bf16[2,128,256]{2,1,0:T(8,128)(2,1)S(1)}, u32[]{:S(2)}, u32[]{:S(2)}) collective-permute-start(bf16[2,128,256]{2,1,0:T(8,128)(2,1)S(1)} %get-tuple-element.155), channel_id=1, source_target_pairs={{0,4},{4,0},{8,12},{12,8},{16,20},{20,16},{24,28},{28,24},{1,5},{5... | collective-permute-start | bytes 393224 | tf_op jit(solution)/shard_map/ppermute | solution.py:612
  77.8 8.4 %collective-permute-start.25 = (bf16[2,2,32,256]{3,2,1,0:T(8,128)(2,1)S(1)}, bf16[2,2,32,256]{3,2,1,0:T(8,128)(2,1)S(1)}, u32[]{:S(2)}, u32[]{:S(2)}) collective-permute-start(bf16[2,2,32,256]{3,2,1,0:T(8,128)(2,1)S(1)} %get-tuple-element.173), channel_id=1, source_target_pairs={{0,8},{4,12},{8,0},{12,4},{16,24},{20,28},{24,16},{28,20},{1,9},{5... | collective-permute-start | bytes 196616 | tf_op jit(solution)/shard_map/ppermute | solution.py:580
  81.5 6.3 %collective-permute-start.26 = (bf16[2,2,32,256]{3,2,1,0:T(8,128)(2,1)S(1)}, bf16[2,2,32,256]{3,2,1,0:T(8,128)(2,1)S(1)}, u32[]{:S(2)}, u32[]{:S(2)}) collective-permute-start(bf16[2,2,32,256]{3,2,1,0:T(8,128)(2,1)S(1)} %get-tuple-element.174), channel_id=1, source_target_pairs={{0,16},{4,20},{8,24},{12,28},{16,0},{20,4},{24,8},{28,12},{1,17},{... | collective-permute-start | bytes 196616 | tf_op jit(solution)/shard_map/ppermute | solution.py:580
  82.6 6.1 %collective-permute-start.27 = (bf16[2,2,32,256]{3,2,1,0:T(8,128)(2,1)S(1)}, bf16[2,2,32,256]{3,2,1,0:T(8,128)(2,1)S(1)}, u32[]{:S(2)}, u32[]{:S(2)}) collective-permute-start(bf16[2,2,32,256]{3,2,1,0:T(8,128)(2,1)S(1)} %get-tuple-element.175), channel_id=1, source_target_pairs={{0,24},{4,28},{8,16},{12,20},{16,8},{20,12},{24,0},{28,4},{1,25},{... | collective-permute-start | bytes 196616 | tf_op jit(solution)/shard_map/ppermute | solution.py:580

commit v3 on v2

--- a/solution.py
+++ b/solution.py
@@ -309,8 +309,8 @@
     measured = dot(dot(mover[0], amplitude[...]).astype(BF16), mover[1])
     ratio[...] = 1.0 - measured / jnp.sqrt(power[...] + 1.0)
     total[...] = jnp.zeros_like(total)
-    size = phi.shape[0] // 2
-    for start in (0, size):
+    size = phi.shape[0]
+    for start in (0,):
         fields = []
         for at in range(start, start + size):
             re, im = load_complex(far, at)
@@ -335,8 +335,8 @@
     total[...] = jnp.zeros_like(total)
     for copy in copies:
         copy.wait()
-    for start in range(0, tiles, 2):
-        which = [(turn, mode) for turn in range(start, start + 2) for mode in range(modes)]
+    for start in range(0, tiles, tiles):
+        which = [(turn, mode) for turn in range(start, start + tiles) for mode in range(modes)]
         fields = forward_folded([(inner[t * modes + m, 0], inner[t * modes + m, 1]) for t, m in which], tables)
         fields = inverse([conj_times(kernel[0], kernel[1], re, im) for re, im in fields], tables)
         for (turn, mode), (re, im) in zip(which, fields):
@@ -598,8 +598,6 @@
         low_in = lax.ppermute(even, "pos", pairs)
         pairs = [(i, i + 2 if i // 2 % 2 else i - 2) for i in range(2, groups - 2)]
         high_in = lax.ppermute(odd, "pos", pairs)
-        if layer == 0:
-            pieces, low_in = lax.optimization_barrier((pieces, low_in))
         if layer:
             pieces[0], low_in = lax.optimization_barrier((pieces[0], low_in))
         keeps[layer], send = call(

time: 89.6 us -> 89.5 us (level)
  no operation moved by 1% of the time
where the time goes in v3:
time: 89.5 us; the launch traced here: 89.3 us
  starting transfers between devices  31.7 us (35%)
  waiting for transfers between devices  26.6 us (30%)
  Pallas kernels  24.5 us (27%)
  local copies, waits for them, and re-layouts  3.63 us (4%)
  between operations  1.52 us (2%)
  other arithmetic  1.37 us (2%)
    pallas_call x14, Pallas kernels, call(): pl.pallas_call(body, out_shape=[pltpu.VMEM(shape, dtype) if at in keep el...  24.5 us
    ppermute x14, waiting for transfers between devices, turned(): return lax.ppermute(value, 'tile', [(i, i ^ turn) for i in range(tiles)])  11.5 us
    ppermute x14, starting transfers between devices, turned(): return lax.ppermute(value, 'tile', [(i, i ^ turn) for i in range(tiles)])  9.88 us
    ppermute x2, waiting for transfers between devices, on_device_by_slot(): low_in = lax.ppermute(even, 'pos', pairs)  7.61 us
    ppermute x3, starting transfers between devices, on_device_by_slot(): lax.ppermute(send, 'pos', [(i, i ^ 2 * turn) for i in range(groups)])  6.26 us
    ppermute x3, starting transfers between devices, on_device_by_slot(): lax.ppermute(merged[turn], 'pos', [(i, i ^ 2 * turn) for i in range(group...  5.2 us
    ppermute x2, starting transfers between devices, on_device_by_slot(): low_in = lax.ppermute(even, 'pos', pairs)  4.66 us
    ppermute x1, waiting for transfers between devices, on_device_by_slot(): lax.ppermute(far, 'pos', aside)  4.38 us
  transfers between devices with their start and end apart: 28, of which 12 were waited for; matrix products, arithmetic and copies ran while one was open for 2% of the time, Pallas kernels for 22%

profile of v3, /device:TPU:0, one launch (start us, length us, event | category | flops | bytes accessed | tf_op | source)
XLA Modules:
  0.0 89.3 jit_solution(13258565967496319620)
XLA Ops:
  0.6 1.4 %convert_element_type.42 = bf16[2,2,256,256]{3,2,1,0:T(8,128)(2,1)S(1)} convert(f32[2,2,256,256]{3,2,1,0:T(8,128)} %refs_1_.1) | non-fusion elementwise | flops 262144 | bytes 1572864 | tf_op jit(solution)/shard_map/convert_element_type | solution.py:461
  2.0 3.0 %collective-permute-start = (bf16[2,2,256,256]{3,2,1,0:T(8,128)(2,1)S(1)}, bf16[2,2,256,256]{3,2,1,0:T(8,128)(2,1)S(1)}, u32[]{:S(2)}, u32[]{:S(2)}) collective-permute-start(bf16[2,2,256,256]{3,2,1,0:T(8,128)(2,1)S(1)} %convert_element_type.42), channel_id=1, source_target_pairs={{0,2},{1,3},{2,0},{3,1},{4,6},{5,7},{6,4},{7,5},{8,10},{9,11},{10,... | collective-permute-start | bytes 1572872 | tf_op jit(solution)/shard_map/ppermute | solution.py:430
  5.0 0.8 copy.11.offsets
  5.8 1.6 %copy-done.2 = bf16[2,2,128,2048]{3,2,1,0:T(8,128)(2,1)S(1)} copy-done((bf16[2,2,128,2048]{3,2,1,0:T(8,128)(2,1)S(1)}, bf16[2,2,128,2048]{3,2,1,0:T(8,128)(2,1)}, u32[]{:S(2)}) %copy-start.2) | copy-done | bytes 2097176
  7.4 0.7 copy-done.6
  8.1 2.1 %first.1 = (bf16[2,2,128,256]{3,2,1,0:T(8,128)(2,1)S(1)}, bf16[2,2,128,256]{3,2,1,0:T(8,128)(2,1)S(1)}, bf16[2,2,128,256]{3,2,1,0:T(8,128)(2,1)S(1)}, bf16[2,2,1...) custom-call(s32[8]{0:T(128)S(1)} %copy-done.6, ...), custom_call_target="tpu_custom_call" | custom-call | flops 100000000 | bytes 300000 | tf_op jit(solution)/shard_map/first/pallas_call | solution.py:116
  10.2 1.5 %collective-permute-start.6 = (bf16[4,256,256]{2,1,0:T(8,128)(2,1)S(1)}, bf16[4,256,256]{2,1,0:T(8,128)(2,1)S(1)}, u32[]{:S(2)}, u32[]{:S(2)}) collective-permute-start(bf16[4,256,256]{2,1,0:T(8,128)(2,1)S(1)} %get-tuple-element.112), channel_id=1, source_target_pairs={{0,4},{4,0},{8,12},{12,8},{16,20},{20,16},{24,28},{28,24},{1,5},{5... | collective-permute-start | bytes 1572872 | tf_op jit(solution)/shard_map/ppermute | solution.py:488
  11.7 0.0 collective-permute-start.4
  11.7 5.3 %collective-permute-done.refs_6_.refs_3_ = bf16[2,2,256,256]{3,2,1,0:T(8,128)(2,1)S(1)} collective-permute-done((bf16[2,2,256,256]{3,2,1,0:T(8,128)(2,1)S(1)}, bf16[2,2,256,256]{3,2,1,0:T(8,128)(2,1)S(1)}, u32[]{:S(2)}, u32[]{:S(2)}) %collective-permute-start) | collective-permute-done | bytes 524320 | tf_op jit(solution)/shard_map/ppermute | solution.py:430
  17.0 0.0 collective-permute-start.5
  17.0 0.5 collective-permute-start.1
  17.5 1.7 %collective-permute-start.2 = (bf16[2,2,128,256]{3,2,1,0:T(8,128)(2,1)S(1)}, bf16[2,2,128,256]{3,2,1,0:T(8,128)(2,1)S(1)}, u32[]{:S(2)}, u32[]{:S(2)}) collective-permute-start(bf16[2,2,128,256]{3,2,1,0:T(8,128)(2,1)S(1)} %get-tuple-element.104), channel_id=1, source_target_pairs={{0,2},{1,3},{2,0},{3,1},{4,6},{5,7},{6,4},{7,5},{8,10},{9,11},{10,... | collective-permute-start | bytes 786440 | tf_op jit(solution)/shard_map/ppermute | solution.py:430
  19.2 4.4 %collective-permute-done.6.came = bf16[4,256,256]{2,1,0:T(8,128)(2,1)S(1)} collective-permute-done((bf16[4,256,256]{2,1,0:T(8,128)(2,1)S(1)}, bf16[4,256,256]{2,1,0:T(8,128)(2,1)S(1)}, u32[]{:S(2)}, u32[]{:S(2)}) %collective-permute-start.6) | collective-permute-done | bytes 524320 | tf_op jit(solution)/shard_map/ppermute | solution.py:488
  23.6 0.7 merge.1
  24.3 1.7 %collective-permute-start.7 = (bf16[256,256]{1,0:T(8,128)(2,1)S(1)}, bf16[256,256]{1,0:T(8,128)(2,1)S(1)}, u32[]{:S(2)}, u32[]{:S(2)}) collective-permute-start(bf16[256,256]{1,0:T(8,128)(2,1)S(1)} %get-tuple-element.114), channel_id=1, source_target_pairs={{0,8},{4,12},{8,0},{12,4},{16,24},{20,28},{24,16},{28,20},{1,9},{5... | collective-permute-start | bytes 393224 | tf_op jit(solution)/shard_map/ppermute | solution.py:494
  26.0 0.0 collective-permute-done.1.refs_1_
  26.0 2.6 %collective-permute-start.8 = (bf16[256,256]{1,0:T(8,128)(2,1)S(1)}, bf16[256,256]{1,0:T(8,128)(2,1)S(1)}, u32[]{:S(2)}, u32[]{:S(2)}) collective-permute-start(bf16[256,256]{1,0:T(8,128)(2,1)S(1)} %get-tuple-element.115), channel_id=1, source_target_pairs={{0,16},{4,20},{8,24},{12,28},{16,0},{20,4},{24,8},{28,12},{1,17},{... | collective-permute-start | bytes 393224 | tf_op jit(solution)/shard_map/ppermute | solution.py:494
  28.6 0.9 %collective-permute-start.9 = (bf16[256,256]{1,0:T(8,128)(2,1)S(1)}, bf16[256,256]{1,0:T(8,128)(2,1)S(1)}, u32[]{:S(2)}, u32[]{:S(2)}) collective-permute-start(bf16[256,256]{1,0:T(8,128)(2,1)S(1)} %get-tuple-element.116), channel_id=1, source_target_pairs={{0,24},{4,28},{8,16},{12,20},{16,8},{20,12},{24,0},{28,4},{1,25},{... | collective-permute-start | bytes 393224 | tf_op jit(solution)/shard_map/ppermute | solution.py:494
  29.5 1.8 %collective-permute-done.3.refs_3_ = bf16[2,2,128,256]{3,2,1,0:T(8,128)(2,1)S(1)} collective-permute-done((bf16[2,2,128,256]{3,2,1,0:T(8,128)(2,1)S(1)}, bf16[2,2,128,256]{3,2,1,0:T(8,128)(2,1)S(1)}, u32[]{:S(2)}, u32[]{:S(2)}) %collective-permute-start.3) | collective-permute-done | bytes 262176 | tf_op jit(solution)/shard_map/ppermute | solution.py:430
  31.3 0.0 collective-permute-done.5.refs_7_.refs_4_
  31.3 7.0 %ahead.1 = (bf16[2,256,256]{2,1,0:T(8,128)(2,1)S(1)}, bf16[2,256,256]{2,1,0:T(8,128)(2,1)S(1)}, bf16[8,2,256,256]{3,2,1,0:T(8,128)(2,1)S(1)}, bf16[8,2,256,256]{3,2,1,0:T(8,128)(2,1)S(1)}, f32[256,256]{1,0:T(8,128)S(1)}) custom-call(s32[8,128]{1,0:T(8,128)S(1)} %get-tuple-element.96.plan, bf16[2,2,128,256]{3,2,1,0:T(8,128)(2,1)S(1)} %get-tuple-element.102.refs_0_, ...), custom_call_target="tpu_custom_call" | custom-call | flops 100000000 | bytes 300000 | tf_op jit(solution)/shard_map/ahead/pallas_call | solution.py:116
  38.4 0.5 collective-permute-done.8.refs_8_
  38.8 0.0 collective-permute-done.9.refs_9_
  38.8 4.1 %back.1 = (bf16[2,128,256]{2,1,0:T(8,128)(2,1)S(1)}, bf16[2,128,256]{2,1,0:T(8,128)(2,1)S(1)}, bf16[8,2,256,256]{3,2,1,0:T(8,128)(2,1)S(1)}) custom-call(s32[8,128]{1,0:T(8,128)S(1)} %get-tuple-element.96.plan, f32[256,256]{1,0:T(8,128)S(1)} %get-tuple-element.107.refs_0_, bf16[8,2,256,256]{3,2,1,0:T(8,128)(2,1)S(1)} %get-tuple-element.108.refs_1_, ...), custom_call_target="tpu_custom_call" | custom-call | flops 100000000 | bytes 300000 | tf_op jit(solution)/shard_map/back/pallas_call | solution.py:116
  43.0 0.1 collective-permute-start.10
  43.0 1.4 %collective-permute-start.11 = (bf16[2,128,256]{2,1,0:T(8,128)(2,1)S(1)}, bf16[2,128,256]{2,1,0:T(8,128)(2,1)S(1)}, u32[]{:S(2)}, u32[]{:S(2)}) collective-permute-start(bf16[2,128,256]{2,1,0:T(8,128)(2,1)S(1)} %get-tuple-element.128.refs_0_), channel_id=1, source_target_pairs={{0,2},{1,3},{2,0},{3,1},{4,6},{5,7},{6,4},{7,5},{8,10},{9,11},{10,... | collective-permute-start | bytes 393224 | tf_op jit(solution)/shard_map/ppermute | solution.py:430
  44.4 0.5 collective-permute-start.12
  44.9 4.6 %last.1 = (bf16[2,128,256]{2,1,0:T(8,128)(2,1)S(1)}, bf16[2,128,256]{2,1,0:T(8,128)(2,1)S(1)}, bf16[2,2,128,256]{3,2,1,0:T(8,128)(2,1)S(1)}, bf16[2,2,256,256]{3...) custom-call(s32[8,128]{1,0:T(8,128)S(1)} %get-tuple-element.96.plan, ...), custom_call_target="tpu_custom_call" | custom-call | flops 100000000 | bytes 300000 | tf_op jit(solution)/shard_map/last/pallas_call | solution.py:116
  49.5 0.0 collective-permute-done.10.refs_1_
  49.5 1.8 %collective-permute-done.12.refs_3_ = bf16[2,128,256]{2,1,0:T(8,128)(2,1)S(1)} collective-permute-done((bf16[2,128,256]{2,1,0:T(8,128)(2,1)S(1)}, bf16[2,128,256]{2,1,0:T(8,128)(2,1)S(1)}, u32[]{:S(2)}, u32[]{:S(2)}) %collective-permute-start.12) | collective-permute-done | bytes 131104 | tf_op jit(solution)/shard_map/ppermute | solution.py:430
  51.3 0.3 collective-permute-start.22
  51.6 1.0 %collective-permute-start.14 = (bf16[2,2,128,256]{3,2,1,0:T(8,128)(2,1)S(1)}, bf16[2,2,128,256]{3,2,1,0:T(8,128)(2,1)S(1)}, u32[]{:S(2)}, u32[]{:S(2)}) collective-permute-start(bf16[2,2,128,256]{3,2,1,0:T(8,128)(2,1)S(1)} %get-tuple-element.127), channel_id=1, source_target_pairs={{0,2},{1,3},{2,0},{3,1},{4,6},{5,7},{6,4},{7,5},{8,10},{9,11},{10,... | collective-permute-start | bytes 786440 | tf_op jit(solution)/shard_map/ppermute | solution.py:430
  52.5 1.4 %collective-permute-done.22.came = bf16[2,2,2,256,256]{4,3,2,1,0:T(8,128)(2,1)S(1)} collective-permute-done((bf16[2,2,2,256,256]{4,3,2,1,0:T(8,128)(2,1)S(1)}, bf16[2,2,2,256,256]{4,3,2,1,0:T(8,128)(2,1)S(1)}, u32[]{:S(2)}, u32[]{:S(2)}) %collective-permute-start.22) | collective-permute-done | bytes 1048608 | tf_op jit(solution)/shard_map/ppermute | solution.py:430
  54.0 0.8 spread.1
  54.8 1.6 %collective-permute-start.23 = (bf16[2,4,2,2,32,256]{5,4,3,2,1,0:T(8,128)(2,1)S(1)}, bf16[2,4,2,2,32,256]{5,4,3,2,1,0:T(8,128)(2,1)S(1)}, u32[]{:S(2)}, u32[]{:S(2)}) collective-permute-start(bf16[2,4,2,2,32,256]{5,4,3,2,1,0:T(8,128)(2,1)S(1)} %get-tuple-element.151), channel_id=1, source_target_pairs={{0,4},{4,0},{8,12},{12,8},{16,20},{20,16},{24,28},{28,24},{1,5},{5... | collective-permute-start | bytes 1572872 | tf_op jit(solution)/shard_map/ppermute | solution.py:567
  56.3 1.1 %place.2 = (bf16[2,2,128,256]{3,2,1,0:T(8,128)(2,1)S(1)}, f32[2,2,128,256]{3,2,1,0:T(8,128)S(1)}, bf16[2,2,128,256]{3,2,1,0:T(8,128)(2,1)S(1)}) custom-call(s32[8,128]{1,0:T(8,128)S(1)} %get-tuple-element.96.plan, bf16[2,128,256]{2,1,0:T(8,128)(2,1)S(1)} %get-tuple-element.128.refs_0_, bf16[2,128,256]{2,1,0:T(8,128)(2,1)S(1)} %collective-permute-done.10.refs_1_, ...), custom_call_target="tpu_custom_call" | custom-call | flops 100000000 | bytes 300000 | tf_op jit(solution)/shard_map/place/pallas_call | solution.py:116
  57.4 2.9 %collective-permute-start.16 = (bf16[2,2,128,256]{3,2,1,0:T(8,128)(2,1)S(1)}, bf16[2,2,128,256]{3,2,1,0:T(8,128)(2,1)S(1)}, u32[]{:S(2)}, u32[]{:S(2)}) collective-permute-start(bf16[2,2,128,256]{3,2,1,0:T(8,128)(2,1)S(1)} %get-tuple-element.132), channel_id=1, source_target_pairs={{0,8},{4,12},{8,0},{12,4},{16,24},{20,28},{24,16},{28,20},{1,9},{5... | collective-permute-start | bytes 786440 | tf_op jit(solution)/shard_map/ppermute | solution.py:598
  60.3 0.5 collective-permute-start.13
  60.8 0.7 collective-permute-start.19
  61.5 0.5 collective-permute-done.13.refs_1_
  62.0 4.7 %collective-permute-done.16.low = bf16[2,2,128,256]{3,2,1,0:T(8,128)(2,1)S(1)} collective-permute-done((bf16[2,2,128,256]{3,2,1,0:T(8,128)(2,1)S(1)}, bf16[2,2,128,256]{3,2,1,0:T(8,128)(2,1)S(1)}, u32[]{:S(2)}, u32[]{:S(2)}) %collective-permute-start.16) | collective-permute-done | bytes 262176 | tf_op jit(solution)/shard_map/ppermute | solution.py:598
  66.8 1.1 %place.3 = (bf16[2,2,128,256]{3,2,1,0:T(8,128)(2,1)S(1)}, f32[2,2,128,256]{3,2,1,0:T(8,128)S(1)}, bf16[2,2,128,256]{3,2,1,0:T(8,128)(2,1)S(1)}) custom-call(s32[8,128]{1,0:T(8,128)S(1)} %get-tuple-element.96.plan, bf16[2,128,256]{2,1,0:T(8,128)(2,1)S(1)} %get-tuple-element.133.refs_0_, bf16[2,128,256]{2,1,0:T(8,128)(2,1)S(1)} %collective-permute-done.13.refs_1_, ...), custom_call_target="tpu_custom_call" | custom-call | flops 100000000 | bytes 300000 | tf_op jit(solution)/shard_map/place/pallas_call | solution.py:116
  67.8 1.8 %collective-permute-start.17 = (bf16[2,2,128,256]{3,2,1,0:T(8,128)(2,1)S(1)}, bf16[2,2,128,256]{3,2,1,0:T(8,128)(2,1)S(1)}, u32[]{:S(2)}, u32[]{:S(2)}) collective-permute-start(bf16[2,2,128,256]{3,2,1,0:T(8,128)(2,1)S(1)} %get-tuple-element.138), channel_id=1, source_target_pairs={{0,8},{4,12},{8,0},{12,4},{16,24},{20,28},{24,16},{28,20},{1,9},{5... | collective-permute-start | bytes 786440 | tf_op jit(solution)/shard_map/ppermute | solution.py:598
  69.6 0.7 collective-permute-start.18
  70.3 0.0 collective-permute-done.23.came
  70.3 0.1 fold.1
  70.4 0.9 %collective-permute-start.24 = (bf16[4,2,2,32,256]{4,3,2,1,0:T(8,128)(2,1)S(1)}, bf16[4,2,2,32,256]{4,3,2,1,0:T(8,128)(2,1)S(1)}, u32[]{:S(2)}, u32[]{:S(2)}) collective-permute-start(bf16[4,2,2,32,256]{4,3,2,1,0:T(8,128)(2,1)S(1)} %get-tuple-element.153), channel_id=1, source_target_pairs={{0,2},{1,3},{2,0},{3,1},{4,6},{5,7},{6,4},{7,5},{8,10},{9,11},{10,... | collective-permute-start | bytes 786440 | tf_op jit(solution)/shard_map/ppermute | solution.py:430
  71.3 0.7 split.3
  72.0 0.7 collective-permute-start.21
  72.7 2.9 %collective-permute-done.17.low = bf16[2,2,128,256]{3,2,1,0:T(8,128)(2,1)S(1)} collective-permute-done((bf16[2,2,128,256]{3,2,1,0:T(8,128)(2,1)S(1)}, bf16[2,2,128,256]{3,2,1,0:T(8,128)(2,1)S(1)}, u32[]{:S(2)}, u32[]{:S(2)}) %collective-permute-start.17) | collective-permute-done | bytes 262176 | tf_op jit(solution)/shard_map/ppermute | solution.py:598
  75.6 0.0 collective-permute-done.18.high
  75.6 0.7 split.2
  76.3 0.6 collective-permute-start.20
  76.9 0.7 collective-permute-done.24.came
  77.6 3.8 %collective-permute-start.25 = (bf16[2,2,32,256]{3,2,1,0:T(8,128)(2,1)S(1)}, bf16[2,2,32,256]{3,2,1,0:T(8,128)(2,1)S(1)}, u32[]{:S(2)}, u32[]{:S(2)}) collective-permute-start(bf16[2,2,32,256]{3,2,1,0:T(8,128)(2,1)S(1)} %get-tuple-element.155), channel_id=1, source_target_pairs={{0,8},{4,12},{8,0},{12,4},{16,24},{20,28},{24,16},{28,20},{1,9},{5... | collective-permute-start | bytes 196616 | tf_op jit(solution)/shard_map/ppermute | solution.py:580
  81.4 1.1 %collective-permute-start.26 = (bf16[2,2,32,256]{3,2,1,0:T(8,128)(2,1)S(1)}, bf16[2,2,32,256]{3,2,1,0:T(8,128)(2,1)S(1)}, u32[]{:S(2)}, u32[]{:S(2)}) collective-permute-start(bf16[2,2,32,256]{3,2,1,0:T(8,128)(2,1)S(1)} %get-tuple-element.156), channel_id=1, source_target_pairs={{0,16},{4,20},{8,24},{12,28},{16,0},{20,4},{24,8},{28,12},{1,17},{... | collective-permute-start | bytes 196616 | tf_op jit(solution)/shard_map/ppermute | solution.py:580
  82.5 1.4 %collective-permute-start.27 = (bf16[2,2,32,256]{3,2,1,0:T(8,128)(2,1)S(1)}, bf16[2,2,32,256]{3,2,1,0:T(8,128)(2,1)S(1)}, u32[]{:S(2)}, u32[]{:S(2)}) collective-permute-start(bf16[2,2,32,256]{3,2,1,0:T(8,128)(2,1)S(1)} %get-tuple-element.157), channel_id=1, source_target_pairs={{0,24},{4,28},{8,16},{12,20},{16,8},{20,12},{24,0},{28,4},{1,25},{... | collective-permute-start | bytes 196616 | tf_op jit(solution)/shard_map/ppermute | solution.py:580
  83.9 0.6 slice.27
  85.2 0.0 collective-permute-done.20.refs_2_
  85.2 0.9 end.1
  86.0 0.0 collective-permute-done.25.refs_1_
  86.0 1.6 %collective-permute-done.26.refs_2_ = bf16[2,2,32,256]{3,2,1,0:T(8,128)(2,1)S(1)} collective-permute-done((bf16[2,2,32,256]{3,2,1,0:T(8,128)(2,1)S(1)}, bf16[2,2,32,256]{3,2,1,0:T(8,128)(2,1)S(1)}, u32[]{:S(2)}, u32[]{:S(2)}) %collective-permute-start.26) | collective-permute-done | bytes 65568 | tf_op jit(solution)/shard_map/ppermute | solution.py:580
  87.7 0.9 %collective-permute-done.27.refs_3_ = bf16[2,2,32,256]{3,2,1,0:T(8,128)(2,1)S(1)} collective-permute-done((bf16[2,2,32,256]{3,2,1,0:T(8,128)(2,1)S(1)}, bf16[2,2,32,256]{3,2,1,0:T(8,128)(2,1)S(1)}, u32[]{:S(2)}, u32[]{:S(2)}) %collective-permute-start.27) | collective-permute-done | bytes 65568 | tf_op jit(solution)/shard_map/ppermute | solution.py:580
  88.6 0.7 total.1
  (25 shorter events, 0.2 us)
Async XLA Ops:
  0.6 5.2 %copy-start.4 = (bf16[8,256,256]{2,1,0:T(8,128)(2,1)S(1)}, bf16[8,256,256]{2,1,0:T(8,128)(2,1)}, u32[]{:S(2)}) copy-start(bf16[8,256,256]{2,1,0:T(8,128)(2,1)} %amplitudes_far.1) | copy-start | bytes 3145732
  2.0 15.0 %collective-permute-start = (bf16[2,2,256,256]{3,2,1,0:T(8,128)(2,1)S(1)}, bf16[2,2,256,256]{3,2,1,0:T(8,128)(2,1)S(1)}, u32[]{:S(2)}, u32[]{:S(2)}) collective-permute-start(bf16[2,2,256,256]{3,2,1,0:T(8,128)(2,1)S(1)} %convert_element_type.42), channel_id=1, source_target_pairs={{0,2},{1,3},{2,0},{3,1},{4,6},{5,7},{6,4},{7,5},{8,10},{9,11},{10,... | collective-permute-start | bytes 1572872 | tf_op jit(solution)/shard_map/ppermute | solution.py:430
  5.8 1.6 %copy-start.2 = (bf16[2,2,128,2048]{3,2,1,0:T(8,128)(2,1)S(1)}, bf16[2,2,128,2048]{3,2,1,0:T(8,128)(2,1)}, u32[]{:S(2)}) copy-start(bf16[2,2,128,2048]{3,2,1,0:T(8,128)(2,1)} %strip_far.1) | copy-start | bytes 6291460
  7.4 0.7 copy-start.6
  8.1 23.3 %copy-start = (f32[2,2,256,256]{3,2,1,0:T(8,128)S(1)}, f32[2,2,256,256]{3,2,1,0:T(8,128)}, u32[]{:S(2)}) copy-start(f32[2,2,256,256]{3,2,1,0:T(8,128)} %refs_1_.1) | copy-start | bytes 3145732
  8.1 23.3 %copy-start.1 = (bf16[4,256,256]{2,1,0:T(8,128)(2,1)S(1)}, bf16[4,256,256]{2,1,0:T(8,128)(2,1)}, u32[]{:S(2)}) copy-start(bf16[4,256,256]{2,1,0:T(8,128)(2,1)} %constant.181.clone.refs_8_.refs_4_.refs_6_) | copy-start | bytes 1572868
  8.1 23.3 %copy-start.3 = (f32[2,256,256]{2,1,0:T(8,128)S(1)}, f32[2,256,256]{2,1,0:T(8,128)}, u32[]{:S(2)}) copy-start(f32[2,256,256]{2,1,0:T(8,128)} %constant.182.clone.refs_9_.refs_7_) | copy-start | bytes 1572868
  10.2 13.4 %collective-permute-start.6 = (bf16[4,256,256]{2,1,0:T(8,128)(2,1)S(1)}, bf16[4,256,256]{2,1,0:T(8,128)(2,1)S(1)}, u32[]{:S(2)}, u32[]{:S(2)}) collective-permute-start(bf16[4,256,256]{2,1,0:T(8,128)(2,1)S(1)} %get-tuple-element.112), channel_id=1, source_target_pairs={{0,4},{4,0},{8,12},{12,8},{16,20},{20,16},{24,28},{28,24},{1,5},{5... | collective-permute-start | bytes 1572872 | tf_op jit(solution)/shard_map/ppermute | solution.py:488
  11.7 12.6 %collective-permute-start.4 = (bf16[2,2,256,256]{3,2,1,0:T(8,128)(2,1)S(1)}, bf16[2,2,256,256]{3,2,1,0:T(8,128)(2,1)S(1)}, u32[]{:S(2)}, u32[]{:S(2)}) collective-permute-start(bf16[2,2,256,256]{3,2,1,0:T(8,128)(2,1)S(1)} %convert_element_type.42), channel_id=1, source_target_pairs={{0,1},{1,0},{2,3},{3,2},{4,5},{5,4},{6,7},{7,6},{8,9},{9,8},{10,11... | collective-permute-start | bytes 1572872 | tf_op jit(solution)/shard_map/ppermute | solution.py:430
  17.0 14.3 %collective-permute-start.5 = (bf16[2,2,256,256]{3,2,1,0:T(8,128)(2,1)S(1)}, bf16[2,2,256,256]{3,2,1,0:T(8,128)(2,1)S(1)}, u32[]{:S(2)}, u32[]{:S(2)}) collective-permute-start(bf16[2,2,256,256]{3,2,1,0:T(8,128)(2,1)S(1)} %collective-permute-done.refs_6_.refs_3_), channel_id=1, source_target_pairs={{0,1},{1,0},{2,3},{3,2},{4,5},{5,4},{6,7},{7,6},{8,9},{9,8},{10,11... | collective-permute-start | bytes 1572872 | tf_op jit(solution)/shard_map/ppermute | solution.py:430
  17.0 9.0 %collective-permute-start.1 = (bf16[2,2,128,256]{3,2,1,0:T(8,128)(2,1)S(1)}, bf16[2,2,128,256]{3,2,1,0:T(8,128)(2,1)S(1)}, u32[]{:S(2)}, u32[]{:S(2)}) collective-permute-start(bf16[2,2,128,256]{3,2,1,0:T(8,128)(2,1)S(1)} %get-tuple-element.103), channel_id=1, source_target_pairs={{0,1},{1,0},{2,3},{3,2},{4,5},{5,4},{6,7},{7,6},{8,9},{9,8},{10,11... | collective-permute-start | bytes 786440 | tf_op jit(solution)/shard_map/ppermute | solution.py:430
  17.5 11.1 %collective-permute-start.2 = (bf16[2,2,128,256]{3,2,1,0:T(8,128)(2,1)S(1)}, bf16[2,2,128,256]{3,2,1,0:T(8,128)(2,1)S(1)}, u32[]{:S(2)}, u32[]{:S(2)}) collective-permute-start(bf16[2,2,128,256]{3,2,1,0:T(8,128)(2,1)S(1)} %get-tuple-element.104), channel_id=1, source_target_pairs={{0,2},{1,3},{2,0},{3,1},{4,6},{5,7},{6,4},{7,5},{8,10},{9,11},{10,... | collective-permute-start | bytes 786440 | tf_op jit(solution)/shard_map/ppermute | solution.py:430
  23.6 7.7 %collective-permute-start.3 = (bf16[2,2,128,256]{3,2,1,0:T(8,128)(2,1)S(1)}, bf16[2,2,128,256]{3,2,1,0:T(8,128)(2,1)S(1)}, u32[]{:S(2)}, u32[]{:S(2)}) collective-permute-start(bf16[2,2,128,256]{3,2,1,0:T(8,128)(2,1)S(1)} %get-tuple-element.105), channel_id=1, source_target_pairs={{0,3},{1,2},{2,1},{3,0},{4,7},{5,6},{6,5},{7,4},{8,11},{9,10},{10,... | collective-permute-start | bytes 786440 | tf_op jit(solution)/shard_map/ppermute | solution.py:430
  24.3 14.0 %collective-permute-start.7 = (bf16[256,256]{1,0:T(8,128)(2,1)S(1)}, bf16[256,256]{1,0:T(8,128)(2,1)S(1)}, u32[]{:S(2)}, u32[]{:S(2)}) collective-permute-start(bf16[256,256]{1,0:T(8,128)(2,1)S(1)} %get-tuple-element.114), channel_id=1, source_target_pairs={{0,8},{4,12},{8,0},{12,4},{16,24},{20,28},{24,16},{28,20},{1,9},{5... | collective-permute-start | bytes 393224 | tf_op jit(solution)/shard_map/ppermute | solution.py:494
  26.0 12.9 %collective-permute-start.8 = (bf16[256,256]{1,0:T(8,128)(2,1)S(1)}, bf16[256,256]{1,0:T(8,128)(2,1)S(1)}, u32[]{:S(2)}, u32[]{:S(2)}) collective-permute-start(bf16[256,256]{1,0:T(8,128)(2,1)S(1)} %get-tuple-element.115), channel_id=1, source_target_pairs={{0,16},{4,20},{8,24},{12,28},{16,0},{20,4},{24,8},{28,12},{1,17},{... | collective-permute-start | bytes 393224 | tf_op jit(solution)/shard_map/ppermute | solution.py:494
  28.6 10.3 %copy-start.5 = (bf16[2,256,256]{2,1,0:T(8,128)(2,1)S(1)}, bf16[2,256,256]{2,1,0:T(8,128)(2,1)}, u32[]{:S(2)}) copy-start(bf16[2,256,256]{2,1,0:T(8,128)(2,1)} %constant.183.clone.refs_5_) | copy-start | bytes 786436
  28.6 10.3 %collective-permute-start.9 = (bf16[256,256]{1,0:T(8,128)(2,1)S(1)}, bf16[256,256]{1,0:T(8,128)(2,1)S(1)}, u32[]{:S(2)}, u32[]{:S(2)}) collective-permute-start(bf16[256,256]{1,0:T(8,128)(2,1)S(1)} %get-tuple-element.116), channel_id=1, source_target_pairs={{0,24},{4,28},{8,16},{12,20},{16,8},{20,12},{24,0},{28,4},{1,25},{... | collective-permute-start | bytes 393224 | tf_op jit(solution)/shard_map/ppermute | solution.py:494
  43.0 6.5 %collective-permute-start.10 = (bf16[2,128,256]{2,1,0:T(8,128)(2,1)S(1)}, bf16[2,128,256]{2,1,0:T(8,128)(2,1)S(1)}, u32[]{:S(2)}, u32[]{:S(2)}) collective-permute-start(bf16[2,128,256]{2,1,0:T(8,128)(2,1)S(1)} %get-tuple-element.118), channel_id=1, source_target_pairs={{0,1},{1,0},{2,3},{3,2},{4,5},{5,4},{6,7},{7,6},{8,9},{9,8},{10,11... | collective-permute-start | bytes 393224 | tf_op jit(solution)/shard_map/ppermute | solution.py:430
  43.0 6.5 %collective-permute-start.11 = (bf16[2,128,256]{2,1,0:T(8,128)(2,1)S(1)}, bf16[2,128,256]{2,1,0:T(8,128)(2,1)S(1)}, u32[]{:S(2)}, u32[]{:S(2)}) collective-permute-start(bf16[2,128,256]{2,1,0:T(8,128)(2,1)S(1)} %get-tuple-element.128.refs_0_), channel_id=1, source_target_pairs={{0,2},{1,3},{2,0},{3,1},{4,6},{5,7},{6,4},{7,5},{8,10},{9,11},{10,... | collective-permute-start | bytes 393224 | tf_op jit(solution)/shard_map/ppermute | solution.py:430
  44.4 6.9 %collective-permute-start.12 = (bf16[2,128,256]{2,1,0:T(8,128)(2,1)S(1)}, bf16[2,128,256]{2,1,0:T(8,128)(2,1)S(1)}, u32[]{:S(2)}, u32[]{:S(2)}) collective-permute-start(bf16[2,128,256]{2,1,0:T(8,128)(2,1)S(1)} %get-tuple-element.118), channel_id=1, source_target_pairs={{0,3},{1,2},{2,1},{3,0},{4,7},{5,6},{6,5},{7,4},{8,11},{9,10},{10,... | collective-permute-start | bytes 393224 | tf_op jit(solution)/shard_map/ppermute | solution.py:430
  51.3 2.7 %collective-permute-start.22 = (bf16[2,2,2,256,256]{4,3,2,1,0:T(8,128)(2,1)S(1)}, bf16[2,2,2,256,256]{4,3,2,1,0:T(8,128)(2,1)S(1)}, u32[]{:S(2)}, u32[]{:S(2)}) collective-permute-start(bf16[2,2,2,256,256]{4,3,2,1,0:T(8,128)(2,1)S(1)} %get-tuple-element.149), channel_id=1, source_target_pairs={{0,1},{1,0},{2,3},{3,2},{4,5},{5,4},{6,7},{7,6},{8,9},{9,8},{10,11... | collective-permute-start | bytes 3145736 | tf_op jit(solution)/shard_map/ppermute | solution.py:430
  51.6 8.7 %collective-permute-start.14 = (bf16[2,2,128,256]{3,2,1,0:T(8,128)(2,1)S(1)}, bf16[2,2,128,256]{3,2,1,0:T(8,128)(2,1)S(1)}, u32[]{:S(2)}, u32[]{:S(2)}) collective-permute-start(bf16[2,2,128,256]{3,2,1,0:T(8,128)(2,1)S(1)} %get-tuple-element.127), channel_id=1, source_target_pairs={{0,2},{1,3},{2,0},{3,1},{4,6},{5,7},{6,4},{7,5},{8,10},{9,11},{10,... | collective-permute-start | bytes 786440 | tf_op jit(solution)/shard_map/ppermute | solution.py:430
  54.8 15.5 %collective-permute-start.23 = (bf16[2,4,2,2,32,256]{5,4,3,2,1,0:T(8,128)(2,1)S(1)}, bf16[2,4,2,2,32,256]{5,4,3,2,1,0:T(8,128)(2,1)S(1)}, u32[]{:S(2)}, u32[]{:S(2)}) collective-permute-start(bf16[2,4,2,2,32,256]{5,4,3,2,1,0:T(8,128)(2,1)S(1)} %get-tuple-element.151), channel_id=1, source_target_pairs={{0,4},{4,0},{8,12},{12,8},{16,20},{20,16},{24,28},{28,24},{1,5},{5... | collective-permute-start | bytes 1572872 | tf_op jit(solution)/shard_map/ppermute | solution.py:567
  57.4 9.3 %collective-permute-start.16 = (bf16[2,2,128,256]{3,2,1,0:T(8,128)(2,1)S(1)}, bf16[2,2,128,256]{3,2,1,0:T(8,128)(2,1)S(1)}, u32[]{:S(2)}, u32[]{:S(2)}) collective-permute-start(bf16[2,2,128,256]{3,2,1,0:T(8,128)(2,1)S(1)} %get-tuple-element.132), channel_id=1, source_target_pairs={{0,8},{4,12},{8,0},{12,4},{16,24},{20,28},{24,16},{28,20},{1,9},{5... | collective-permute-start | bytes 786440 | tf_op jit(solution)/shard_map/ppermute | solution.py:598
  60.3 6.5 %collective-permute-start.15 = (bf16[2,2,128,256]{3,2,1,0:T(8,128)(2,1)S(1)}, bf16[2,2,128,256]{3,2,1,0:T(8,128)(2,1)S(1)}, u32[]{:S(2)}, u32[]{:S(2)}) collective-permute-start(bf16[2,2,128,256]{3,2,1,0:T(8,128)(2,1)S(1)} %collective-permute-done.14.refs_2_), channel_id=1, source_target_pairs={{0,1},{1,0},{2,3},{3,2},{4,5},{5,4},{6,7},{7,6},{8,9},{9,8},{10,11... | collective-permute-start | bytes 786440 | tf_op jit(solution)/shard_map/ppermute | solution.py:430
  60.3 1.7 %collective-permute-start.13 = (bf16[2,128,256]{2,1,0:T(8,128)(2,1)S(1)}, bf16[2,128,256]{2,1,0:T(8,128)(2,1)S(1)}, u32[]{:S(2)}, u32[]{:S(2)}) collective-permute-start(bf16[2,128,256]{2,1,0:T(8,128)(2,1)S(1)} %get-tuple-element.126), channel_id=1, source_target_pairs={{0,1},{1,0},{2,3},{3,2},{4,5},{5,4},{6,7},{7,6},{8,9},{9,8},{10,11... | collective-permute-start | bytes 393224 | tf_op jit(solution)/shard_map/ppermute | solution.py:430
  60.8 10.5 %collective-permute-start.19 = (bf16[2,2,128,256]{3,2,1,0:T(8,128)(2,1)S(1)}, bf16[2,2,128,256]{3,2,1,0:T(8,128)(2,1)S(1)}, u32[]{:S(2)}, u32[]{:S(2)}) collective-permute-start(bf16[2,2,128,256]{3,2,1,0:T(8,128)(2,1)S(1)} %get-tuple-element.143), channel_id=1, source_target_pairs={{8,16},{12,20},{16,8},{20,12},{9,17},{13,21},{17,9},{21,13},{10,18... | collective-permute-start | bytes 786440 | tf_op jit(solution)/shard_map/ppermute | solution.py:600
  67.8 7.7 %collective-permute-start.17 = (bf16[2,2,128,256]{3,2,1,0:T(8,128)(2,1)S(1)}, bf16[2,2,128,256]{3,2,1,0:T(8,128)(2,1)S(1)}, u32[]{:S(2)}, u32[]{:S(2)}) collective-permute-start(bf16[2,2,128,256]{3,2,1,0:T(8,128)(2,1)S(1)} %get-tuple-element.138), channel_id=1, source_target_pairs={{0,8},{4,12},{8,0},{12,4},{16,24},{20,28},{24,16},{28,20},{1,9},{5... | collective-permute-start | bytes 786440 | tf_op jit(solution)/shard_map/ppermute | solution.py:598
  69.6 5.9 %collective-permute-start.18 = (bf16[2,2,128,256]{3,2,1,0:T(8,128)(2,1)S(1)}, bf16[2,2,128,256]{3,2,1,0:T(8,128)(2,1)S(1)}, u32[]{:S(2)}, u32[]{:S(2)}) collective-permute-start(bf16[2,2,128,256]{3,2,1,0:T(8,128)(2,1)S(1)} %get-tuple-element.139), channel_id=1, source_target_pairs={{8,16},{12,20},{16,8},{20,12},{9,17},{13,21},{17,9},{21,13},{10,18... | collective-permute-start | bytes 786440 | tf_op jit(solution)/shard_map/ppermute | solution.py:600
  70.4 7.1 %collective-permute-start.24 = (bf16[4,2,2,32,256]{4,3,2,1,0:T(8,128)(2,1)S(1)}, bf16[4,2,2,32,256]{4,3,2,1,0:T(8,128)(2,1)S(1)}, u32[]{:S(2)}, u32[]{:S(2)}) collective-permute-start(bf16[4,2,2,32,256]{4,3,2,1,0:T(8,128)(2,1)S(1)} %get-tuple-element.153), channel_id=1, source_target_pairs={{0,2},{1,3},{2,0},{3,1},{4,6},{5,7},{6,4},{7,5},{8,10},{9,11},{10,... | collective-permute-start | bytes 786440 | tf_op jit(solution)/shard_map/ppermute | solution.py:430
  72.0 13.1 %collective-permute-start.21 = (bf16[2,128,256]{2,1,0:T(8,128)(2,1)S(1)}, bf16[2,128,256]{2,1,0:T(8,128)(2,1)S(1)}, u32[]{:S(2)}, u32[]{:S(2)}) collective-permute-start(bf16[2,128,256]{2,1,0:T(8,128)(2,1)S(1)} %get-tuple-element.146), channel_id=1, source_target_pairs={{0,4},{4,0},{8,12},{12,8},{16,20},{20,16},{24,28},{28,24},{1,5},{5... | collective-permute-start | bytes 393224 | tf_op jit(solution)/shard_map/ppermute | solution.py:610
  76.3 8.9 %collective-permute-start.20 = (bf16[2,128,256]{2,1,0:T(8,128)(2,1)S(1)}, bf16[2,128,256]{2,1,0:T(8,128)(2,1)S(1)}, u32[]{:S(2)}, u32[]{:S(2)}) collective-permute-start(bf16[2,128,256]{2,1,0:T(8,128)(2,1)S(1)} %get-tuple-element.145), channel_id=1, source_target_pairs={{0,4},{4,0},{8,12},{12,8},{16,20},{20,16},{24,28},{28,24},{1,5},{5... | collective-permute-start | bytes 393224 | tf_op jit(solution)/shard_map/ppermute | solution.py:610
  77.6 8.4 %collective-permute-start.25 = (bf16[2,2,32,256]{3,2,1,0:T(8,128)(2,1)S(1)}, bf16[2,2,32,256]{3,2,1,0:T(8,128)(2,1)S(1)}, u32[]{:S(2)}, u32[]{:S(2)}) collective-permute-start(bf16[2,2,32,256]{3,2,1,0:T(8,128)(2,1)S(1)} %get-tuple-element.155), channel_id=1, source_target_pairs={{0,8},{4,12},{8,0},{12,4},{16,24},{20,28},{24,16},{28,20},{1,9},{5... | collective-permute-start | bytes 196616 | tf_op jit(solution)/shard_map/ppermute | solution.py:580
  81.4 6.3 %collective-permute-start.26 = (bf16[2,2,32,256]{3,2,1,0:T(8,128)(2,1)S(1)}, bf16[2,2,32,256]{3,2,1,0:T(8,128)(2,1)S(1)}, u32[]{:S(2)}, u32[]{:S(2)}) collective-permute-start(bf16[2,2,32,256]{3,2,1,0:T(8,128)(2,1)S(1)} %get-tuple-element.156), channel_id=1, source_target_pairs={{0,16},{4,20},{8,24},{12,28},{16,0},{20,4},{24,8},{28,12},{1,17},{... | collective-permute-start | bytes 196616 | tf_op jit(solution)/shard_map/ppermute | solution.py:580
  82.5 6.1 %collective-permute-start.27 = (bf16[2,2,32,256]{3,2,1,0:T(8,128)(2,1)S(1)}, bf16[2,2,32,256]{3,2,1,0:T(8,128)(2,1)S(1)}, u32[]{:S(2)}, u32[]{:S(2)}) collective-permute-start(bf16[2,2,32,256]{3,2,1,0:T(8,128)(2,1)S(1)} %get-tuple-element.157), channel_id=1, source_target_pairs={{0,24},{4,28},{8,16},{12,20},{16,8},{20,12},{24,0},{28,4},{1,25},{... | collective-permute-start | bytes 196616 | tf_op jit(solution)/shard_map/ppermute | solution.py:580

commit v4 on v3

--- a/solution.py
+++ b/solution.py
@@ -551,7 +551,7 @@
         us=0.1,
         mib=24,
     )
-    pieces[1], own, other, pair, beside = lax.optimization_barrier((pieces[1], own, other, pair, beside))
+    pieces[1], beside = lax.optimization_barrier((pieces[1], beside))
     pair = turned(pair, 2, tiles)
     pieces[0] = [own, turned(other, 1, tiles), pair, turned(pair, 1, tiles)]
     share = (groups // 2, modes, 2, points // groups, points)

time: 89.5 us -> 89.5 us (level)
  no operation moved by 1% of the time
where the time goes in v4:
time: 89.5 us; the launch traced here: 89.3 us
  starting transfers between devices  31.5 us (35%)
  waiting for transfers between devices  26.8 us (30%)
  Pallas kernels  24.5 us (27%)
  local copies, waits for them, and re-layouts  3.63 us (4%)
  between operations  1.52 us (2%)
  other arithmetic  1.37 us (2%)
    pallas_call x14, Pallas kernels, call(): pl.pallas_call(body, out_shape=[pltpu.VMEM(shape, dtype) if at in keep el...  24.5 us
    ppermute x14, waiting for transfers between devices, turned(): return lax.ppermute(value, 'tile', [(i, i ^ turn) for i in range(tiles)])  11.6 us
    ppermute x14, starting transfers between devices, turned(): return lax.ppermute(value, 'tile', [(i, i ^ turn) for i in range(tiles)])  9.86 us
    ppermute x2, waiting for transfers between devices, on_device_by_slot(): low_in = lax.ppermute(even, 'pos', pairs)  7.74 us
    ppermute x3, starting transfers between devices, on_device_by_slot(): lax.ppermute(send, 'pos', [(i, i ^ 2 * turn) for i in range(groups)])  6.23 us
    ppermute x3, starting transfers between devices, on_device_by_slot(): lax.ppermute(merged[turn], 'pos', [(i, i ^ 2 * turn) for i in range(group...  5.2 us
    ppermute x2, starting transfers between devices, on_device_by_slot(): low_in = lax.ppermute(even, 'pos', pairs)  4.67 us
    ppermute x1, waiting for transfers between devices, on_device_by_slot(): lax.ppermute(far, 'pos', aside)  4.38 us
  transfers between devices with their start and end apart: 28, of which 12 were waited for; matrix products, arithmetic and copies ran while one was open for 2% of the time, Pallas kernels for 22%

profile of v4, /device:TPU:0, one launch (start us, length us, event | category | flops | bytes accessed | tf_op | source)
XLA Modules:
  0.0 89.3 jit_solution(13258565967496319620)
XLA Ops:
  0.6 1.4 %convert_element_type.42 = bf16[2,2,256,256]{3,2,1,0:T(8,128)(2,1)S(1)} convert(f32[2,2,256,256]{3,2,1,0:T(8,128)} %refs_1_.1) | non-fusion elementwise | flops 262144 | bytes 1572864 | tf_op jit(solution)/shard_map/convert_element_type | solution.py:461
  2.0 3.0 %collective-permute-start = (bf16[2,2,256,256]{3,2,1,0:T(8,128)(2,1)S(1)}, bf16[2,2,256,256]{3,2,1,0:T(8,128)(2,1)S(1)}, u32[]{:S(2)}, u32[]{:S(2)}) collective-permute-start(bf16[2,2,256,256]{3,2,1,0:T(8,128)(2,1)S(1)} %convert_element_type.42), channel_id=1, source_target_pairs={{0,2},{1,3},{2,0},{3,1},{4,6},{5,7},{6,4},{7,5},{8,10},{9,11},{10,... | collective-permute-start | bytes 1572872 | tf_op jit(solution)/shard_map/ppermute | solution.py:430
  5.0 0.8 copy.11.offsets
  5.8 1.6 %copy-done.2 = bf16[2,2,128,2048]{3,2,1,0:T(8,128)(2,1)S(1)} copy-done((bf16[2,2,128,2048]{3,2,1,0:T(8,128)(2,1)S(1)}, bf16[2,2,128,2048]{3,2,1,0:T(8,128)(2,1)}, u32[]{:S(2)}) %copy-start.2) | copy-done | bytes 2097176
  7.4 0.7 copy-done.6
  8.1 2.1 %first.1 = (bf16[2,2,128,256]{3,2,1,0:T(8,128)(2,1)S(1)}, bf16[2,2,128,256]{3,2,1,0:T(8,128)(2,1)S(1)}, bf16[2,2,128,256]{3,2,1,0:T(8,128)(2,1)S(1)}, bf16[2,2,1...) custom-call(s32[8]{0:T(128)S(1)} %copy-done.6, ...), custom_call_target="tpu_custom_call" | custom-call | flops 100000000 | bytes 300000 | tf_op jit(solution)/shard_map/first/pallas_call | solution.py:116
  10.2 1.5 %collective-permute-start.6 = (bf16[4,256,256]{2,1,0:T(8,128)(2,1)S(1)}, bf16[4,256,256]{2,1,0:T(8,128)(2,1)S(1)}, u32[]{:S(2)}, u32[]{:S(2)}) collective-permute-start(bf16[4,256,256]{2,1,0:T(8,128)(2,1)S(1)} %get-tuple-element.109), channel_id=1, source_target_pairs={{0,4},{4,0},{8,12},{12,8},{16,20},{20,16},{24,28},{28,24},{1,5},{5... | collective-permute-start | bytes 1572872 | tf_op jit(solution)/shard_map/ppermute | solution.py:488
  11.7 0.0 collective-permute-start.4
  11.7 5.3 %collective-permute-done.refs_6_.refs_3_ = bf16[2,2,256,256]{3,2,1,0:T(8,128)(2,1)S(1)} collective-permute-done((bf16[2,2,256,256]{3,2,1,0:T(8,128)(2,1)S(1)}, bf16[2,2,256,256]{3,2,1,0:T(8,128)(2,1)S(1)}, u32[]{:S(2)}, u32[]{:S(2)}) %collective-permute-start) | collective-permute-done | bytes 524320 | tf_op jit(solution)/shard_map/ppermute | solution.py:430
  17.0 0.0 collective-permute-start.5
  17.0 0.5 collective-permute-start.1
  17.5 1.7 %collective-permute-start.2 = (bf16[2,2,128,256]{3,2,1,0:T(8,128)(2,1)S(1)}, bf16[2,2,128,256]{3,2,1,0:T(8,128)(2,1)S(1)}, u32[]{:S(2)}, u32[]{:S(2)}) collective-permute-start(bf16[2,2,128,256]{3,2,1,0:T(8,128)(2,1)S(1)} %get-tuple-element.101), channel_id=1, source_target_pairs={{0,2},{1,3},{2,0},{3,1},{4,6},{5,7},{6,4},{7,5},{8,10},{9,11},{10,... | collective-permute-start | bytes 786440 | tf_op jit(solution)/shard_map/ppermute | solution.py:430
  19.2 4.4 %collective-permute-done.6.came = bf16[4,256,256]{2,1,0:T(8,128)(2,1)S(1)} collective-permute-done((bf16[4,256,256]{2,1,0:T(8,128)(2,1)S(1)}, bf16[4,256,256]{2,1,0:T(8,128)(2,1)S(1)}, u32[]{:S(2)}, u32[]{:S(2)}) %collective-permute-start.6) | collective-permute-done | bytes 524320 | tf_op jit(solution)/shard_map/ppermute | solution.py:488
  23.6 0.0 collective-permute-start.3
  23.6 0.7 merge.1
  24.3 0.0 collective-permute-done.4.refs_5_.refs_2_
  24.3 1.7 %collective-permute-start.7 = (bf16[256,256]{1,0:T(8,128)(2,1)S(1)}, bf16[256,256]{1,0:T(8,128)(2,1)S(1)}, u32[]{:S(2)}, u32[]{:S(2)}) collective-permute-start(bf16[256,256]{1,0:T(8,128)(2,1)S(1)} %get-tuple-element.111), channel_id=1, source_target_pairs={{0,8},{4,12},{8,0},{12,4},{16,24},{20,28},{24,16},{28,20},{1,9},{5... | collective-permute-start | bytes 393224 | tf_op jit(solution)/shard_map/ppermute | solution.py:494
  26.0 2.6 %collective-permute-start.8 = (bf16[256,256]{1,0:T(8,128)(2,1)S(1)}, bf16[256,256]{1,0:T(8,128)(2,1)S(1)}, u32[]{:S(2)}, u32[]{:S(2)}) collective-permute-start(bf16[256,256]{1,0:T(8,128)(2,1)S(1)} %get-tuple-element.112), channel_id=1, source_target_pairs={{0,16},{4,20},{8,24},{12,28},{16,0},{20,4},{24,8},{28,12},{1,17},{... | collective-permute-start | bytes 393224 | tf_op jit(solution)/shard_map/ppermute | solution.py:494
  28.6 0.9 %collective-permute-start.9 = (bf16[256,256]{1,0:T(8,128)(2,1)S(1)}, bf16[256,256]{1,0:T(8,128)(2,1)S(1)}, u32[]{:S(2)}, u32[]{:S(2)}) collective-permute-start(bf16[256,256]{1,0:T(8,128)(2,1)S(1)} %get-tuple-element.113), channel_id=1, source_target_pairs={{0,24},{4,28},{8,16},{12,20},{16,8},{20,12},{24,0},{28,4},{1,25},{... | collective-permute-start | bytes 393224 | tf_op jit(solution)/shard_map/ppermute | solution.py:494
  29.5 1.8 %collective-permute-done.3.refs_3_ = bf16[2,2,128,256]{3,2,1,0:T(8,128)(2,1)S(1)} collective-permute-done((bf16[2,2,128,256]{3,2,1,0:T(8,128)(2,1)S(1)}, bf16[2,2,128,256]{3,2,1,0:T(8,128)(2,1)S(1)}, u32[]{:S(2)}, u32[]{:S(2)}) %collective-permute-start.3) | collective-permute-done | bytes 262176 | tf_op jit(solution)/shard_map/ppermute | solution.py:430
  31.3 0.0 collective-permute-done.5.refs_7_.refs_4_
  31.3 7.0 %ahead.1 = (bf16[2,256,256]{2,1,0:T(8,128)(2,1)S(1)}, bf16[2,256,256]{2,1,0:T(8,128)(2,1)S(1)}, bf16[8,2,256,256]{3,2,1,0:T(8,128)(2,1)S(1)}, bf16[8,2,256,256]{3,2,1,0:T(8,128)(2,1)S(1)}, f32[256,256]{1,0:T(8,128)S(1)}) custom-call(s32[8,128]{1,0:T(8,128)S(1)} %get-tuple-element.93.plan, bf16[2,2,128,256]{3,2,1,0:T(8,128)(2,1)S(1)} %get-tuple-element.99.refs_0_, ...), custom_call_target="tpu_custom_call" | custom-call | flops 100000000 | bytes 300000 | tf_op jit(solution)/shard_map/ahead/pallas_call | solution.py:116
  38.3 0.0 collective-permute-done.7.refs_7_
  38.4 0.5 collective-permute-done.8.refs_8_
  38.9 4.1 %back.1 = (bf16[2,128,256]{2,1,0:T(8,128)(2,1)S(1)}, bf16[2,128,256]{2,1,0:T(8,128)(2,1)S(1)}, bf16[8,2,256,256]{3,2,1,0:T(8,128)(2,1)S(1)}) custom-call(s32[8,128]{1,0:T(8,128)S(1)} %get-tuple-element.93.plan, f32[256,256]{1,0:T(8,128)S(1)} %get-tuple-element.104.refs_0_, bf16[8,2,256,256]{3,2,1,0:T(8,128)(2,1)S(1)} %get-tuple-element.105.refs_1_, ...), custom_call_target="tpu_custom_call" | custom-call | flops 100000000 | bytes 300000 | tf_op jit(solution)/shard_map/back/pallas_call | solution.py:116
  43.0 0.1 collective-permute-start.13
  43.1 1.4 %collective-permute-start.14 = (bf16[2,128,256]{2,1,0:T(8,128)(2,1)S(1)}, bf16[2,128,256]{2,1,0:T(8,128)(2,1)S(1)}, u32[]{:S(2)}, u32[]{:S(2)}) collective-permute-start(bf16[2,128,256]{2,1,0:T(8,128)(2,1)S(1)} %get-tuple-element.122.refs_0_), channel_id=1, source_target_pairs={{0,2},{1,3},{2,0},{3,1},{4,6},{5,7},{6,4},{7,5},{8,10},{9,11},{10,... | collective-permute-start | bytes 393224 | tf_op jit(solution)/shard_map/ppermute | solution.py:430
  44.4 0.5 collective-permute-start.15
  44.9 4.6 %last.1 = (bf16[2,128,256]{2,1,0:T(8,128)(2,1)S(1)}, bf16[2,128,256]{2,1,0:T(8,128)(2,1)S(1)}, bf16[2,2,128,256]{3,2,1,0:T(8,128)(2,1)S(1)}, bf16[2,2,256,256]{3...) custom-call(s32[8,128]{1,0:T(8,128)S(1)} %get-tuple-element.93.plan, ...), custom_call_target="tpu_custom_call" | custom-call | flops 100000000 | bytes 300000 | tf_op jit(solution)/shard_map/last/pallas_call | solution.py:116
  49.5 0.0 collective-permute-done.13.refs_1_
  49.5 1.8 %collective-permute-done.15.refs_3_ = bf16[2,128,256]{2,1,0:T(8,128)(2,1)S(1)} collective-permute-done((bf16[2,128,256]{2,1,0:T(8,128)(2,1)S(1)}, bf16[2,128,256]{2,1,0:T(8,128)(2,1)S(1)}, u32[]{:S(2)}, u32[]{:S(2)}) %collective-permute-start.15) | collective-permute-done | bytes 131104 | tf_op jit(solution)/shard_map/ppermute | solution.py:430
  51.3 0.3 collective-permute-start.22
  51.6 0.9 %collective-permute-start.11 = (bf16[2,2,128,256]{3,2,1,0:T(8,128)(2,1)S(1)}, bf16[2,2,128,256]{3,2,1,0:T(8,128)(2,1)S(1)}, u32[]{:S(2)}, u32[]{:S(2)}) collective-permute-start(bf16[2,2,128,256]{3,2,1,0:T(8,128)(2,1)S(1)} %get-tuple-element.118), channel_id=1, source_target_pairs={{0,2},{1,3},{2,0},{3,1},{4,6},{5,7},{6,4},{7,5},{8,10},{9,11},{10,... | collective-permute-start | bytes 786440 | tf_op jit(solution)/shard_map/ppermute | solution.py:430
  52.5 1.5 %collective-permute-done.22.came = bf16[2,2,2,256,256]{4,3,2,1,0:T(8,128)(2,1)S(1)} collective-permute-done((bf16[2,2,2,256,256]{4,3,2,1,0:T(8,128)(2,1)S(1)}, bf16[2,2,2,256,256]{4,3,2,1,0:T(8,128)(2,1)S(1)}, u32[]{:S(2)}, u32[]{:S(2)}) %collective-permute-start.22) | collective-permute-done | bytes 1048608 | tf_op jit(solution)/shard_map/ppermute | solution.py:430
  54.0 0.8 spread.1
  54.8 1.5 %collective-permute-start.23 = (bf16[2,4,2,2,32,256]{5,4,3,2,1,0:T(8,128)(2,1)S(1)}, bf16[2,4,2,2,32,256]{5,4,3,2,1,0:T(8,128)(2,1)S(1)}, u32[]{:S(2)}, u32[]{:S(2)}) collective-permute-start(bf16[2,4,2,2,32,256]{5,4,3,2,1,0:T(8,128)(2,1)S(1)} %get-tuple-element.145), channel_id=1, source_target_pairs={{0,4},{4,0},{8,12},{12,8},{16,20},{20,16},{24,28},{28,24},{1,5},{5... | collective-permute-start | bytes 1572872 | tf_op jit(solution)/shard_map/ppermute | solution.py:567
  56.4 1.1 %place.2 = (bf16[2,2,128,256]{3,2,1,0:T(8,128)(2,1)S(1)}, f32[2,2,128,256]{3,2,1,0:T(8,128)S(1)}, bf16[2,2,128,256]{3,2,1,0:T(8,128)(2,1)S(1)}) custom-call(s32[8,128]{1,0:T(8,128)S(1)} %get-tuple-element.93.plan, bf16[2,128,256]{2,1,0:T(8,128)(2,1)S(1)} %get-tuple-element.122.refs_0_, bf16[2,128,256]{2,1,0:T(8,128)(2,1)S(1)} %collective-permute-done.13.refs_1_, ...), custom_call_target="tpu_custom_call" | custom-call | flops 100000000 | bytes 300000 | tf_op jit(solution)/shard_map/place/pallas_call | solution.py:116
  57.4 2.9 %collective-permute-start.16 = (bf16[2,2,128,256]{3,2,1,0:T(8,128)(2,1)S(1)}, bf16[2,2,128,256]{3,2,1,0:T(8,128)(2,1)S(1)}, u32[]{:S(2)}, u32[]{:S(2)}) collective-permute-start(bf16[2,2,128,256]{3,2,1,0:T(8,128)(2,1)S(1)} %get-tuple-element.126), channel_id=1, source_target_pairs={{0,8},{4,12},{8,0},{12,4},{16,24},{20,28},{24,16},{28,20},{1,9},{5... | collective-permute-start | bytes 786440 | tf_op jit(solution)/shard_map/ppermute | solution.py:598
  60.3 0.5 collective-permute-start.10
  60.8 0.7 collective-permute-start.19
  61.5 0.5 collective-permute-done.10.refs_1_
  62.0 4.7 %collective-permute-done.16.low = bf16[2,2,128,256]{3,2,1,0:T(8,128)(2,1)S(1)} collective-permute-done((bf16[2,2,128,256]{3,2,1,0:T(8,128)(2,1)S(1)}, bf16[2,2,128,256]{3,2,1,0:T(8,128)(2,1)S(1)}, u32[]{:S(2)}, u32[]{:S(2)}) %collective-permute-start.16) | collective-permute-done | bytes 262176 | tf_op jit(solution)/shard_map/ppermute | solution.py:598
  66.8 1.1 %place.3 = (bf16[2,2,128,256]{3,2,1,0:T(8,128)(2,1)S(1)}, f32[2,2,128,256]{3,2,1,0:T(8,128)S(1)}, bf16[2,2,128,256]{3,2,1,0:T(8,128)(2,1)S(1)}) custom-call(s32[8,128]{1,0:T(8,128)S(1)} %get-tuple-element.93.plan, bf16[2,128,256]{2,1,0:T(8,128)(2,1)S(1)} %get-tuple-element.127.refs_0_, bf16[2,128,256]{2,1,0:T(8,128)(2,1)S(1)} %collective-permute-done.10.refs_1_, ...), custom_call_target="tpu_custom_call" | custom-call | flops 100000000 | bytes 300000 | tf_op jit(solution)/shard_map/place/pallas_call | solution.py:116
  67.9 1.8 %collective-permute-start.17 = (bf16[2,2,128,256]{3,2,1,0:T(8,128)(2,1)S(1)}, bf16[2,2,128,256]{3,2,1,0:T(8,128)(2,1)S(1)}, u32[]{:S(2)}, u32[]{:S(2)}) collective-permute-start(bf16[2,2,128,256]{3,2,1,0:T(8,128)(2,1)S(1)} %get-tuple-element.132), channel_id=1, source_target_pairs={{0,8},{4,12},{8,0},{12,4},{16,24},{20,28},{24,16},{28,20},{1,9},{5... | collective-permute-start | bytes 786440 | tf_op jit(solution)/shard_map/ppermute | solution.py:598
  69.7 0.7 collective-permute-start.18
  70.3 0.0 collective-permute-done.23.came
  70.4 0.1 fold.1
  70.5 0.9 %collective-permute-start.24 = (bf16[4,2,2,32,256]{4,3,2,1,0:T(8,128)(2,1)S(1)}, bf16[4,2,2,32,256]{4,3,2,1,0:T(8,128)(2,1)S(1)}, u32[]{:S(2)}, u32[]{:S(2)}) collective-permute-start(bf16[4,2,2,32,256]{4,3,2,1,0:T(8,128)(2,1)S(1)} %get-tuple-element.147), channel_id=1, source_target_pairs={{0,2},{1,3},{2,0},{3,1},{4,6},{5,7},{6,4},{7,5},{8,10},{9,11},{10,... | collective-permute-start | bytes 786440 | tf_op jit(solution)/shard_map/ppermute | solution.py:430
  71.4 0.0 collective-permute-done.19.high
  71.4 0.7 split.3
  72.1 0.5 collective-permute-start.21
  72.6 3.0 %collective-permute-done.17.low = bf16[2,2,128,256]{3,2,1,0:T(8,128)(2,1)S(1)} collective-permute-done((bf16[2,2,128,256]{3,2,1,0:T(8,128)(2,1)S(1)}, bf16[2,2,128,256]{3,2,1,0:T(8,128)(2,1)S(1)}, u32[]{:S(2)}, u32[]{:S(2)}) %collective-permute-start.17) | collective-permute-done | bytes 262176 | tf_op jit(solution)/shard_map/ppermute | solution.py:598
  75.6 0.0 collective-permute-done.18.high
  75.6 0.7 split.2
  76.3 0.6 collective-permute-start.20
  76.9 0.7 collective-permute-done.24.came
  77.6 3.8 %collective-permute-start.25 = (bf16[2,2,32,256]{3,2,1,0:T(8,128)(2,1)S(1)}, bf16[2,2,32,256]{3,2,1,0:T(8,128)(2,1)S(1)}, u32[]{:S(2)}, u32[]{:S(2)}) collective-permute-start(bf16[2,2,32,256]{3,2,1,0:T(8,128)(2,1)S(1)} %get-tuple-element.149), channel_id=1, source_target_pairs={{0,8},{4,12},{8,0},{12,4},{16,24},{20,28},{24,16},{28,20},{1,9},{5... | collective-permute-start | bytes 196616 | tf_op jit(solution)/shard_map/ppermute | solution.py:580
  81.4 1.1 %collective-permute-start.26 = (bf16[2,2,32,256]{3,2,1,0:T(8,128)(2,1)S(1)}, bf16[2,2,32,256]{3,2,1,0:T(8,128)(2,1)S(1)}, u32[]{:S(2)}, u32[]{:S(2)}) collective-permute-start(bf16[2,2,32,256]{3,2,1,0:T(8,128)(2,1)S(1)} %get-tuple-element.150), channel_id=1, source_target_pairs={{0,16},{4,20},{8,24},{12,28},{16,0},{20,4},{24,8},{28,12},{1,17},{... | collective-permute-start | bytes 196616 | tf_op jit(solution)/shard_map/ppermute | solution.py:580
  82.5 1.4 %collective-permute-start.27 = (bf16[2,2,32,256]{3,2,1,0:T(8,128)(2,1)S(1)}, bf16[2,2,32,256]{3,2,1,0:T(8,128)(2,1)S(1)}, u32[]{:S(2)}, u32[]{:S(2)}) collective-permute-start(bf16[2,2,32,256]{3,2,1,0:T(8,128)(2,1)S(1)} %get-tuple-element.151), channel_id=1, source_target_pairs={{0,24},{4,28},{8,16},{12,20},{16,8},{20,12},{24,0},{28,4},{1,25},{... | collective-permute-start | bytes 196616 | tf_op jit(solution)/shard_map/ppermute | solution.py:580
  83.9 0.6 slice.27
  85.2 0.9 end.1
  86.1 1.7 %collective-permute-done.26.refs_2_ = bf16[2,2,32,256]{3,2,1,0:T(8,128)(2,1)S(1)} collective-permute-done((bf16[2,2,32,256]{3,2,1,0:T(8,128)(2,1)S(1)}, bf16[2,2,32,256]{3,2,1,0:T(8,128)(2,1)S(1)}, u32[]{:S(2)}, u32[]{:S(2)}) %collective-permute-start.26) | collective-permute-done | bytes 65568 | tf_op jit(solution)/shard_map/ppermute | solution.py:580
  87.7 0.9 %collective-permute-done.27.refs_3_ = bf16[2,2,32,256]{3,2,1,0:T(8,128)(2,1)S(1)} collective-permute-done((bf16[2,2,32,256]{3,2,1,0:T(8,128)(2,1)S(1)}, bf16[2,2,32,256]{3,2,1,0:T(8,128)(2,1)S(1)}, u32[]{:S(2)}, u32[]{:S(2)}) %collective-permute-start.27) | collective-permute-done | bytes 65568 | tf_op jit(solution)/shard_map/ppermute | solution.py:580
  88.6 0.7 total.1
  (25 shorter events, 0.2 us)
Async XLA Ops:
  0.6 5.2 %copy-start.4 = (bf16[8,256,256]{2,1,0:T(8,128)(2,1)S(1)}, bf16[8,256,256]{2,1,0:T(8,128)(2,1)}, u32[]{:S(2)}) copy-start(bf16[8,256,256]{2,1,0:T(8,128)(2,1)} %amplitudes_far.1) | copy-start | bytes 3145732
  2.0 15.0 %collective-permute-start = (bf16[2,2,256,256]{3,2,1,0:T(8,128)(2,1)S(1)}, bf16[2,2,256,256]{3,2,1,0:T(8,128)(2,1)S(1)}, u32[]{:S(2)}, u32[]{:S(2)}) collective-permute-start(bf16[2,2,256,256]{3,2,1,0:T(8,128)(2,1)S(1)} %convert_element_type.42), channel_id=1, source_target_pairs={{0,2},{1,3},{2,0},{3,1},{4,6},{5,7},{6,4},{7,5},{8,10},{9,11},{10,... | collective-permute-start | bytes 1572872 | tf_op jit(solution)/shard_map/ppermute | solution.py:430
  5.8 1.6 %copy-start.2 = (bf16[2,2,128,2048]{3,2,1,0:T(8,128)(2,1)S(1)}, bf16[2,2,128,2048]{3,2,1,0:T(8,128)(2,1)}, u32[]{:S(2)}) copy-start(bf16[2,2,128,2048]{3,2,1,0:T(8,128)(2,1)} %strip_far.1) | copy-start | bytes 6291460
  7.4 0.7 copy-start.6
  8.1 23.3 %copy-start = (f32[2,2,256,256]{3,2,1,0:T(8,128)S(1)}, f32[2,2,256,256]{3,2,1,0:T(8,128)}, u32[]{:S(2)}) copy-start(f32[2,2,256,256]{3,2,1,0:T(8,128)} %refs_1_.1) | copy-start | bytes 3145732
  8.1 23.3 %copy-start.1 = (bf16[4,256,256]{2,1,0:T(8,128)(2,1)S(1)}, bf16[4,256,256]{2,1,0:T(8,128)(2,1)}, u32[]{:S(2)}) copy-start(bf16[4,256,256]{2,1,0:T(8,128)(2,1)} %constant.181.clone.refs_8_.refs_4_.refs_6_) | copy-start | bytes 1572868
  8.1 23.3 %copy-start.3 = (f32[2,256,256]{2,1,0:T(8,128)S(1)}, f32[2,256,256]{2,1,0:T(8,128)}, u32[]{:S(2)}) copy-start(f32[2,256,256]{2,1,0:T(8,128)} %constant.182.clone.refs_9_.refs_7_) | copy-start | bytes 1572868
  10.2 13.4 %collective-permute-start.6 = (bf16[4,256,256]{2,1,0:T(8,128)(2,1)S(1)}, bf16[4,256,256]{2,1,0:T(8,128)(2,1)S(1)}, u32[]{:S(2)}, u32[]{:S(2)}) collective-permute-start(bf16[4,256,256]{2,1,0:T(8,128)(2,1)S(1)} %get-tuple-element.109), channel_id=1, source_target_pairs={{0,4},{4,0},{8,12},{12,8},{16,20},{20,16},{24,28},{28,24},{1,5},{5... | collective-permute-start | bytes 1572872 | tf_op jit(solution)/shard_map/ppermute | solution.py:488
  11.7 12.6 %collective-permute-start.4 = (bf16[2,2,256,256]{3,2,1,0:T(8,128)(2,1)S(1)}, bf16[2,2,256,256]{3,2,1,0:T(8,128)(2,1)S(1)}, u32[]{:S(2)}, u32[]{:S(2)}) collective-permute-start(bf16[2,2,256,256]{3,2,1,0:T(8,128)(2,1)S(1)} %convert_element_type.42), channel_id=1, source_target_pairs={{0,1},{1,0},{2,3},{3,2},{4,5},{5,4},{6,7},{7,6},{8,9},{9,8},{10,11... | collective-permute-start | bytes 1572872 | tf_op jit(solution)/shard_map/ppermute | solution.py:430
  17.0 14.3 %collective-permute-start.5 = (bf16[2,2,256,256]{3,2,1,0:T(8,128)(2,1)S(1)}, bf16[2,2,256,256]{3,2,1,0:T(8,128)(2,1)S(1)}, u32[]{:S(2)}, u32[]{:S(2)}) collective-permute-start(bf16[2,2,256,256]{3,2,1,0:T(8,128)(2,1)S(1)} %collective-permute-done.refs_6_.refs_3_), channel_id=1, source_target_pairs={{0,1},{1,0},{2,3},{3,2},{4,5},{5,4},{6,7},{7,6},{8,9},{9,8},{10,11... | collective-permute-start | bytes 1572872 | tf_op jit(solution)/shard_map/ppermute | solution.py:430
  17.0 9.0 %collective-permute-start.1 = (bf16[2,2,128,256]{3,2,1,0:T(8,128)(2,1)S(1)}, bf16[2,2,128,256]{3,2,1,0:T(8,128)(2,1)S(1)}, u32[]{:S(2)}, u32[]{:S(2)}) collective-permute-start(bf16[2,2,128,256]{3,2,1,0:T(8,128)(2,1)S(1)} %get-tuple-element.100), channel_id=1, source_target_pairs={{0,1},{1,0},{2,3},{3,2},{4,5},{5,4},{6,7},{7,6},{8,9},{9,8},{10,11... | collective-permute-start | bytes 786440 | tf_op jit(solution)/shard_map/ppermute | solution.py:430
  17.5 11.1 %collective-permute-start.2 = (bf16[2,2,128,256]{3,2,1,0:T(8,128)(2,1)S(1)}, bf16[2,2,128,256]{3,2,1,0:T(8,128)(2,1)S(1)}, u32[]{:S(2)}, u32[]{:S(2)}) collective-permute-start(bf16[2,2,128,256]{3,2,1,0:T(8,128)(2,1)S(1)} %get-tuple-element.101), channel_id=1, source_target_pairs={{0,2},{1,3},{2,0},{3,1},{4,6},{5,7},{6,4},{7,5},{8,10},{9,11},{10,... | collective-permute-start | bytes 786440 | tf_op jit(solution)/shard_map/ppermute | solution.py:430
  23.6 7.7 %collective-permute-start.3 = (bf16[2,2,128,256]{3,2,1,0:T(8,128)(2,1)S(1)}, bf16[2,2,128,256]{3,2,1,0:T(8,128)(2,1)S(1)}, u32[]{:S(2)}, u32[]{:S(2)}) collective-permute-start(bf16[2,2,128,256]{3,2,1,0:T(8,128)(2,1)S(1)} %get-tuple-element.102), channel_id=1, source_target_pairs={{0,3},{1,2},{2,1},{3,0},{4,7},{5,6},{6,5},{7,4},{8,11},{9,10},{10,... | collective-permute-start | bytes 786440 | tf_op jit(solution)/shard_map/ppermute | solution.py:430
  24.3 14.0 %collective-permute-start.7 = (bf16[256,256]{1,0:T(8,128)(2,1)S(1)}, bf16[256,256]{1,0:T(8,128)(2,1)S(1)}, u32[]{:S(2)}, u32[]{:S(2)}) collective-permute-start(bf16[256,256]{1,0:T(8,128)(2,1)S(1)} %get-tuple-element.111), channel_id=1, source_target_pairs={{0,8},{4,12},{8,0},{12,4},{16,24},{20,28},{24,16},{28,20},{1,9},{5... | collective-permute-start | bytes 393224 | tf_op jit(solution)/shard_map/ppermute | solution.py:494
  26.0 12.9 %collective-permute-start.8 = (bf16[256,256]{1,0:T(8,128)(2,1)S(1)}, bf16[256,256]{1,0:T(8,128)(2,1)S(1)}, u32[]{:S(2)}, u32[]{:S(2)}) collective-permute-start(bf16[256,256]{1,0:T(8,128)(2,1)S(1)} %get-tuple-element.112), channel_id=1, source_target_pairs={{0,16},{4,20},{8,24},{12,28},{16,0},{20,4},{24,8},{28,12},{1,17},{... | collective-permute-start | bytes 393224 | tf_op jit(solution)/shard_map/ppermute | solution.py:494
  28.6 10.3 %copy-start.5 = (bf16[2,256,256]{2,1,0:T(8,128)(2,1)S(1)}, bf16[2,256,256]{2,1,0:T(8,128)(2,1)}, u32[]{:S(2)}) copy-start(bf16[2,256,256]{2,1,0:T(8,128)(2,1)} %constant.183.clone.refs_5_) | copy-start | bytes 786436
  28.6 10.3 %collective-permute-start.9 = (bf16[256,256]{1,0:T(8,128)(2,1)S(1)}, bf16[256,256]{1,0:T(8,128)(2,1)S(1)}, u32[]{:S(2)}, u32[]{:S(2)}) collective-permute-start(bf16[256,256]{1,0:T(8,128)(2,1)S(1)} %get-tuple-element.113), channel_id=1, source_target_pairs={{0,24},{4,28},{8,16},{12,20},{16,8},{20,12},{24,0},{28,4},{1,25},{... | collective-permute-start | bytes 393224 | tf_op jit(solution)/shard_map/ppermute | solution.py:494
  43.0 6.5 %collective-permute-start.13 = (bf16[2,128,256]{2,1,0:T(8,128)(2,1)S(1)}, bf16[2,128,256]{2,1,0:T(8,128)(2,1)S(1)}, u32[]{:S(2)}, u32[]{:S(2)}) collective-permute-start(bf16[2,128,256]{2,1,0:T(8,128)(2,1)S(1)} %get-tuple-element.120), channel_id=1, source_target_pairs={{0,1},{1,0},{2,3},{3,2},{4,5},{5,4},{6,7},{7,6},{8,9},{9,8},{10,11... | collective-permute-start | bytes 393224 | tf_op jit(solution)/shard_map/ppermute | solution.py:430
  43.1 6.5 %collective-permute-start.14 = (bf16[2,128,256]{2,1,0:T(8,128)(2,1)S(1)}, bf16[2,128,256]{2,1,0:T(8,128)(2,1)S(1)}, u32[]{:S(2)}, u32[]{:S(2)}) collective-permute-start(bf16[2,128,256]{2,1,0:T(8,128)(2,1)S(1)} %get-tuple-element.122.refs_0_), channel_id=1, source_target_pairs={{0,2},{1,3},{2,0},{3,1},{4,6},{5,7},{6,4},{7,5},{8,10},{9,11},{10,... | collective-permute-start | bytes 393224 | tf_op jit(solution)/shard_map/ppermute | solution.py:430
  44.4 6.9 %collective-permute-start.15 = (bf16[2,128,256]{2,1,0:T(8,128)(2,1)S(1)}, bf16[2,128,256]{2,1,0:T(8,128)(2,1)S(1)}, u32[]{:S(2)}, u32[]{:S(2)}) collective-permute-start(bf16[2,128,256]{2,1,0:T(8,128)(2,1)S(1)} %get-tuple-element.120), channel_id=1, source_target_pairs={{0,3},{1,2},{2,1},{3,0},{4,7},{5,6},{6,5},{7,4},{8,11},{9,10},{10,... | collective-permute-start | bytes 393224 | tf_op jit(solution)/shard_map/ppermute | solution.py:430
  51.3 2.7 %collective-permute-start.22 = (bf16[2,2,2,256,256]{4,3,2,1,0:T(8,128)(2,1)S(1)}, bf16[2,2,2,256,256]{4,3,2,1,0:T(8,128)(2,1)S(1)}, u32[]{:S(2)}, u32[]{:S(2)}) collective-permute-start(bf16[2,2,2,256,256]{4,3,2,1,0:T(8,128)(2,1)S(1)} %get-tuple-element.143), channel_id=1, source_target_pairs={{0,1},{1,0},{2,3},{3,2},{4,5},{5,4},{6,7},{7,6},{8,9},{9,8},{10,11... | collective-permute-start | bytes 3145736 | tf_op jit(solution)/shard_map/ppermute | solution.py:430
  51.6 8.7 %collective-permute-start.11 = (bf16[2,2,128,256]{3,2,1,0:T(8,128)(2,1)S(1)}, bf16[2,2,128,256]{3,2,1,0:T(8,128)(2,1)S(1)}, u32[]{:S(2)}, u32[]{:S(2)}) collective-permute-start(bf16[2,2,128,256]{3,2,1,0:T(8,128)(2,1)S(1)} %get-tuple-element.118), channel_id=1, source_target_pairs={{0,2},{1,3},{2,0},{3,1},{4,6},{5,7},{6,4},{7,5},{8,10},{9,11},{10,... | collective-permute-start | bytes 786440 | tf_op jit(solution)/shard_map/ppermute | solution.py:430
  54.8 15.5 %collective-permute-start.23 = (bf16[2,4,2,2,32,256]{5,4,3,2,1,0:T(8,128)(2,1)S(1)}, bf16[2,4,2,2,32,256]{5,4,3,2,1,0:T(8,128)(2,1)S(1)}, u32[]{:S(2)}, u32[]{:S(2)}) collective-permute-start(bf16[2,4,2,2,32,256]{5,4,3,2,1,0:T(8,128)(2,1)S(1)} %get-tuple-element.145), channel_id=1, source_target_pairs={{0,4},{4,0},{8,12},{12,8},{16,20},{20,16},{24,28},{28,24},{1,5},{5... | collective-permute-start | bytes 1572872 | tf_op jit(solution)/shard_map/ppermute | solution.py:567
  57.4 9.3 %collective-permute-start.16 = (bf16[2,2,128,256]{3,2,1,0:T(8,128)(2,1)S(1)}, bf16[2,2,128,256]{3,2,1,0:T(8,128)(2,1)S(1)}, u32[]{:S(2)}, u32[]{:S(2)}) collective-permute-start(bf16[2,2,128,256]{3,2,1,0:T(8,128)(2,1)S(1)} %get-tuple-element.126), channel_id=1, source_target_pairs={{0,8},{4,12},{8,0},{12,4},{16,24},{20,28},{24,16},{28,20},{1,9},{5... | collective-permute-start | bytes 786440 | tf_op jit(solution)/shard_map/ppermute | solution.py:598
  60.3 6.5 %collective-permute-start.12 = (bf16[2,2,128,256]{3,2,1,0:T(8,128)(2,1)S(1)}, bf16[2,2,128,256]{3,2,1,0:T(8,128)(2,1)S(1)}, u32[]{:S(2)}, u32[]{:S(2)}) collective-permute-start(bf16[2,2,128,256]{3,2,1,0:T(8,128)(2,1)S(1)} %collective-permute-done.11.refs_2_), channel_id=1, source_target_pairs={{0,1},{1,0},{2,3},{3,2},{4,5},{5,4},{6,7},{7,6},{8,9},{9,8},{10,11... | collective-permute-start | bytes 786440 | tf_op jit(solution)/shard_map/ppermute | solution.py:430
  60.3 1.7 %collective-permute-start.10 = (bf16[2,128,256]{2,1,0:T(8,128)(2,1)S(1)}, bf16[2,128,256]{2,1,0:T(8,128)(2,1)S(1)}, u32[]{:S(2)}, u32[]{:S(2)}) collective-permute-start(bf16[2,128,256]{2,1,0:T(8,128)(2,1)S(1)} %get-tuple-element.117), channel_id=1, source_target_pairs={{0,1},{1,0},{2,3},{3,2},{4,5},{5,4},{6,7},{7,6},{8,9},{9,8},{10,11... | collective-permute-start | bytes 393224 | tf_op jit(solution)/shard_map/ppermute | solution.py:430
  60.8 10.6 %collective-permute-start.19 = (bf16[2,2,128,256]{3,2,1,0:T(8,128)(2,1)S(1)}, bf16[2,2,128,256]{3,2,1,0:T(8,128)(2,1)S(1)}, u32[]{:S(2)}, u32[]{:S(2)}) collective-permute-start(bf16[2,2,128,256]{3,2,1,0:T(8,128)(2,1)S(1)} %get-tuple-element.137), channel_id=1, source_target_pairs={{8,16},{12,20},{16,8},{20,12},{9,17},{13,21},{17,9},{21,13},{10,18... | collective-permute-start | bytes 786440 | tf_op jit(solution)/shard_map/ppermute | solution.py:600
  67.9 7.7 %collective-permute-start.17 = (bf16[2,2,128,256]{3,2,1,0:T(8,128)(2,1)S(1)}, bf16[2,2,128,256]{3,2,1,0:T(8,128)(2,1)S(1)}, u32[]{:S(2)}, u32[]{:S(2)}) collective-permute-start(bf16[2,2,128,256]{3,2,1,0:T(8,128)(2,1)S(1)} %get-tuple-element.132), channel_id=1, source_target_pairs={{0,8},{4,12},{8,0},{12,4},{16,24},{20,28},{24,16},{28,20},{1,9},{5... | collective-permute-start | bytes 786440 | tf_op jit(solution)/shard_map/ppermute | solution.py:598
  69.7 5.9 %collective-permute-start.18 = (bf16[2,2,128,256]{3,2,1,0:T(8,128)(2,1)S(1)}, bf16[2,2,128,256]{3,2,1,0:T(8,128)(2,1)S(1)}, u32[]{:S(2)}, u32[]{:S(2)}) collective-permute-start(bf16[2,2,128,256]{3,2,1,0:T(8,128)(2,1)S(1)} %get-tuple-element.133), channel_id=1, source_target_pairs={{8,16},{12,20},{16,8},{20,12},{9,17},{13,21},{17,9},{21,13},{10,18... | collective-permute-start | bytes 786440 | tf_op jit(solution)/shard_map/ppermute | solution.py:600
  70.5 7.1 %collective-permute-start.24 = (bf16[4,2,2,32,256]{4,3,2,1,0:T(8,128)(2,1)S(1)}, bf16[4,2,2,32,256]{4,3,2,1,0:T(8,128)(2,1)S(1)}, u32[]{:S(2)}, u32[]{:S(2)}) collective-permute-start(bf16[4,2,2,32,256]{4,3,2,1,0:T(8,128)(2,1)S(1)} %get-tuple-element.147), channel_id=1, source_target_pairs={{0,2},{1,3},{2,0},{3,1},{4,6},{5,7},{6,4},{7,5},{8,10},{9,11},{10,... | collective-permute-start | bytes 786440 | tf_op jit(solution)/shard_map/ppermute | solution.py:430
  72.1 13.1 %collective-permute-start.21 = (bf16[2,128,256]{2,1,0:T(8,128)(2,1)S(1)}, bf16[2,128,256]{2,1,0:T(8,128)(2,1)S(1)}, u32[]{:S(2)}, u32[]{:S(2)}) collective-permute-start(bf16[2,128,256]{2,1,0:T(8,128)(2,1)S(1)} %get-tuple-element.140), channel_id=1, source_target_pairs={{0,4},{4,0},{8,12},{12,8},{16,20},{20,16},{24,28},{28,24},{1,5},{5... | collective-permute-start | bytes 393224 | tf_op jit(solution)/shard_map/ppermute | solution.py:610
  76.3 8.9 %collective-permute-start.20 = (bf16[2,128,256]{2,1,0:T(8,128)(2,1)S(1)}, bf16[2,128,256]{2,1,0:T(8,128)(2,1)S(1)}, u32[]{:S(2)}, u32[]{:S(2)}) collective-permute-start(bf16[2,128,256]{2,1,0:T(8,128)(2,1)S(1)} %get-tuple-element.139), channel_id=1, source_target_pairs={{0,4},{4,0},{8,12},{12,8},{16,20},{20,16},{24,28},{28,24},{1,5},{5... | collective-permute-start | bytes 393224 | tf_op jit(solution)/shard_map/ppermute | solution.py:610
  77.6 8.4 %collective-permute-start.25 = (bf16[2,2,32,256]{3,2,1,0:T(8,128)(2,1)S(1)}, bf16[2,2,32,256]{3,2,1,0:T(8,128)(2,1)S(1)}, u32[]{:S(2)}, u32[]{:S(2)}) collective-permute-start(bf16[2,2,32,256]{3,2,1,0:T(8,128)(2,1)S(1)} %get-tuple-element.149), channel_id=1, source_target_pairs={{0,8},{4,12},{8,0},{12,4},{16,24},{20,28},{24,16},{28,20},{1,9},{5... | collective-permute-start | bytes 196616 | tf_op jit(solution)/shard_map/ppermute | solution.py:580
  81.4 6.3 %collective-permute-start.26 = (bf16[2,2,32,256]{3,2,1,0:T(8,128)(2,1)S(1)}, bf16[2,2,32,256]{3,2,1,0:T(8,128)(2,1)S(1)}, u32[]{:S(2)}, u32[]{:S(2)}) collective-permute-start(bf16[2,2,32,256]{3,2,1,0:T(8,128)(2,1)S(1)} %get-tuple-element.150), channel_id=1, source_target_pairs={{0,16},{4,20},{8,24},{12,28},{16,0},{20,4},{24,8},{28,12},{1,17},{... | collective-permute-start | bytes 196616 | tf_op jit(solution)/shard_map/ppermute | solution.py:580
  82.5 6.1 %collective-permute-start.27 = (bf16[2,2,32,256]{3,2,1,0:T(8,128)(2,1)S(1)}, bf16[2,2,32,256]{3,2,1,0:T(8,128)(2,1)S(1)}, u32[]{:S(2)}, u32[]{:S(2)}) collective-permute-start(bf16[2,2,32,256]{3,2,1,0:T(8,128)(2,1)S(1)} %get-tuple-element.151), channel_id=1, source_target_pairs={{0,24},{4,28},{8,16},{12,20},{16,8},{20,12},{24,0},{28,4},{1,25},{... | collective-permute-start | bytes 196616 | tf_op jit(solution)/shard_map/ppermute | solution.py:580
